TPU v7x, 32 devices: a whole 2x2x4 slice. The times are simulated.
32 devices in a mesh: dp: 4 (over x, core), seq: 8 (over z, y).
Axes of the slice: x: 2, y: 2, z: 4, core: 2. Of those that a mesh axis runs over, the one named last changes fastest.
Arguments:
- inputs: bfloat16 [4, 1024, 768], P('dp', 'seq'), may hold values from -6 to 6
- segments: int32 [4, 1024], P('dp'), may hold values from 0 to 5, as said below
- rand_blocks: int32 [4, 16, 3], P('dp'), may hold values from 0 to 15, as said below
- glob_blocks: int32 [4, 6, 2], P('dp'), may hold values from 0 to 15, as said below
- w_qkv: bfloat16 [768, 2304], P(('dp', 'seq')), may hold values from -0.21875 to 0.21875
- w_out: bfloat16 [768, 768], P(('dp', 'seq')), may hold values from -2.5 to 2.5
- w_in: bfloat16 [768, 3072], P(('dp', 'seq')), may hold values from -0.21875 to 0.21875
- w_down: bfloat16 [3072, 768], P(('dp', 'seq')), may hold values from -0.109375 to 0.109375
- vec_bias: bfloat16 [4, 768], P(None, ('dp', 'seq')), may hold values from -3 to 3
- ffn_bias: bfloat16 [3072], P(('dp', 'seq')), may hold values from -3 to 3
- norm_gain: bfloat16 [2, 768], P(None, ('dp', 'seq')), may hold values from 0.5 to 1.5
- norm_shift: bfloat16 [2, 768], P(None, ('dp', 'seq')), may hold values from -3 to 3
- cotangent: bfloat16 [4, 1024, 768], P('dp', 'seq'), may hold values from -6 to 6
Outputs:
- output: bfloat16 [4, 1024, 768], P('dp', 'seq')
- input_grad: float32 [4, 1024, 768], P('dp', 'seq')
- grad_qkv: float32 [768, 2304], P(('dp', 'seq'))
- grad_out: float32 [768, 768], P(('dp', 'seq'))
- grad_in: float32 [768, 3072], P(('dp', 'seq'))
- grad_down: float32 [3072, 768], P(('dp', 'seq'))
- grad_vec_bias: float32 [4, 768], P(None, ('dp', 'seq'))
- grad_ffn_bias: float32 [3072], P(('dp', 'seq'))
- grad_norm_gain: float32 [2, 768], P(None, ('dp', 'seq'))
- grad_norm_shift: float32 [2, 768], P(None, ('dp', 'seq'))
Inputs may be any that keep to these rules, and one draw needn't show every extreme that they name: segments never fall along a sequence; every document but the last of a sequence has 200 to 2000 tokens. rand_blocks[s, b, :] are blocks that hold tokens of the document of block b's first token. glob_blocks[s, d, :] are blocks that hold tokens of document d, where document d occurs in sequence s.
All inputs are finite; a program needn't handle non-finite values.
Results may differ from a plain program's by a relative error of at most 0.014.
Values may be sent and summed in bfloat16 or wider, within the bound.
No kernel may reach another device: no remote copies, remote signals or barrier semaphores. Data moves between devices by JAX's collectives and lax.ppermute only.
A program may use at most 192 MiB of HBM per device.

v0:
```python
import jax
import jax.numpy as jnp
from jax import lax
from jax.sharding import PartitionSpec as P

HD = 64
BLK = 64
NRAND = 3
NGLOB = 2


norm_eps = 1e-05
masked_score = -1e30


def key_lists(query_block, rand_rows, glob_first, glob_last, block_count):
    window = query_block[..., None] + jnp.arange(-1, 2, dtype=jnp.int32)
    listed = jnp.concatenate([window, rand_rows, glob_first, glob_last], axis=-1)
    inside = (listed >= 0) & (listed < block_count)
    entry_order = jnp.arange(listed.shape[-1])
    earlier = entry_order[None, :] < entry_order[:, None]
    same_block = listed[..., :, None] == listed[..., None, :]
    repeated = jnp.any(same_block & earlier & inside[..., None, :], axis=-1)
    return (jnp.clip(listed, 0, block_count - 1), inside & jnp.logical_not(repeated))


def allowed_mask(seg_query, seg_key, glob_query, listed, valid):
    same_seg = seg_query[:, :, None, None] == seg_key[:, None, :, :]
    member = jnp.any(glob_query[:, :, None, :] == listed[:, None, :, None], axis=-1)
    fixed_part = jnp.arange(listed.shape[1]) < 3 + NRAND
    reach_mask = valid[:, None, :] & (fixed_part[None, None, :] | member)
    return same_seg & reach_mask[..., None]


def lookup_rows(table, row_ids):
    id_match = row_ids[:, :, None] == jnp.arange(table.shape[1], dtype=jnp.int32)[None, None, :]
    return jnp.sum(jnp.where(id_match[..., None], table[:, None, :, :], 0), axis=2)


def take_blocks(blocks, listed):
    return jax.vmap(lambda block_set, picks: block_set[picks])(blocks, listed)


def normalize(field_in):
    mean_row = jnp.mean(field_in, axis=-1, keepdims=True)
    centred = field_in - mean_row
    inverse = lax.rsqrt(jnp.mean(centred * centred, axis=-1, keepdims=True) + norm_eps)
    return (centred * inverse, inverse)


def norm_back(grad_in, normed, inverse, gain_row):
    weighted = grad_in * gain_row
    inner = jnp.mean(weighted * normed, axis=-1, keepdims=True)
    return inverse * (weighted - jnp.mean(weighted, axis=-1, keepdims=True) - normed * inner)


def gelu_slope(field_in):
    return (
        0.5 * (1.0 + lax.erf(field_in * 0.7071067811865476))
        + field_in * jnp.exp(-0.5 * field_in * field_in) * 0.3989422804014327
    )


def on_device(
    inputs,
    segments,
    rand_blocks,
    glob_blocks,
    w_qkv,
    w_out,
    w_in,
    w_down,
    vec_bias,
    ffn_bias,
    norm_gain,
    norm_shift,
    cotangent,
):
    seq_count, local_len, model_width = inputs.shape
    full_len = segments.shape[1]
    block_count = full_len // BLK
    own_blocks = local_len // BLK
    head_count = model_width // HD
    group_count = seq_count * own_blocks
    row_count = seq_count * local_len
    score_scale = HD ** (-0.5)
    seq_place = lax.axis_index("seq")
    gathered = (
        lax.all_gather(w_qkv, ("dp", "seq"), axis=0, tiled=True),
        lax.all_gather(w_out, ("dp", "seq"), axis=0, tiled=True),
        lax.all_gather(w_in, ("dp", "seq"), axis=0, tiled=True),
        lax.all_gather(w_down, ("dp", "seq"), axis=0, tiled=True),
        lax.all_gather(vec_bias, ("dp", "seq"), axis=1, tiled=True),
        lax.all_gather(ffn_bias, ("dp", "seq"), axis=0, tiled=True),
        lax.all_gather(norm_gain, ("dp", "seq"), axis=1, tiled=True),
        lax.all_gather(norm_shift, ("dp", "seq"), axis=1, tiled=True),
    )
    qkv_full, out_full, in_full, down_full, bias_full, ffn_full, gain_full, shift_full = gathered
    bias_rows = bias_full.astype(jnp.float32)
    shift_rows = shift_full.astype(jnp.float32)
    tokens = inputs.reshape(row_count, model_width)
    qkv_mixed = jnp.dot(tokens, qkv_full, preferred_element_type=jnp.float32)
    query_low = (qkv_mixed[:, :model_width] + bias_rows[0]).astype(jnp.bfloat16)
    key_low = qkv_mixed[:, model_width : 2 * model_width].astype(jnp.bfloat16)
    value_low = (qkv_mixed[:, 2 * model_width :] + bias_rows[1]).astype(jnp.bfloat16)
    all_keys, all_values = (
        lax.all_gather(
            key_low.reshape(seq_count, local_len, model_width), "seq", axis=1, tiled=True
        ),
        lax.all_gather(
            value_low.reshape(seq_count, local_len, model_width), "seq", axis=1, tiled=True
        ),
    )
    seg_query = lax.dynamic_slice_in_dim(segments, seq_place * local_len, local_len, 1)
    own_index = seq_place * own_blocks + jnp.arange(own_blocks, dtype=jnp.int32)
    rand_rows = lax.dynamic_slice_in_dim(rand_blocks, seq_place * own_blocks, own_blocks, 1)
    glob_first = lookup_rows(glob_blocks, seg_query[:, ::BLK])
    glob_last = lookup_rows(glob_blocks, seg_query[:, BLK - 1 :: BLK])
    query_block = own_index[None, :]
    listed, valid = key_lists(query_block, rand_rows, glob_first, glob_last, block_count)
    entry_count = listed.shape[-1]
    flat_listed = listed.reshape(seq_count, own_blocks * entry_count)
    key_blocks = take_blocks(
        all_keys.reshape(seq_count, block_count, BLK, model_width), flat_listed
    )
    value_blocks = take_blocks(
        all_values.reshape(seq_count, block_count, BLK, model_width), flat_listed
    )
    seg_key = take_blocks(segments.reshape(seq_count, block_count, BLK), flat_listed)
    glob_query = lookup_rows(glob_blocks, seg_query)
    allowed = allowed_mask(
        seg_query.reshape(group_count, BLK),
        seg_key.reshape(group_count, entry_count, BLK),
        glob_query.reshape(group_count, BLK, NGLOB),
        listed.reshape(group_count, entry_count),
        valid.reshape(group_count, entry_count),
    )
    query_g = query_low.reshape(group_count, BLK, head_count, HD)
    key_g = key_blocks.reshape(group_count, entry_count, BLK, head_count, HD)
    value_g = value_blocks.reshape(group_count, entry_count, BLK, head_count, HD)

    def masked_scores():
        raw_scores = (
            jnp.einsum("gihd,gejhd->ghiej", query_g, key_g, preferred_element_type=jnp.float32)
            * score_scale
        )
        return jnp.where(allowed[:, None], raw_scores, masked_score).reshape(
            group_count, head_count, BLK, entry_count * BLK
        )

    scores = masked_scores()
    row_top = jnp.max(scores, axis=-1, keepdims=True)
    exp_terms = jnp.exp(scores - row_top)
    row_total = jnp.sum(exp_terms, axis=-1, keepdims=True)
    log_total = row_top + jnp.log(row_total)
    attn_probs = (
        (exp_terms / row_total)
        .astype(jnp.bfloat16)
        .reshape(group_count, head_count, BLK, entry_count, BLK)
    )
    attended = (
        jnp.einsum("ghiej,gejhd->gihd", attn_probs, value_g, preferred_element_type=jnp.float32)
        .astype(jnp.bfloat16)
        .reshape(row_count, model_width)
    )
    x_float = tokens.astype(jnp.float32)
    branch = jnp.dot(attended, out_full, preferred_element_type=jnp.float32) + bias_rows[2]
    gain_rows = gain_full.astype(jnp.float32)
    first_normed, first_inverse = normalize(x_float + branch)
    first = first_normed * gain_rows[0] + shift_rows[0]
    first_low = first.astype(jnp.bfloat16)
    hidden = jnp.dot(first_low, in_full, preferred_element_type=jnp.float32) + ffn_full.astype(
        jnp.float32
    )
    active = jax.nn.gelu(hidden, approximate=False).astype(jnp.bfloat16)
    second = jnp.dot(active, down_full, preferred_element_type=jnp.float32) + bias_rows[3]
    second_normed, second_inverse = normalize(first + second)
    output = (second_normed * gain_rows[1] + shift_rows[1]).astype(jnp.bfloat16)
    again = (
        lax.all_gather(w_qkv, ("dp", "seq"), axis=0, tiled=True),
        lax.all_gather(w_out, ("dp", "seq"), axis=0, tiled=True),
        lax.all_gather(w_in, ("dp", "seq"), axis=0, tiled=True),
        lax.all_gather(w_down, ("dp", "seq"), axis=0, tiled=True),
        lax.all_gather(norm_gain, ("dp", "seq"), axis=1, tiled=True),
    )
    qkv_back, out_back, in_back, down_back, gain_back = again
    gain_again = gain_back.astype(jnp.float32)
    out_grad = cotangent.reshape(row_count, model_width).astype(jnp.float32)
    gain_two = jnp.sum(out_grad * second_normed, axis=0)
    shift_two = jnp.sum(out_grad, axis=0)
    d_two = norm_back(out_grad, second_normed, second_inverse, gain_again[1])
    d_second = d_two.astype(jnp.bfloat16)
    grad_down = jnp.einsum("tf,td->fd", active, d_second, preferred_element_type=jnp.float32)
    bias_two = jnp.sum(d_second.astype(jnp.float32), axis=0)
    d_active = jnp.einsum("td,fd->tf", d_second, down_back, preferred_element_type=jnp.float32)
    d_hidden = (d_active * gelu_slope(hidden)).astype(jnp.bfloat16)
    grad_in = jnp.einsum("td,tf->df", first_low, d_hidden, preferred_element_type=jnp.float32)
    bias_ffn = jnp.sum(d_hidden.astype(jnp.float32), axis=0)
    d_first = d_two + jnp.einsum("tf,df->td", d_hidden, in_back, preferred_element_type=jnp.float32)
    gain_one = jnp.sum(d_first * first_normed, axis=0)
    shift_one = jnp.sum(d_first, axis=0)
    d_one = norm_back(d_first, first_normed, first_inverse, gain_again[0])
    d_branch = d_one.astype(jnp.bfloat16)
    grad_out = jnp.einsum("tc,td->cd", attended, d_branch, preferred_element_type=jnp.float32)
    bias_out = jnp.sum(d_branch.astype(jnp.float32), axis=0)
    d_attended = jnp.einsum(
        "td,cd->tc", d_branch, out_back, preferred_element_type=jnp.float32
    ).astype(jnp.bfloat16)
    d_att_g = d_attended.reshape(group_count, BLK, head_count, HD)
    soft_weights = jnp.exp(masked_scores() - log_total)
    d_probs = jnp.einsum(
        "gihd,gejhd->ghiej", d_att_g, value_g, preferred_element_type=jnp.float32
    ).reshape(group_count, head_count, BLK, entry_count * BLK)
    row_delta = jnp.sum(soft_weights * d_probs, axis=-1, keepdims=True)
    d_scores = (
        (soft_weights * (d_probs - row_delta))
        .astype(jnp.bfloat16)
        .reshape(group_count, head_count, BLK, entry_count, BLK)
    )
    d_query = (
        (
            jnp.einsum("ghiej,gejhd->gihd", d_scores, key_g, preferred_element_type=jnp.float32)
            * score_scale
        )
        .astype(jnp.bfloat16)
        .reshape(row_count, model_width)
    )
    key_terms = (
        jnp.einsum("ghiej,gihd->gejhd", d_scores, query_g, preferred_element_type=jnp.float32)
        * score_scale
    ).reshape(seq_count, own_blocks * entry_count, BLK, model_width)
    value_terms = jnp.einsum(
        "ghiej,gihd->gejhd", attn_probs, d_att_g, preferred_element_type=jnp.float32
    ).reshape(seq_count, own_blocks * entry_count, BLK, model_width)
    holder = jnp.zeros((block_count, BLK, model_width), jnp.float32)
    key_sum = holder.at[flat_listed[0]].add(key_terms[0])
    value_sum = holder.at[flat_listed[0]].add(value_terms[0])
    key_mine = lax.psum_scatter(
        key_sum.reshape(full_len, model_width).astype(jnp.bfloat16),
        "seq",
        scatter_dimension=0,
        tiled=True,
    )
    value_mine = lax.psum_scatter(
        value_sum.reshape(full_len, model_width).astype(jnp.bfloat16),
        "seq",
        scatter_dimension=0,
        tiled=True,
    )
    d_mixed = jnp.concatenate([d_query, key_mine, value_mine], axis=1)
    grad_qkv = jnp.einsum("tc,tk->ck", tokens, d_mixed, preferred_element_type=jnp.float32)
    bias_query = jnp.sum(d_query.astype(jnp.float32), axis=0)
    bias_value = jnp.sum(value_mine.astype(jnp.float32), axis=0)
    input_grad = d_one + jnp.einsum(
        "tk,ck->tc", d_mixed, qkv_back, preferred_element_type=jnp.float32
    )
    grad_vec = jnp.stack([bias_query, bias_value, bias_out, bias_two])
    grad_gain = jnp.stack([gain_one, gain_two])
    grad_shift = jnp.stack([shift_one, shift_two])
    sum_qkv, sum_out, sum_in, sum_down, sum_vec, sum_ffn, sum_gain, sum_shift = (
        lax.psum_scatter(grad_qkv, ("dp", "seq"), scatter_dimension=0, tiled=True),
        lax.psum_scatter(grad_out, ("dp", "seq"), scatter_dimension=0, tiled=True),
        lax.psum_scatter(grad_in, ("dp", "seq"), scatter_dimension=0, tiled=True),
        lax.psum_scatter(grad_down, ("dp", "seq"), scatter_dimension=0, tiled=True),
        lax.psum_scatter(grad_vec, ("dp", "seq"), scatter_dimension=1, tiled=True),
        lax.psum_scatter(bias_ffn, ("dp", "seq"), scatter_dimension=0, tiled=True),
        lax.psum_scatter(grad_gain, ("dp", "seq"), scatter_dimension=1, tiled=True),
        lax.psum_scatter(grad_shift, ("dp", "seq"), scatter_dimension=1, tiled=True),
    )
    return (
        output.reshape(seq_count, local_len, model_width),
        input_grad.reshape(seq_count, local_len, model_width),
        sum_qkv,
        sum_out,
        sum_in,
        sum_down,
        sum_vec,
        sum_ffn,
        sum_gain,
        sum_shift,
    )


def solution(mesh):
    return jax.shard_map(
        on_device,
        mesh=mesh,
        in_specs=(
            P("dp", "seq", None),
            P("dp", None),
            P("dp", None, None),
            P("dp", None, None),
            P(("dp", "seq"), None),
            P(("dp", "seq"), None),
            P(("dp", "seq"), None),
            P(("dp", "seq"), None),
            P(None, ("dp", "seq")),
            P(("dp", "seq")),
            P(None, ("dp", "seq")),
            P(None, ("dp", "seq")),
            P("dp", "seq", None),
        ),
        out_specs=(
            P("dp", "seq", None),
            P("dp", "seq", None),
            P(("dp", "seq"), None),
            P(("dp", "seq"), None),
            P(("dp", "seq"), None),
            P(("dp", "seq"), None),
            P(None, ("dp", "seq")),
            P(("dp", "seq")),
            P(None, ("dp", "seq")),
            P(None, ("dp", "seq")),
        ),
        check_vma=False,
    )
```

profile of v0, /device:TPU:0, one launch (start us, length us, event | category | flops | bytes accessed | tf_op | source)
XLA Modules:
  0.0 1075.7 jit_solution(30104089791012242)
XLA Ops:
  8.0 65.9 %all-gather.12.cloned.1.call-done = bf16[768,2304]{1,0:T(8,128)(2,1)} async-done(((bf16[24,2304]{1,0:T(8,128)(2,1)}), bf16[768,2304]{1,0:T(8,128)(2,1)}) %all-gather.12.cloned.1.call-update) | async-done | bytes 3538960 | tf_op jit(solution)/shard_map/all_gather | solution.py:89
  77.5 66.3 %all-gather.2 = bf16[32,24,4]{1,2,0:T(4,128)(2,1)S(1)} all-gather(bf16[1,24,4]{1,2,0:T(4,128)(2,1)S(1)} %bitcast.172), channel_id=1, replica_groups=mesh['dp'=4,'seq'=8] {'dp','seq'}, dimensions={0}, use_global_device_ids=true | all-gather | bytes 6336 | tf_op jit(solution)/shard_map/all_gather | solution.py:93
  150.6 63.1 %all-gather.3 = bf16[32,24,2]{1,2,0:T(2,128)(2,1)S(1)} all-gather(bf16[1,24,2]{1,2,0:T(2,128)(2,1)S(1)} %bitcast.173), channel_id=1, replica_groups=mesh['dp'=4,'seq'=8] {'dp','seq'}, dimensions={0}, use_global_device_ids=true | all-gather | bytes 3168 | tf_op jit(solution)/shard_map/all_gather | solution.py:95
  213.9 65.2 %all-gather.4 = bf16[32,24,2]{1,2,0:T(2,128)(2,1)S(1)} all-gather(bf16[1,24,2]{1,2,0:T(2,128)(2,1)S(1)} %bitcast.174), channel_id=1, replica_groups=mesh['dp'=4,'seq'=8] {'dp','seq'}, dimensions={0}, use_global_device_ids=true | all-gather | bytes 3168 | tf_op jit(solution)/shard_map/all_gather | solution.py:96
  279.7 38.1 %all-reduce = bf16[3072]{0:T(1024)(128)(2,1)S(1)} all-reduce(bf16[3072]{0:T(1024)(128)(2,1)S(1)} %dynamic-update-slice), channel_id=1, replica_groups=mesh['dp'=4,'seq'=8] {'dp','seq'}, use_global_device_ids=true, to_apply=%add | all-reduce | flops 3072 | bytes 12288
  321.8 4.8 reshape.713
  326.6 5.5 copy.169
  334.2 4.8 reshape.708
  339.0 3.7 copy.179
  354.2 5.8 fusion.5
  360.0 13.8 %all-gather.18.cloned.1.call-done = bf16[3072,768]{1,0:T(8,128)(2,1)} async-done(((bf16[96,768]{1,0:T(8,128)(2,1)}), bf16[3072,768]{1,0:T(8,128)(2,1)}) %all-gather.18.cloned.1.call-update) | async-done | bytes 4718608 | tf_op jit(solution)/shard_map/all_gather | solution.py:92
  373.8 3.4 fusion.62
  386.3 9.2 convolution_bitcast_fusion.1
  395.6 11.4 %copy.190 = f32[2,10,64,12,64]{4,3,2,1,0:T(8,128)} copy(f32[2,10,64,12,64]{2,4,1,3,0:T(8,128)} %convolution_bitcast_fusion.1) | data formatting | bytes 7864320 | tf_op jit(solution)/shard_map/ghiej,gihd->gejhd/transpose | solution.py:232
  406.9 8.9 reshape.755
  416.1 7.7 scatter_fusion.1
  426.0 3.5 fusion.38
  437.0 10.2 copy.186
  447.2 9.0 reshape.747
  456.5 7.5 scatter_fusion
  468.7 5.1 fusion.56
  473.9 4.8 convert_reduce_fusion.1
  479.4 9.2 reduce-scatter.24.cloned.1.call-done
  489.7 66.4 %reduce-scatter.22.cloned.1.call-done = bf16[128,768]{1,0:T(8,128)(2,1)} async-done(((bf16[1024,768]{1,0:T(8,128)(2,1)}), bf16[128,768]{1,0:T(8,128)(2,1)}) %reduce-scatter.22.cloned.1.call-update) | async-done | bytes 196624
  557.2 3.9 convolution_bitcast_fusion
  561.1 8.0 copy.210
  570.4 5.1 fusion.53
  583.6 41.3 %all-reduce.5 = (f32[4,768]{1,0:T(4,128)}, f32[3072]{0:T(1024)}, f32[2,768]{1,0:T(2,128)}, f32[2,768]{1,0:T(2,128)}) all-reduce(f32[4,768]{1,0:T(4,128)S(1)} %pad_maximum_fusion.3, f32[3072]{0:T(1024)} %get-tuple-element.113, f32[2,768]{1,0:T(2,128)} %pad_maximum_fusion.4, ...), channel_id=10, replica_groups=mesh['dp'=4,'seq'=8] {'dp','seq'}, use_global_device_ids=true, to_apply=%region_28.29.clone | all-reduce | flops 9216 | bytes 73728
  633.5 26.4 %reduce-scatter.16.cloned.1.call-done = f32[24,768]{1,0:T(8,128)} async-done(((f32[768,768]{1,0:T(8,128)}), f32[24,768]{1,0:T(8,128)}) %reduce-scatter.16.cloned.1.call-update) | async-done | bytes 73744 | tf_op jit(solution)/shard_map/reduce_scatter | solution.py:262
  659.9 141.8 %reduce-scatter.18.cloned.1.call-done = f32[24,3072]{1,0:T(8,128)} async-done(((f32[768,3072]{1,0:T(8,128)}), f32[24,3072]{1,0:T(8,128)}) %reduce-scatter.18.cloned.1.call-update) | async-done | bytes 294928 | tf_op jit(solution)/shard_map/reduce_scatter | solution.py:263
  801.7 124.6 %reduce-scatter.26.cloned.1.call-done = f32[24,2304]{1,0:T(8,128)} async-done(((f32[768,2304]{1,0:T(8,128)}), f32[24,2304]{1,0:T(8,128)}) %reduce-scatter.26.cloned.1.call-update) | async-done | bytes 221200
  926.3 142.3 %reduce-scatter.20.cloned.1.call-done = f32[96,768]{1,0:T(8,128)} async-done(((f32[3072,768]{1,0:T(8,128)}), f32[96,768]{1,0:T(8,128)}) %reduce-scatter.20.cloned.1.call-update) | async-done | bytes 294928 | tf_op jit(solution)/shard_map/reduce_scatter | solution.py:264
  (234 shorter events, 73.6 us)
Async XLA Ops:
  7.2 139.5 %copy-start = (s32[1,16,3]{1,0,2:T(1,128)S(1)}, s32[1,16,3]{1,0,2:T(1,128)}, u32[]{:S(2)}) copy-start(s32[1,16,3]{1,0,2:T(1,128)} %param.15) | copy-start | bytes 580
  7.2 66.6 %all-gather.12.cloned.1.call-start = ((), (), s32[]{:S(2)}) async-start(), calls=%async_computation.6 | async-start | bytes 3649536 | tf_op jit(solution)/shard_map/all_gather | solution.py:89
  7.9 69.5 %copy-start.36 = (bf16[4,24]{1,0:T(4,128)(2,1)S(1)}, bf16[4,24]{1,0:T(4,128)(2,1)}, u32[]{:S(2)}) copy-start(bf16[4,24]{1,0:T(4,128)(2,1)} %param.21) | copy-start | bytes 580
  7.9 311.6 %all-gather.22.cloned.1.call-start = ((), (), s32[]{:S(2)}) async-start(), calls=%async_computation.14 | async-start | bytes 1769472 | tf_op jit(solution)/shard_map/all_gather | solution.py:107
  76.6 70.7 %copy-start.34 = (s32[1,1024]{1,0:T(1,128)S(1)}, s32[1,1024]{1,0:T(1,128)}, u32[]{:S(2)}) copy-start(s32[1,1024]{1,0:T(1,128)} %param.14) | copy-start | bytes 12292
  76.6 72.3 %copy-start.35 = (s32[1,6,2]{1,2,0:T(2,128)S(1)}, s32[1,6,2]{1,2,0:T(2,128)}, u32[]{:S(2)}) copy-start(s32[1,6,2]{1,2,0:T(2,128)} %param.16) | copy-start | bytes 148
  76.6 73.9 %copy-start.37 = (bf16[2,24]{1,0:T(2,128)(2,1)S(1)}, bf16[2,24]{1,0:T(2,128)(2,1)}, u32[]{:S(2)}) copy-start(bf16[2,24]{1,0:T(2,128)(2,1)} %param.23) | copy-start | bytes 292
  76.6 137.3 %copy-start.38 = (bf16[2,24]{1,0:T(2,128)(2,1)S(1)}, bf16[2,24]{1,0:T(2,128)(2,1)}, u32[]{:S(2)}) copy-start(bf16[2,24]{1,0:T(2,128)(2,1)} %param.24) | copy-start | bytes 292
  76.7 202.8 %copy-start.39 = (bf16[96]{0:T(256)(128)(2,1)S(1)}, bf16[96]{0:T(256)(128)(2,1)}, u32[]{:S(2)}) copy-start(bf16[96]{0:T(256)(128)(2,1)} %param.22) | copy-start | bytes 580
  77.4 254.7 %all-gather.20.cloned.1.call-start = ((), (), s32[]{:S(2)}) async-start(), calls=%async_computation.13 | async-start | bytes 1769472 | tf_op jit(solution)/shard_map/all_gather | solution.py:110
  144.8 207.3 %all-gather.14.cloned.1.call-start = ((), (), s32[]{:S(2)}) async-start(), calls=%async_computation.7 | async-start | bytes 1216512 | tf_op jit(solution)/shard_map/all_gather | solution.py:90
  145.4 208.7 %all-gather.16.cloned.1.call-start = ((), (), s32[]{:S(2)}) async-start(), calls=%async_computation.8 | async-start | bytes 4866048 | tf_op jit(solution)/shard_map/all_gather | solution.py:91
  146.0 227.7 %all-gather.18.cloned.1.call-start = ((), (), s32[]{:S(2)}) async-start(), calls=%async_computation.9 | async-start | bytes 4866048 | tf_op jit(solution)/shard_map/all_gather | solution.py:92
  146.6 342.0 %reduce-scatter.24.cloned.1.call-start = ((), (), s32[]{:S(2)}) async-start(), calls=%async_computation.16 | async-start | bytes 1769472
  319.1 27.8 %copy-start.10 = (pred[2,64,10,64]{1,3,2,0:T(8,128)(4,1)}, pred[2,64,10,64]{1,3,2,0:T(8,128)(4,1)S(1)}, u32[]{:S(2)}) copy-start(pred[2,64,10,64]{1,3,2,0:T(8,128)(4,1)S(1)} %compare_and_fusion) | copy-start | bytes 245764
  319.5 23.2 %copy-start.15 = (bf16[2,64,12,64]{1,0,3,2:T(2,128)(2,1)}, bf16[2,64,12,64]{1,0,3,2:T(2,128)(2,1)S(1)}, u32[]{:S(2)}) copy-start(bf16[2,64,12,64]{1,0,3,2:T(2,128)(2,1)S(1)} %reshape.710) | copy-start | bytes 589828
  342.7 6.8 copy-start.6
  354.1 29.8 %copy-start.32 = (f32[128]{0:T(128)}, f32[128]{0:T(128)S(1)}, u32[]{:S(2)}) copy-start(f32[128]{0:T(128)S(1)} %add_rsqrt_fusion.1) | copy-start | bytes 1540
  360.0 17.2 %copy-start.13 = (bf16[128,3072]{1,0:T(8,128)(2,1)}, bf16[128,3072]{1,0:T(8,128)(2,1)S(1)}, u32[]{:S(2)}) copy-start(bf16[128,3072]{1,0:T(8,128)(2,1)S(1)} %get-tuple-element.106) | copy-start | bytes 2359300
  373.7 5.4 slice-start
  373.8 5.4 slice-start.1
  386.3 9.3 copy-start.17
  425.1 131.0 %reduce-scatter.22.cloned.1.call-start = ((), (), s32[]{:S(2)}) async-start(), calls=%async_computation.15 | async-start | bytes 1769472
  465.4 194.5 %reduce-scatter.16.cloned.1.call-start = ((), (), s32[]{:S(2)}) async-start(), calls=%async_computation.10 | async-start | bytes 2433024 | tf_op jit(solution)/shard_map/reduce_scatter | solution.py:262
  468.7 333.0 %reduce-scatter.18.cloned.1.call-start = ((), (), s32[]{:S(2)}) async-start(), calls=%async_computation.11 | async-start | bytes 9732096 | tf_op jit(solution)/shard_map/reduce_scatter | solution.py:263
  473.9 452.4 %reduce-scatter.26.cloned.1.call-start = ((), (), s32[]{:S(2)}) async-start(), calls=%async_computation.17 | async-start | bytes 7299072
  478.7 78.5 %copy-start.24 = (bf16[1,128,768]{2,1,0:T(8,128)(2,1)S(1)}, bf16[1,128,768]{2,1,0:T(8,128)(2,1)}, u32[]{:S(2)}) copy-start(bf16[1,128,768]{2,1,0:T(8,128)(2,1)} %param.13) | copy-start | bytes 589828
  479.3 81.8 %copy-start.28 = (bf16[128,768]{0,1:T(8,128)(2,1)}, bf16[128,768]{0,1:T(8,128)(2,1)S(1)}, u32[]{:S(2)}) copy-start(bf16[128,768]{0,1:T(8,128)(2,1)S(1)} %reshape.717) | copy-start | bytes 589828
  489.7 71.4 %copy-start.20 = (bf16[128,768]{0,1:T(8,128)(2,1)}, bf16[128,768]{0,1:T(8,128)(2,1)S(1)}, u32[]{:S(2)}) copy-start(bf16[128,768]{0,1:T(8,128)(2,1)S(1)} %copy.209) | copy-start | bytes 589828
  569.2 499.4 %reduce-scatter.20.cloned.1.call-start = ((), (), s32[]{:S(2)}) async-start(), calls=%async_computation.12 | async-start | bytes 9732096 | tf_op jit(solution)/shard_map/reduce_scatter | solution.py:264
  575.5 54.7 %copy-start.8 = (bf16[768,2304]{1,0:T(8,128)(2,1)S(1)}, bf16[768,2304]{1,0:T(8,128)(2,1)}, u32[]{:S(2)}) copy-start(bf16[768,2304]{1,0:T(8,128)(2,1)} %all-gather.12.cloned.1.call-done) | copy-start | bytes 10616836
  628.8 439.8 %copy-start.1 = (s32[1,16,3]{1,0,2:T(1,128)S(1)}, s32[1,16,3]{1,0,2:T(1,128)}, u32[]{:S(2)}) copy-start(s32[1,16,3]{1,0,2:T(1,128)} %param.15) | copy-start | bytes 580
  (24 other events, 66.6 us)
Sparse Core Ops, SparseCore 0:
  10.9 62.8 all-gather.11
  77.5 42.8 all-gather.21
  145.0 41.4 all-gather.19
  189.3 52.9 all-gather.13
  245.0 63.5 all-gather.15
  311.4 62.3 all-gather.17
  425.3 63.2 reduce-scatter.23
  492.4 63.6 reduce-scatter.21
  562.0 97.8 reduce-scatter.15
  667.2 134.3 reduce-scatter.17
  807.9 118.2 reduce-scatter.25
  933.6 134.9 reduce-scatter.19
where the time goes:
time: 1080 us
  waiting for transfers between devices  593 us (55%)
  blocking collectives  274 us (25%)
  local copies, waits for them, and re-layouts  93.1 us (9%)
  matrix products  60.5 us (6%)
  other arithmetic  39.3 us (4%)
  between operations  15.3 us (1%)
    unnamed x15, waiting for transfers between devices  203 us
    reduce_scatter x1, waiting for transfers between devices, on_device(): lax.psum_scatter(grad_down, ('dp', 'seq'), scatter_dimension=0, tiled=True)  142 us
    reduce_scatter x1, waiting for transfers between devices, on_device(): lax.psum_scatter(grad_in, ('dp', 'seq'), scatter_dimension=0, tiled=True)  142 us
    unnamed x2, blocking collectives  79.4 us
    all_gather x1, blocking collectives, on_device(): lax.all_gather(vec_bias, ('dp', 'seq'), axis=1, tiled=True)  66.3 us
    all_gather x1, waiting for transfers between devices, on_device(): lax.all_gather(w_qkv, ('dp', 'seq'), axis=0, tiled=True)  65.9 us
    all_gather x1, blocking collectives, on_device(): lax.all_gather(norm_shift, ('dp', 'seq'), axis=1, tiled=True)  65.2 us
    all_gather x1, blocking collectives, on_device(): lax.all_gather(norm_gain, ('dp', 'seq'), axis=1, tiled=True)  63.1 us
  transfers between devices with their start and end apart: 12, of which 8 were waited for; matrix products, arithmetic and copies ran while one was open for 12% of the time, Pallas kernels for 0%

commit v1 on v0

v1 whole, which is shorter than its diff:
```python
import functools

import jax
import jax.numpy as jnp
import numpy as np
from jax import lax
from jax.experimental import pallas as pl
from jax.experimental.pallas import tpu as pltpu
from jax.sharding import PartitionSpec as P

HD = 64
BLK = 64
HEAD_GROUPS = 4
SCORE_CELLS = 512 * 1024

norm_eps = 1e-05
masked_score = -1e30
BOTH = ("dp", "seq")
bf16 = jnp.bfloat16
f32 = jnp.float32


def normalize(field_in):
    mean_row = jnp.mean(field_in, axis=-1, keepdims=True)
    centred = field_in - mean_row
    inverse = lax.rsqrt(jnp.mean(centred * centred, axis=-1, keepdims=True) + norm_eps)
    return (centred * inverse, inverse)


def norm_back(grad_in, normed, inverse, gain_row):
    weighted = grad_in * gain_row
    inner = jnp.mean(weighted * normed, axis=-1, keepdims=True)
    return inverse * (weighted - jnp.mean(weighted, axis=-1, keepdims=True) - normed * inner)


def gelu_slope(field_in):
    return (
        0.5 * (1.0 + lax.erf(field_in * 0.7071067811865476))
        + field_in * jnp.exp(-0.5 * field_in * field_in) * 0.3989422804014327
    )


def dot(left, right, left_dim=1, right_dim=0):
    return lax.dot_general(
        left, right, (((left_dim,), (right_dim,)), ((), ())), preferred_element_type=f32
    )


def call(body, outs, *args, name, scratch=(), flops=1e8, in_place=()):
    space = lambda i, a: (
        pl.ANY if i in in_place else pltpu.SMEM if a.dtype == jnp.int32 else pltpu.VMEM
    )
    specs = [pl.BlockSpec(memory_space=space(i, a)) for i, a in enumerate(args)]
    moved = sum(int(np.prod(a.shape)) * a.dtype.itemsize for a in args)
    return pl.pallas_call(
        body,
        in_specs=specs,
        out_specs=[pl.BlockSpec(memory_space=pltpu.VMEM)] * len(outs),
        out_shape=[jax.ShapeDtypeStruct(shape, dtype) for shape, dtype in outs],
        scratch_shapes=list(scratch),
        compiler_params=pltpu.CompilerParams(vmem_limit_bytes=56 * 1024 * 1024),
        cost_estimate=pl.CostEstimate(flops=int(flops), bytes_accessed=moved, transcendentals=0),
        name=name,
    )(*args)


def copies(pairs, sems):
    started = []
    for i, (source, target) in enumerate(pairs):
        copy = pltpu.make_async_copy(source, target, sems.at[i])
        copy.start()
        started.append(copy)
    return started


def exact(left, right, left_dim=1, right_dim=0):
    return lax.dot_general(
        left,
        right,
        (((left_dim,), (right_dim,)), ((), ())),
        preferred_element_type=f32,
        precision=lax.Precision.HIGHEST,
    )


def iota(shape, dim):
    return lax.broadcasted_iota(jnp.int32, shape, dim)


def spread_rows(row, rows, each):
    lanes = row.shape[1]
    picked = jnp.where(iota((rows, lanes), 1) // each == iota((rows, lanes), 0), row, 0.0)
    select = (iota((lanes, each), 0) % each == iota((lanes, each), 1)).astype(f32)
    return exact(picked, select)


def pick(options, index):
    chosen = options[0]
    for i, option in enumerate(options[1:]):
        chosen = jnp.where(index == i + 1, option, chosen)
    return chosen


def pack_kernel(unit_ids, place_ref, qkv_ref, out_ref, in_ref, vec_ref, ffn_ref, gain_ref, shift_ref, *outs):
    core, group = place_ref[0], place_ref[1]
    rows, width = out_ref.shape
    columns = width // HEAD_GROUPS
    rolled = lambda g: [
        qkv_ref[:, kind * width + g * columns : kind * width + (g + 1) * columns] for kind in (1, 2, 0)
    ]
    by_group = [jnp.concatenate(rolled(g), axis=1) for g in range(HEAD_GROUPS)]
    same_row = (iota((rows, rows), 0) == iota((rows, rows), 1)).astype(bf16)
    turned = [dot(same_row, ref[...], 1, 1) for ref in (vec_ref, gain_ref, shift_ref)]
    turned.append(spread_rows(ffn_ref[...].astype(f32), rows, ffn_ref.shape[1] // rows))
    small = jnp.concatenate(turned, axis=1).astype(bf16)
    for k in range(HEAD_GROUPS):
        chosen = pick(by_group, (group + k) % HEAD_GROUPS)
        rest = outs[k].shape[1] - 3 * columns - width - small.shape[1]
        outs[k][...] = jnp.concatenate(
            [chosen, out_ref[...], small, jnp.zeros((rows, rest), bf16)], axis=1
        )
    each = ffn_ref.shape[1]
    units = [
        jnp.concatenate([in_ref[:, i * each : (i + 1) * each] for i in ids], axis=1) for ids in unit_ids
    ]
    outs[HEAD_GROUPS][...] = jnp.where(core == 0, units[0], units[1])
    outs[HEAD_GROUPS + 1][...] = jnp.where(core == 0, units[1], units[0])


def qkv_kernel(x_ref, table_ref, sel_ref, q_ref, pair_ref):
    columns = sel_ref.shape[1]
    width = x_ref.shape[1]
    mixed = dot(x_ref[...], table_ref[:, : 3 * columns])
    small = table_ref[:, 3 * columns + width : 3 * columns + width + 4]
    biases = dot(small, sel_ref[...], 0, 0)
    keys = mixed[:, :columns]
    values = mixed[:, columns : 2 * columns] + biases[1:2]
    pair_ref[...] = jnp.concatenate([keys, values], axis=1).astype(bf16)
    q_ref[...] = ((mixed[:, 2 * columns :] + biases[0:1]) * HD ** (-0.5)).astype(bf16)


def unfold_kernel(small_each, table_ref, near_ref, line_ref, unit_ref, qkv_ref, out_ref, par_ref, ffn_ref):
    columns = qkv_ref.shape[1]
    width = out_ref.shape[1]
    qkv_ref[...] = dot(near_ref[...], table_ref[:, :columns]).astype(bf16)
    out_ref[...] = dot(line_ref[...], table_ref[:, columns : columns + width]).astype(bf16)
    small = table_ref[:, columns + width : columns + width + 8 + small_each]
    par_ref[...] = dot(small[:, :8], near_ref[...], 0, 1)
    by_slot = dot(small[:, 8:], unit_ref[...], 0, 0)
    slot = iota(by_slot.shape, 1) % small_each == iota(by_slot.shape, 0)
    ffn_ref[...] = jnp.sum(jnp.where(slot, by_slot, 0.0), axis=0, keepdims=True)


def head_mask(shape, head):
    lane = iota(shape, 1)
    return (lane >= head * HD) & (lane < (head + 1) * HD)


def split_pairs(pair_ref, k_ref, v_ref):
    width = k_ref.shape[1]
    k_ref[...] = pair_ref[:, :width]
    v_ref[...] = pair_ref[:, width:]


def forward_kernel(q_ref, kv_ref, b_ref, *refs):
    *o_refs, l_ref, k_ref, v_ref = refs
    step = pl.program_id(0)

    @pl.when(step == 0)
    def _():
        split_pairs(kv_ref, k_ref, v_ref)

    query, keys, values, bias = q_ref[...], k_ref[...], v_ref[...], b_ref[...]
    rows, width = query.shape
    out = jnp.zeros(query.shape, f32)
    logs = jnp.zeros(l_ref.shape, f32)
    for head in range(width // HD):
        mine = head_mask(query.shape, head)
        scores = dot(jnp.where(mine, query, jnp.zeros_like(query)), keys, 1, 1) + bias
        top = jnp.max(scores, axis=1, keepdims=True)
        terms = jnp.exp(scores - top)
        total = jnp.sum(terms, axis=1, keepdims=True)
        probs = (terms * (1.0 / total)).astype(bf16)
        out = out + jnp.where(mine, dot(probs, values), 0.0)
        logs = jnp.where(iota(l_ref.shape, 1) == head, top + jnp.log(total), logs)
    l_ref[...] = logs
    low = out.astype(bf16)
    piece = o_refs[0].shape[0]
    each = rows // piece
    for k, o_ref in enumerate(o_refs):
        start = (k % each) * piece

        @pl.when(step == k // each)
        def _(o_ref=o_ref, start=start):
            o_ref[...] = low[start : start + piece]


def backward_kernel(q_ref, kv_ref, b_ref, *refs):
    pieces, refs = refs[:HEAD_GROUPS], refs[HEAD_GROUPS:]
    l_ref, dq_ref, own_ref, send_ref, k_ref, v_ref, d_ref, dk_ref, dv_ref = refs
    step = pl.program_id(0)
    rows, width = q_ref.shape

    @pl.when(step == 0)
    def _():
        split_pairs(kv_ref, k_ref, v_ref)
        dk_ref[...] = jnp.zeros(dk_ref.shape, f32)
        dv_ref[...] = jnp.zeros(dv_ref.shape, f32)
        piece = pieces[0].shape[0]
        for k, ref in enumerate(pieces):
            d_ref[k * piece : (k + 1) * piece] = ref[...]

    query, keys, values, bias = q_ref[...], k_ref[...], v_ref[...], b_ref[...]
    d_att = d_ref[pl.ds(pl.multiple_of(step * rows, rows), rows)]
    logs = l_ref[...]
    d_query = jnp.zeros(query.shape, f32)
    for head in range(width // HD):
        mine = head_mask(query.shape, head)
        q_head = jnp.where(mine, query, jnp.zeros_like(query))
        d_head = jnp.where(mine, d_att, jnp.zeros_like(d_att))
        scores = dot(q_head, keys, 1, 1) + bias
        weights = jnp.exp(scores - logs[:, head : head + 1])
        d_probs = dot(d_head, values, 1, 1)
        delta = jnp.sum(weights * d_probs, axis=1, keepdims=True)
        d_scores = (weights * (d_probs - delta)).astype(bf16)
        d_query = d_query + jnp.where(mine, dot(d_scores, keys), 0.0)
        dk_ref[...] += dot(d_scores, q_head, 0, 0)
        dv_ref[...] += dot(weights.astype(bf16), d_head, 0, 0)
    dq_ref[...] = (d_query * HD ** (-0.5)).astype(bf16)

    @pl.when(step == pl.num_programs(0) - 1)
    def _():
        kept = own_ref.shape[0]
        own_ref[:, :width] = dk_ref[:kept]
        own_ref[:, width:] = dv_ref[:kept]
        send_ref[:, :width] = dk_ref[kept:].astype(bf16)
        send_ref[:, width:] = dv_ref[kept:].astype(bf16)


def attention_forward(query, pairs, bias):
    rows, width = query.shape
    key_rows = pairs.shape[0]
    tile = min(rows, SCORE_CELLS // key_rows)
    piece = rows // HEAD_GROUPS
    results = pl.pallas_call(
        forward_kernel,
        grid=(rows // tile,),
        in_specs=[
            pl.BlockSpec((tile, width), lambda i: (i, 0)),
            pl.BlockSpec((key_rows, 2 * width), lambda i: (0, 0)),
            pl.BlockSpec((tile, key_rows), lambda i: (i, 0)),
        ],
        out_specs=[pl.BlockSpec((piece, width), lambda i: (0, 0))] * HEAD_GROUPS
        + [pl.BlockSpec((tile, 128), lambda i: (i, 0))],
        out_shape=[jax.ShapeDtypeStruct((piece, width), bf16)] * HEAD_GROUPS
        + [jax.ShapeDtypeStruct((rows, 128), f32)],
        scratch_shapes=[pltpu.VMEM((key_rows, width), bf16)] * 2,
        compiler_params=pltpu.CompilerParams(vmem_limit_bytes=56 * 1024 * 1024),
        cost_estimate=pl.CostEstimate(
            flops=16 * rows * key_rows * width, bytes_accessed=4 * rows * key_rows, transcendentals=0
        ),
        name="attention_forward",
    )(query, pairs, bias)
    return results[:-1], results[-1]


def attention_backward(query, pairs, bias, d_pieces, logs):
    rows, width = query.shape
    key_rows = pairs.shape[0]
    tile = min(rows, SCORE_CELLS // key_rows)
    fixed = lambda n: pl.BlockSpec((n, 2 * width), lambda i: (0, 0))
    return pl.pallas_call(
        backward_kernel,
        grid=(rows // tile,),
        in_specs=[
            pl.BlockSpec((tile, width), lambda i: (i, 0)),
            fixed(key_rows),
            pl.BlockSpec((tile, key_rows), lambda i: (i, 0)),
        ]
        + [pl.BlockSpec(d_pieces[0].shape, lambda i: (0, 0))] * HEAD_GROUPS
        + [pl.BlockSpec((tile, 128), lambda i: (i, 0))],
        out_specs=[
            pl.BlockSpec((tile, width), lambda i: (i, 0)),
            fixed(rows),
            fixed(key_rows - rows),
        ],
        out_shape=[
            jax.ShapeDtypeStruct((rows, width), bf16),
            jax.ShapeDtypeStruct((rows, 2 * width), f32),
            jax.ShapeDtypeStruct((key_rows - rows, 2 * width), bf16),
        ],
        scratch_shapes=[pltpu.VMEM((key_rows, width), bf16)] * 2
        + [pltpu.VMEM((rows, width), bf16)]
        + [pltpu.VMEM((key_rows, width), f32)] * 2,
        compiler_params=pltpu.CompilerParams(vmem_limit_bytes=56 * 1024 * 1024),
        cost_estimate=pl.CostEstimate(
            flops=30 * rows * key_rows * width, bytes_accessed=4 * rows * key_rows, transcendentals=0
        ),
        name="attention_backward",
    )(query, pairs, bias, *d_pieces, logs)


def swap_blocks(a, flags, block):
    for step, flag in enumerate(flags):
        size = block << step
        blocks = [a[:, i : i + size] for i in range(0, a.shape[1], size)]
        flipped = [blocks[i ^ 1] for i in range(len(blocks))]
        a = jnp.where(flag == 1, jnp.concatenate(flipped, axis=1), a)
    return a


def ffn_forward_kernel(
    flag_count,
    block,
    flag_ref,
    att_ref,
    att_far_ref,
    x_ref,
    x_far_ref,
    par_ref,
    ffn_ref,
    out_hbm,
    mix_hbm,
    in_near_hbm,
    in_far_hbm,
    down_near_hbm,
    down_far_hbm,
    first_ref,
    normed_ref,
    inverse_ref,
    mixed_ref,
    hidden_ref,
    active_ref,
    part_ref,
    send_ref,
    out_ref,
    mix_ref,
    in_near_ref,
    in_far_ref,
    down_near_ref,
    down_far_ref,
    sems,
):
    waits = copies(
        [
            (out_hbm, out_ref),
            (mix_hbm, mix_ref),
            (in_near_hbm, in_near_ref),
            (in_far_hbm, in_far_ref),
            (down_near_hbm, down_near_ref),
            (down_far_hbm, down_far_ref),
        ],
        sems,
    )
    flags = [flag_ref[i] for i in range(flag_count)]
    attended = jnp.concatenate([att_ref[...], att_far_ref[...]], axis=0)
    tokens = jnp.concatenate([x_ref[...], x_far_ref[...]], axis=0).astype(f32)
    waits[0].wait()
    branch = dot(attended, out_ref[...]) + par_ref[2:3]
    normed, inverse = normalize(tokens + branch)
    first = normed * par_ref[4:5] + par_ref[6:7]
    first_ref[...] = first
    normed_ref[...] = normed
    inverse_ref[...] = jnp.broadcast_to(inverse, inverse_ref.shape)
    waits[1].wait()
    mixed = dot(first.astype(bf16), mix_ref[...]).astype(bf16)
    mixed_ref[...] = mixed
    half = mixed.shape[1] // 2
    waits[2].wait()
    hidden = dot(mixed[:, :half], in_near_ref[...])
    waits[3].wait()
    hidden = hidden + dot(mixed[:, half:], in_far_ref[...]) + ffn_ref[...]
    hidden = swap_blocks(hidden, flags, block)
    hidden_ref[...] = hidden
    active = (0.5 * hidden * (1.0 + lax.erf(hidden * 0.7071067811865476))).astype(bf16)
    active_ref[...] = active
    units = active.shape[1] // 2
    waits[4].wait()
    part = dot(active[:, :units], down_near_ref[...])
    waits[5].wait()
    part = part + dot(active[:, units:], down_far_ref[...])
    part_ref[...] = part
    send_ref[...] = part.astype(bf16)


def column_sum(a):
    return jnp.sum(a, axis=0, keepdims=True)


def ffn_backward_kernel(
    flag_count,
    block,
    flag_ref,
    part_ref,
    got_ref,
    first_ref,
    cot_ref,
    cot_far_ref,
    hidden_ref,
    par_ref,
    mix_hbm,
    in_near_hbm,
    in_far_hbm,
    down_near_hbm,
    down_far_hbm,
    output_ref,
    keep_ref,
    send_ref,
    second_ref,
    d_hidden_ref,
    sums_ref,
    ffn_sum_ref,
    mix_ref,
    in_near_ref,
    in_far_ref,
    down_near_ref,
    down_far_ref,
    sems,
):
    waits = copies(
        [
            (down_near_hbm, down_near_ref),
            (down_far_hbm, down_far_ref),
            (in_near_hbm, in_near_ref),
            (in_far_hbm, in_far_ref),
            (mix_hbm, mix_ref),
        ],
        sems,
    )
    flags = [flag_ref[i] for i in range(flag_count)]
    rows = got_ref.shape[0] // 2
    other = jnp.concatenate([got_ref[rows:], got_ref[:rows]], axis=0).astype(f32)
    normed, inverse = normalize(first_ref[...] + part_ref[...] + other + par_ref[3:4])
    gain = par_ref[5:6]
    output_ref[...] = (normed[:rows] * gain + par_ref[7:8]).astype(bf16)
    out_grad = jnp.concatenate([cot_ref[...], cot_far_ref[...]], axis=0).astype(f32)
    d_two = norm_back(out_grad, normed, inverse, gain)
    d_second = d_two.astype(bf16)
    second_ref[...] = d_second
    sums_ref[...] = jnp.concatenate(
        [
            column_sum(out_grad[:rows] * normed[:rows]),
            column_sum(out_grad[:rows]),
            column_sum(d_second[:rows].astype(f32)),
            jnp.zeros((5, normed.shape[1]), f32),
        ],
        axis=0,
    )
    waits[0].wait()
    near = dot(d_second, down_near_ref[...], 1, 1)
    waits[1].wait()
    far = dot(d_second, down_far_ref[...], 1, 1)
    slope = gelu_slope(hidden_ref[...])
    d_hidden = jnp.concatenate([near, far], axis=1) * slope
    d_hidden = swap_blocks(d_hidden, flags, block).astype(bf16)
    d_hidden_ref[...] = d_hidden
    ffn_sum_ref[...] = column_sum(d_hidden.astype(f32))
    waits[2].wait()
    near = dot(d_hidden, in_near_ref[...], 1, 1).astype(bf16)
    waits[3].wait()
    far = dot(d_hidden, in_far_ref[...], 1, 1).astype(bf16)
    waits[4].wait()
    part = dot(jnp.concatenate([near, far], axis=1), mix_ref[...], 1, 1)
    keep_ref[...] = d_two[:rows] + part[:rows]
    send_ref[...] = part[rows:].astype(bf16)


def branch_backward_kernel(
    keep_ref, got_ref, normed_ref, inverse_ref, par_ref, out_ref, d_one_ref, branch_ref, sums_ref, *pieces
):
    d_first = keep_ref[...] + got_ref[...].astype(f32)
    normed, inverse = normed_ref[...], inverse_ref[:, :1]
    d_one = norm_back(d_first, normed, inverse, par_ref[4:5])
    d_one_ref[...] = d_one
    d_branch = d_one.astype(bf16)
    branch_ref[...] = d_branch
    sums_ref[...] = jnp.concatenate(
        [
            column_sum(d_first * normed),
            column_sum(d_first),
            column_sum(d_branch.astype(f32)),
            jnp.zeros((5, normed.shape[1]), f32),
        ],
        axis=0,
    )
    d_attended = dot(d_branch, out_ref[...], 1, 1).astype(bf16)
    columns = pieces[0].shape[1]
    for k, piece in enumerate(pieces):
        piece[...] = d_attended[:, k * columns : (k + 1) * columns]


def early_grads_kernel(
    small_each,
    x_ref,
    dq_ref,
    att_ref,
    branch_ref,
    sums_ref,
    sums_two_ref,
    ffn_ref,
    sel_ref,
    near_ref,
    line_ref,
    unit_ref,
    qkv_ref,
    keep_ref,
    send_ref,
    back_ref,
):
    columns = dq_ref.shape[1]
    d_query = dq_ref[...]
    back_ref[...] = dot(d_query, qkv_ref[:, 2 * columns :], 1, 1)
    queries = dot(x_ref[...], d_query, 0, 0)
    attended = dot(att_ref[...], line_ref[...]).astype(bf16)
    outs = dot(attended, branch_ref[...], 0, 0)
    sums = jnp.concatenate([column_sum(d_query.astype(f32)), jnp.zeros((7, columns), f32)], axis=0)
    biases = dot(sel_ref[...], sums.astype(bf16), 1, 1)[:, :2]
    first, second = sums_ref[...], sums_two_ref[...]
    vectors = jnp.concatenate(
        [first[2:3], second[2:3], first[0:1], second[0:1], first[1:2], second[1:2], first[3:5]], axis=0
    )
    vectors = dot(near_ref[...], vectors.astype(bf16), 0, 1)[:, :6]
    units = ffn_ref.shape[1]
    slot = iota((8, units), 1) % small_each == iota((8, units), 0)
    by_slot = jnp.where(slot, ffn_ref[...], 0.0).astype(bf16)
    ffn = dot(unit_ref[...], by_slot, 1, 1)[:, :small_each]
    total = [queries, outs, biases, vectors, ffn]
    rest = keep_ref.shape[1] - sum(a.shape[1] for a in total)
    total = jnp.concatenate([*total, jnp.zeros((queries.shape[0], rest), f32)], axis=1)
    half = total.shape[0] // 2
    keep_ref[...] = total[:half]
    send_ref[...] = total[half:].astype(bf16)


def late_grads_kernel(
    x_ref, own_ref, got_ref, sel_ref, qkv_ref, early_ref, early_send_ref, early_back_ref, *outs
):
    keep_ref, send_ref, back_ref, *back_pieces = outs
    pair_columns = own_ref.shape[1]
    columns = pair_columns // 2
    d_pairs = (own_ref[...] + got_ref[...].astype(f32)).astype(bf16)
    grad_back = early_back_ref[...] + dot(d_pairs, qkv_ref[:, :pair_columns], 1, 1)
    rows = back_ref.shape[0]
    back_ref[...] = grad_back[:rows]
    for k, piece in enumerate(back_pieces):
        piece[...] = grad_back[(k + 1) * rows : (k + 2) * rows].astype(bf16)
    pairs = dot(x_ref[...], d_pairs, 0, 0)
    sums = [jnp.zeros((1, columns), f32), column_sum(d_pairs[:, columns:].astype(f32))]
    sums = jnp.concatenate([*sums, jnp.zeros((6, columns), f32)], axis=0)
    bias = dot(sel_ref[...], sums.astype(bf16), 1, 1)[:, 1:2]
    half = pairs.shape[0] // 2
    width = x_ref.shape[1]
    at = columns + width + 1
    lane = iota(early_ref.shape, 1)
    keep_ref[:, :pair_columns] = pairs[:half]
    keep_ref[:, pair_columns:] = early_ref[...] + jnp.where(lane == at, bias[:half], 0.0)
    send_ref[:, :pair_columns] = pairs[half:].astype(bf16)
    late = early_send_ref[...].astype(f32) + jnp.where(lane == at, bias[half:], 0.0)
    send_ref[:, pair_columns:] = late.astype(bf16)


def finish_kernel(small_each, place_ref, own_ref, *refs):
    pieces, outs = refs[: HEAD_GROUPS - 1], refs[HEAD_GROUPS - 1 :]
    qkv_ref, out_ref, vec_ref, ffn_ref, gain_ref, shift_ref = outs
    group = place_ref[1]
    rows, width = out_ref.shape
    columns = width // HEAD_GROUPS
    line = [own_ref[...]] + [piece[...].astype(f32) for piece in pieces]
    for g in range(HEAD_GROUPS):
        mine = pick([a[:, : 3 * columns] for a in line], (g - group) % HEAD_GROUPS)
        for kind, at in enumerate((2, 0, 1)):
            start = kind * width + g * columns
            qkv_ref[:, start : start + columns] = mine[:, at * columns : (at + 1) * columns]
    rest = sum(a[:, 3 * columns :] for a in line[1:]) + line[0][:, 3 * columns :]
    out_ref[...] = rest[:, :width]
    small = rest[:, width : width + 8 + small_each]
    same_row = (iota((rows, rows), 0) == iota((rows, rows), 1)).astype(f32)
    turned = exact(small[:, :8], same_row, 0, 0)
    vec_ref[...] = turned[:4]
    gain_ref[...] = turned[4:6]
    shift_ref[...] = turned[6:8]
    each = small.shape[1] - 8
    lanes = rows * each
    select = (iota((each, lanes), 1) % each == iota((each, lanes), 0)).astype(f32)
    wide = exact(small[:, 8:], select)
    mine = iota((rows, lanes), 1) // each == iota((rows, lanes), 0)
    ffn_ref[...] = column_sum(jnp.where(mine, wide, 0.0))


def units_kernel(unit_ids, place_ref, keep_ref, got_ref, out_ref):
    core = place_ref[0]
    keep, got = keep_ref[...], got_ref[...].astype(f32)
    sources = [jnp.where(core == 0, keep, got), jnp.where(core == 0, got, keep)]
    count = 2 * len(unit_ids[0])
    each = out_ref.shape[1] // count
    blocks = {}
    for c, ids in enumerate(unit_ids):
        for slot, device in enumerate(ids):
            blocks[int(device)] = sources[c][:, slot * each : (slot + 1) * each]
    out_ref[...] = jnp.concatenate([blocks[i] for i in range(count)], axis=1)


class Grid:
    def __init__(self, mesh):
        self.dp, self.seq = mesh.shape["dp"], mesh.shape["seq"]
        self.count = self.dp * self.seq
        self.xs, self.parts = self.dp // 2, self.seq // HEAD_GROUPS
        bits = lambda axis, size: [(axis, b) for b in range(size.bit_length() - 1)]
        x_bits, self.part_bits = bits("x", self.xs), bits("q", self.parts)
        self.group_bits = [("g", 1), ("g", 0)]
        alternate = len(x_bits) == len(self.part_bits)
        self.plane = (
            x_bits + self.part_bits,
            self.part_bits + x_bits if alternate else x_bits + self.part_bits,
        )
        self.core_bit = [(("c", 0), ("c", 0))]
        self.plane_bits = list(zip(*self.plane))

    def place(self, device):
        dp, seq = divmod(device, self.seq)
        return {"x": dp // 2, "c": dp % 2, "g": seq // self.parts, "q": seq % self.parts}

    def device(self, at):
        return (at["x"] * 2 + at["c"]) * self.seq + at["g"] * self.parts + at["q"]

    def flip(self, bits_of_core):
        pairs = []
        for device in range(self.count):
            at = self.place(device)
            axis, bit = bits_of_core[at["c"]]
            at[axis] ^= 1 << bit
            pairs.append((device, self.device(at)))
        return pairs

    def shift(self, by):
        pairs = []
        for device in range(self.count):
            at = self.place(device)
            at["g"] = (at["g"] + by) % HEAD_GROUPS
            pairs.append((device, self.device(at)))
        return pairs

    def plane_masks(self, core):
        masks = {"x": [], "q": []}
        for index in range(self.xs * self.parts):
            for axis in masks:
                flips = [
                    1 << bit
                    for step, (a, bit) in enumerate(self.plane[core])
                    if a == axis and (index >> step) & 1
                ]
                masks[axis].append(sum(flips))
        return {axis: np.array(m, np.int32) for axis, m in masks.items()}


def same(bits):
    return [(bit, bit) for bit in bits]


def swap(grid, held, bits):
    return lax.ppermute(held, BOTH, grid.flip(bits))


def gather_near(grid, held, bit_pairs):
    for pair in bit_pairs:
        held = jnp.concatenate([held, swap(grid, held, pair)], axis=0)
    return held


def reduce_near(grid, total, bit_pairs):
    for pair in reversed(bit_pairs):
        half = total.shape[0] // 2
        got = swap(grid, total[half:].astype(bf16), pair)
        total = total[:half].astype(f32) + got.astype(f32)
    return total


def line_send(grid, pieces, sign):
    return [
        lax.ppermute(piece, BOTH, grid.shift(sign * (k + 1))) for k, piece in enumerate(pieces)
    ]


def tie(*values):
    return lax.optimization_barrier(values)


def on_device(
    grid,
    inputs,
    segments,
    rand_blocks,
    glob_blocks,
    w_qkv,
    w_out,
    w_in,
    w_down,
    vec_bias,
    ffn_bias,
    norm_gain,
    norm_shift,
    cotangent,
):
    local_len, width = inputs.shape[1:]
    rows_each, ff_each = w_in.shape[0], w_down.shape[0]
    ff = w_in.shape[1]
    ff_half = ff // 2
    groups, parts, xs = HEAD_GROUPS, grid.parts, grid.xs
    planes = xs * parts
    columns = width // groups
    line_len = groups * local_len
    small_each = ff_each // rows_each
    table_width = -(-(3 * columns + width + 8 + small_each) // 128) * 128
    dp_place, seq_place = lax.axis_index("dp"), lax.axis_index("seq")
    core, group, part = dp_place % 2, seq_place // parts, seq_place % parts
    coords = {"x": dp_place // 2, "c": core, "g": group, "q": part}
    place = jnp.stack([core, group]).astype(jnp.int32)
    chip_swap = lambda a: swap(grid, a, grid.core_bit[0])
    group_order = np.array([0, 2, 1, 3])
    group_slot = lambda g: (g % 2) * 2 + g // 2
    tokens = inputs.reshape(local_len, width)
    cot = cotangent.reshape(local_len, width)
    part_bits = same(grid.part_bits)

    masks = [grid.plane_masks(c) for c in range(2)]
    unit_ids = []
    for c in range(2):
        ids = [
            grid.device({"x": masks[c]["x"][index], "c": c, "g": g, "q": masks[c]["q"][index]})
            for index in range(planes)
            for g in group_order
        ]
        unit_ids.append(np.array(ids))

    *packets, own_units, far_units = call(
        functools.partial(pack_kernel, unit_ids),
        [((rows_each, table_width), bf16)] * groups
        + [((rows_each, ff_half), bf16)] * 2,
        place,
        w_qkv,
        w_out,
        w_in,
        vec_bias,
        ffn_bias.reshape(1, ff_each),
        norm_gain,
        norm_shift,
        name="pack_weights",
        scratch=(),
    )
    got_packets = line_send(grid, packets[1:], 1)

    plane_x = [coords["x"] ^ jnp.asarray(masks[c]["x"]) for c in range(2)]
    plane_q = [part ^ jnp.asarray(masks[c]["q"]) for c in range(2)]
    line_groups = (group - jnp.arange(groups, dtype=jnp.int32)) % groups
    row = jnp.arange(rows_each, dtype=jnp.int32)
    row_ids = jnp.arange(width, dtype=jnp.int32)
    by_core = lambda c, pair: jnp.where(c == 0, pair[0], pair[1])

    def device_of(x, c, g, q):
        return (x * 2 + c) * grid.seq + g * parts + q

    near_ids = jnp.stack(
        [
            device_of(by_core(c, plane_x)[:, None], c, line_groups[None, :], by_core(c, plane_q)[:, None])
            for c in (core, 1 - core)
        ]
    )
    near_rows = (near_ids[..., None] * rows_each + row).reshape(width)
    to_near = (row_ids[:, None] == near_rows[None, :]).astype(bf16)
    line_rows = (row_ids + group * columns) % width
    line_near = (line_rows[:, None] == near_rows[None, :]).astype(bf16)
    group_rows = group * columns + jnp.arange(columns, dtype=jnp.int32)
    near_group = (near_rows[:, None] == group_rows[None, :]).astype(bf16)
    own_x, own_q = by_core(core, plane_x), by_core(core, plane_q)
    slot_groups = jnp.asarray(group_order, jnp.int32)
    piece_ids = jnp.stack(
        [
            device_of(own_x[:, None], c, slot_groups[None, :], own_q[:, None])
            for c in (core, 1 - core)
        ],
        axis=2,
    )
    piece_rows = (piece_ids[..., None] * rows_each + row).reshape(width)
    to_piece = (row_ids[:, None] == piece_rows[None, :]).astype(bf16)
    own_ids = by_core(core, [jnp.asarray(ids, jnp.int32) for ids in unit_ids])
    unit = jnp.arange(ff_half, dtype=jnp.int32)
    unit_rows = jnp.repeat(own_ids, ff_each) * rows_each + (unit % ff_each) // small_each
    near_unit = (near_rows[:, None] == unit_rows[None, :]).astype(bf16)

    flags = [
        by_core(core, [(coords[axis] >> bit) & 1 for axis, bit in pair]) for pair in grid.plane_bits
    ]
    unit_block = ff_half // planes
    aligned = unit_block % 128 == 0
    kernel_flags = len(flags) if aligned else 0
    flag_row = jnp.stack(flags).astype(jnp.int32)
    outer_swap = (lambda a: a) if aligned else (lambda a: swap_blocks(a, flags, unit_block))

    own_blocks = local_len // BLK
    part_near = part ^ jnp.arange(parts, dtype=jnp.int32)
    chunk_ids = (line_groups[None, :] * parts + part_near[:, None]).reshape(-1)
    chunk_hot = chunk_ids[:, None] == jnp.arange(grid.seq, dtype=jnp.int32)[None, :]

    def take_chunks(chunks, hot):
        return jnp.sum(jnp.where(hot[:, :, None], chunks[None], 0), axis=1)

    offsets = jnp.arange(local_len, dtype=jnp.int32) // BLK
    block_near = (chunk_ids[:, None] * own_blocks + offsets[None, :]).reshape(-1)
    seg_near = take_chunks(segments.reshape(grid.seq, local_len), chunk_hot).reshape(-1)
    rand_line = take_chunks(rand_blocks.reshape(grid.seq, -1), chunk_hot[:groups])
    rand_line = rand_line.reshape(groups, own_blocks, 1, -1)
    rand_rows = jnp.broadcast_to(rand_line, (groups, own_blocks, BLK, rand_line.shape[-1]))
    rand_rows = rand_rows.reshape(line_len, -1)
    key_block, key_seg = block_near[None, :], seg_near[None, :]
    query_block, query_seg = block_near[:line_len, None], seg_near[:line_len, None]
    near = (key_block >= query_block - 1) & (key_block <= query_block + 1)
    for entry in range(rand_rows.shape[1]):
        near = near | (key_block == rand_rows[:, entry : entry + 1])
    glob_table = glob_blocks[0]
    doc = jnp.arange(glob_table.shape[0], dtype=jnp.int32)[None, :]
    for entry in range(glob_table.shape[1]):
        picked = jnp.sum(
            jnp.where(query_seg == doc, glob_table[None, :, entry], 0), axis=1, keepdims=True
        )
        near = near | (key_block == picked)
    mask_bias = jnp.where(near & (query_seg == key_seg), 0.0, masked_score).astype(f32)

    def group_step(held, entry):
        axis, bit = grid.group_bits[entry]
        got = swap(grid, held, ((axis, bit), (axis, bit)))
        upper = (group >> bit) & 1 == 1
        return jnp.where(upper, jnp.concatenate([got, held]), jnp.concatenate([held, got]))

    def plane_gather(held):
        for pair in grid.plane_bits[:-1]:
            held = jnp.concatenate([held, swap(grid, held, pair)], axis=0)
        return held

    got_units = chip_swap(far_units)
    down = group_step(w_down[None], 0)
    packet, sent_tokens = tie(packets[0], tokens)
    got_tokens = line_send(grid, [sent_tokens] * (groups - 1), 1)
    table = jnp.concatenate([packet, *got_packets], axis=0)
    units = jnp.concatenate([own_units, got_units], axis=0)[None]
    table, units, down = tie(table, units, down)
    down, units = group_step(down, 1), group_step(units, 0)
    table = gather_near(grid, table, grid.plane_bits)
    table, units, down = tie(table, units, down)
    units = group_step(units, 1)
    down_near = plane_gather(down.reshape(-1, width))
    table = gather_near(grid, table, grid.core_bit)
    table, *got_tokens = tie(table, *got_tokens)
    x_line = jnp.concatenate([tokens, *got_tokens], axis=0)
    x_near = dot(x_line, to_near).astype(bf16)

    query, own_pairs = call(
        qkv_kernel,
        [((line_len, columns), bf16), ((line_len, 2 * columns), bf16)],
        x_near,
        table,
        near_group,
        name="project",
    )
    own_pairs, units, down_near = tie(own_pairs, units, down_near)
    down_far = swap(grid, down_near, grid.plane_bits[-1])
    x_far, cot_far = chip_swap(tokens), chip_swap(cot)
    qkv_slice, out_line, params, ffn_row = call(
        functools.partial(unfold_kernel, small_each),
        [
            ((width, 3 * columns), bf16),
            ((width, width), bf16),
            ((8, width), f32),
            ((1, ff_half), f32),
        ],
        table,
        to_near,
        line_near,
        near_unit,
        name="unfold_weights",
    )
    ffn_row = outer_swap(ffn_row)
    kept_pairs, out_line, params, to_piece = tie(own_pairs, out_line, params, to_piece)
    pairs = jnp.concatenate([kept_pairs, swap(grid, own_pairs, part_bits[0])], axis=0)
    pairs = gather_near(grid, pairs, part_bits[1:])

    in_near = plane_gather(units.reshape(-1, ff_half))
    pairs, in_near = tie(pairs, in_near)
    in_far = swap(grid, in_near, grid.plane_bits[-1])
    in_near, in_far = outer_swap(in_near), outer_swap(in_far)

    att_pieces, logs = attention_forward(query, pairs, mask_bias)
    got_att = line_send(grid, att_pieces[1:], -1)
    attended = jnp.concatenate([att_pieces[0], *got_att], axis=1)
    attended_far = chip_swap(attended)

    half = width // 2
    chip_len = 2 * local_len
    weight_scratch = lambda *arrays: [pltpu.VMEM(a.shape, bf16) for a in arrays]
    first, normed, inverse, mixed, hidden, active, part_own, part_send = call(
        functools.partial(ffn_forward_kernel, kernel_flags, unit_block),
        [
            ((chip_len, width), f32),
            ((chip_len, width), f32),
            ((chip_len, 128), f32),
            ((chip_len, width), bf16),
            ((chip_len, ff_half), f32),
            ((chip_len, ff_half), bf16),
            ((chip_len, width), f32),
            ((chip_len, width), bf16),
        ],
        flag_row,
        attended,
        attended_far,
        tokens,
        x_far,
        params,
        ffn_row,
        out_line,
        to_piece,
        in_near,
        in_far,
        down_near,
        down_far,
        name="ffn_forward",
        in_place=(7, 8, 9, 10, 11, 12),
        scratch=weight_scratch(out_line, to_piece, in_near, in_far, down_near, down_far)
        + [pltpu.SemaphoreType.DMA((6,))],
    )
    part_got = chip_swap(part_send)

    output, first_keep, first_send, d_second, d_hidden, sums_two, ffn_sums = call(
        functools.partial(ffn_backward_kernel, kernel_flags, unit_block),
        [
            ((local_len, width), bf16),
            ((local_len, width), f32),
            ((local_len, width), bf16),
            ((chip_len, width), bf16),
            ((chip_len, ff_half), bf16),
            ((8, width), f32),
            ((1, ff_half), f32),
        ],
        flag_row,
        part_own,
        part_got,
        first,
        cot,
        cot_far,
        hidden,
        params,
        to_piece,
        in_near,
        in_far,
        down_near,
        down_far,
        name="ffn_backward",
        in_place=(8, 9, 10, 11, 12),
        scratch=weight_scratch(to_piece, in_near, in_far, down_near, down_far)
        + [pltpu.SemaphoreType.DMA((5,))],
    )
    first_got = chip_swap(first_send)
    down_send = dot(active[:, width:], d_second, 0, 0).astype(bf16)
    down_keep = dot(active[:, :width], d_second, 0, 0).astype(bf16)
    d_hidden, ffn_sums = outer_swap(d_hidden), outer_swap(ffn_sums)
    in_send = dot(mixed[:, half:], d_hidden, 0, 0).astype(bf16)
    in_keep = dot(mixed[:, :half], d_hidden, 0, 0).astype(bf16)
    d_one, d_branch, sums_one, *d_pieces = call(
        branch_backward_kernel,
        [((local_len, width), f32), ((local_len, width), bf16), ((8, width), f32)]
        + [((local_len, columns), bf16)] * groups,
        first_keep,
        first_got,
        normed[:local_len],
        inverse[:local_len],
        params,
        out_line,
        name="branch_backward",
    )
    got_d_att = line_send(grid, d_pieces[1:], 1)

    def far_sum(keep, send):
        return keep.astype(f32) + swap(grid, send, grid.plane_bits[-1]).astype(f32)

    down_total = far_sum(down_keep, down_send)
    in_total = far_sum(in_keep, in_send)

    def line_sum(total):
        total = total.reshape(groups, -1, total.shape[1])
        piece = lambda k: lax.dynamic_index_in_dim(
            total, group_slot((group + k) % groups), 0, keepdims=False
        )
        got = line_send(grid, [piece(k).astype(bf16) for k in range(1, groups)], 1)
        return sum((g.astype(f32) for g in got), piece(0))

    d_query, pairs_own, pairs_send = attention_backward(
        query, pairs, mask_bias, [d_pieces[0], *got_d_att], logs
    )
    pairs_own, pairs_send, down_total, in_total = tie(pairs_own, pairs_send, down_total, in_total)
    down_total = reduce_near(grid, down_total, grid.plane_bits[:-1])
    in_total = reduce_near(grid, in_total, grid.plane_bits[:-1])
    if parts == 2:
        pairs_got = swap(grid, pairs_send, part_bits[0])
    else:
        pairs_all = jnp.concatenate([pairs_own, pairs_send.astype(f32)])
        pairs_own = reduce_near(grid, pairs_all, part_bits)
        pairs_got = jnp.zeros(pairs_own.shape, bf16)
    early_width = table_width - 2 * columns
    early, early_send, early_back = call(
        functools.partial(early_grads_kernel, small_each),
        [
            ((width // 2, early_width), f32),
            ((width // 2, early_width), bf16),
            ((line_len, width), f32),
        ],
        x_near,
        d_query,
        attended,
        d_branch,
        sums_one,
        sums_two,
        ffn_sums,
        near_group,
        to_near,
        line_near,
        near_unit,
        qkv_slice,
        name="early_gradients",
    )
    pairs_own, down_total, early = tie(pairs_own, down_total, early)
    grad_keep, grad_send, back_own, *back_pieces = call(
        late_grads_kernel,
        [
            ((width // 2, table_width), f32),
            ((width // 2, table_width), bf16),
            ((local_len, width), f32),
        ]
        + [((local_len, width), bf16)] * (groups - 1),
        x_near,
        pairs_own,
        pairs_got,
        near_group,
        qkv_slice,
        early,
        early_send,
        early_back,
        name="late_gradients",
    )
    grad_send, in_total = tie(grad_send, in_total)
    sum_down = line_sum(down_total)
    in_pairs = line_sum(in_total)
    got_back = line_send(grid, back_pieces, -1)
    total = grad_keep + chip_swap(grad_send).astype(f32)
    total = reduce_near(grid, total, grid.plane_bits)
    total, in_pairs, d_one = tie(total, in_pairs, d_one)
    in_got = chip_swap(in_pairs[rows_each:])
    (sum_in,) = call(
        functools.partial(units_kernel, unit_ids),
        [((rows_each, ff), f32)],
        place,
        in_pairs[:rows_each],
        in_got,
        name="order_units",
    )

    got_total = line_send(
        grid, [total[k * rows_each : (k + 1) * rows_each].astype(bf16) for k in range(1, groups)], -1
    )
    input_grad = d_one + sum((g.astype(f32) for g in got_back), back_own)
    sum_qkv, sum_out, sum_vec, sum_ffn, sum_gain, sum_shift = call(
        functools.partial(finish_kernel, small_each),
        [
            ((rows_each, 3 * width), f32),
            ((rows_each, width), f32),
            ((4, rows_each), f32),
            ((1, ff_each), f32),
            ((2, rows_each), f32),
            ((2, rows_each), f32),
        ],
        place,
        total[:rows_each],
        *got_total,
        name="finish",
    )
    return (
        output[None],
        input_grad[None],
        sum_qkv,
        sum_out,
        sum_in,
        sum_down,
        sum_vec,
        sum_ffn.reshape(ff_each),
        sum_gain,
        sum_shift,
    )


def solution(mesh):
    return jax.shard_map(
        functools.partial(on_device, Grid(mesh)),
        mesh=mesh,
        in_specs=(
            P("dp", "seq", None),
            P("dp", None),
            P("dp", None, None),
            P("dp", None, None),
            P(("dp", "seq"), None),
            P(("dp", "seq"), None),
            P(("dp", "seq"), None),
            P(("dp", "seq"), None),
            P(None, ("dp", "seq")),
            P(("dp", "seq")),
            P(None, ("dp", "seq")),
            P(None, ("dp", "seq")),
            P("dp", "seq", None),
        ),
        out_specs=(
            P("dp", "seq", None),
            P("dp", "seq", None),
            P(("dp", "seq"), None),
            P(("dp", "seq"), None),
            P(("dp", "seq"), None),
            P(("dp", "seq"), None),
            P(None, ("dp", "seq")),
            P(("dp", "seq")),
            P(None, ("dp", "seq")),
            P(None, ("dp", "seq")),
        ),
        check_vma=False,
    )
```

time: 1080 us -> 261 us (0.24)
  waiting for transfers between devices: 593 us -> 72 us
  blocking collectives: 274 us -> 0 us
  local copies, waits for them, and re-layouts: 93.1 us -> 11.9 us
  starting transfers between devices: 0.69 us -> 74.7 us
  Pallas kernels: 0 us -> 63.2 us
  matrix products: 60.5 us -> 7.37 us
  between operations: 15.3 us -> 1.29 us
    reduce_scatter x3 -> x0, waiting for transfers between devices: 311 us -> none  [the longest x1 142 us: on_device(): lax.psum_scatter(grad_down, ('dp', 'seq'), scatter_dimension=0, tiled=True)]
    unnamed x15 -> x0, waiting for transfers between devices: 203 us -> none
    all_gather x3 -> x0, blocking collectives: 195 us -> none  [the longest x1 66.3 us: on_device(): lax.all_gather(vec_bias, ('dp', 'seq'), axis=1, tiled=True)]
    all_gather x6 -> x0, waiting for transfers between devices: 79.7 us -> none  [the longest x1 65.9 us: on_device(): lax.all_gather(w_qkv, ('dp', 'seq'), axis=0, tiled=True)]
    unnamed x2 -> x0, blocking collectives: 79.4 us -> none
    ppermute x0 -> x51, starting transfers between devices: none -> 74.7 us  [the longest x24 37.9 us: line_send(): lax.ppermute(piece, BOTH, grid.shift(sign * (k + 1)))]
    ppermute x0 -> x51, waiting for transfers between devices: none -> 72 us  [the longest x27 40.2 us: swap(): return lax.ppermute(held, BOTH, grid.flip(bits))]
    pallas_call x0 -> x12, Pallas kernels: none -> 63.2 us  [the longest x10 48 us: call(): pl.pallas_call(body, in_specs=specs, out_specs=[pl.BlockSpec(memory_space...]
  transfers between devices with their start and end apart: 12 -> 51, of which waited for: 8 -> 24; matrix products, arithmetic and copies ran while one was open for 12% -> 14% of each run, Pallas kernels for 0% -> 13%
where the time goes in v1:
time: 261 us
  starting transfers between devices  74.7 us (29%)
  waiting for transfers between devices  72 us (28%)
  Pallas kernels  63.2 us (24%)
  other arithmetic  30 us (11%)
  local copies, waits for them, and re-layouts  11.9 us (5%)
  matrix products  7.37 us (3%)
    pallas_call x10, Pallas kernels, call(): pl.pallas_call(body, in_specs=specs, out_specs=[pl.BlockSpec(memory_space...  48 us
    ppermute x27, waiting for transfers between devices, swap(): return lax.ppermute(held, BOTH, grid.flip(bits))  40.2 us
    ppermute x24, starting transfers between devices, line_send(): lax.ppermute(piece, BOTH, grid.shift(sign * (k + 1)))  37.9 us
    ppermute x27, starting transfers between devices, swap(): return lax.ppermute(held, BOTH, grid.flip(bits))  36.8 us
    ppermute x24, waiting for transfers between devices, line_send(): lax.ppermute(piece, BOTH, grid.shift(sign * (k + 1)))  31.8 us
    pallas_call x1, Pallas kernels, attention_backward(): pl.pallas_call(backward_kernel, grid=(rows // tile,), in_specs=[pl.BlockS...  9.08 us
    dot_general x5, matrix products, dot(): lax.dot_general(left, right, (((left_dim,), (right_dim,)), ((), ())), pre...  7.37 us
    pallas_call x1, Pallas kernels, attention_forward(): pl.pallas_call(forward_kernel, grid=(rows // tile,), in_specs=[pl.BlockSp...  6.12 us
  transfers between devices with their start and end apart: 51, of which 24 were waited for; matrix products, arithmetic and copies ran while one was open for 14% of the time, Pallas kernels for 13%

profile of v1, /device:TPU:0, one launch (start us, length us, event | category | flops | bytes accessed | tf_op | source)
XLA Modules:
  0.0 260.5 jit_solution(6177133476455992581)
XLA Ops:
  3.3 5.1 %collective-permute-start.12 = (bf16[128,768]{1,0:T(8,128)(2,1)}, bf16[128,768]{1,0:T(8,128)(2,1)}, u32[]{:S(2)}, u32[]{:S(2)}) collective-permute-start(bf16[128,768]{1,0:T(8,128)(2,1)} %bitcast.2.x_ref), channel_id=1, source_target_pairs={{0,6},{1,7},{2,0},{3,1},{4,2},{5,3},{6,4},{7,5},{8,14},{9,15},{10,... | collective-permute-start | bytes 589832 | tf_op jit(solution)/shard_map/ppermute | solution.py:680
  11.4 2.9 %collective-permute-start.2 = (bf16[24,1408]{1,0:T(8,128)(2,1)}, bf16[24,1408]{1,0:T(8,128)(2,1)S(1)}, u32[]{:S(2)}, u32[]{:S(2)}) collective-permute-start(bf16[24,1408]{1,0:T(8,128)(2,1)} %get-tuple-element.104), channel_id=1, source_target_pairs={{0,6},{1,7},{2,0},{3,1},{4,2},{5,3},{6,4},{7,5},{8,14},{9,15},{10,... | collective-permute-start | bytes 202760 | tf_op jit(solution)/shard_map/ppermute | solution.py:680
  20.6 8.6 %collective-permute-start.4 = (bf16[1,96,768]{2,1,0:T(8,128)(2,1)S(1)}, bf16[1,96,768]{2,1,0:T(8,128)(2,1)S(1)}, u32[]{:S(2)}, u32[]{:S(2)}) collective-permute-start(bf16[1,96,768]{2,1,0:T(8,128)(2,1)S(1)} %bitcast.78), channel_id=1, source_target_pairs={{0,4},{1,5},{2,6},{3,7},{4,0},{5,1},{6,2},{7,3},{8,12},{9,13},{10,... | collective-permute-start | bytes 442376 | tf_op jit(solution)/shard_map/ppermute | solution.py:661
  30.4 3.9 %collective-permute-done.4 = bf16[1,96,768]{2,1,0:T(8,128)(2,1)S(1)} collective-permute-done((bf16[1,96,768]{2,1,0:T(8,128)(2,1)S(1)}, bf16[1,96,768]{2,1,0:T(8,128)(2,1)S(1)}, u32[]{:S(2)}, u32[]{:S(2)}) %collective-permute-start.4) | collective-permute-done | bytes 147488 | tf_op jit(solution)/shard_map/ppermute | solution.py:661
  37.8 3.1 %collective-permute-done.5 = bf16[96,1408]{1,0:T(8,128)(2,1)S(1)} collective-permute-done((bf16[96,1408]{1,0:T(8,128)(2,1)S(1)}, bf16[96,1408]{1,0:T(8,128)(2,1)S(1)}, u32[]{:S(2)}, u32[]{:S(2)}) %collective-permute-start.5) | collective-permute-done | bytes 270368 | tf_op jit(solution)/shard_map/ppermute | solution.py:661
  44.3 6.2 %collective-permute-done.8 = bf16[2,96,768]{2,1,0:T(8,128)(2,1)S(1)} collective-permute-done((bf16[2,96,768]{2,1,0:T(8,128)(2,1)S(1)}, bf16[2,96,768]{2,1,0:T(8,128)(2,1)S(1)}, u32[]{:S(2)}, u32[]{:S(2)}) %collective-permute-start.8) | collective-permute-done | bytes 294944 | tf_op jit(solution)/shard_map/ppermute | solution.py:661
  55.4 5.3 %collective-permute-done.13 = bf16[2,48,1536]{2,1,0:T(8,128)(2,1)S(1)} collective-permute-done((bf16[2,48,1536]{2,1,0:T(8,128)(2,1)S(1)}, bf16[2,48,1536]{2,1,0:T(8,128)(2,1)S(1)}, u32[]{:S(2)}, u32[]{:S(2)}) %collective-permute-start.13) | collective-permute-done | bytes 294944 | tf_op jit(solution)/shard_map/ppermute | solution.py:661
  62.8 3.2 %pad_maximum_fusion.table_ref = bf16[768,1408]{1,0:T(8,128)(2,1)} fusion(bf16[384,1408]{1,0:T(8,128)(2,1)} %collective-permute-done.9, bf16[384,1408]{1,0:T(8,128)(2,1)S(1)} %pad_maximum_fusion.3), kind=kLoop, calls=%fused_computation.12 | loop fusion | flops 4325376 | bytes 4325376 | tf_op jit(solution)/shard_map/concatenate | solution.py:666
  65.9 3.4 %collective-permute-done.10 = bf16[128,768]{1,0:T(8,128)(2,1)S(1)} collective-permute-done((bf16[128,768]{1,0:T(8,128)(2,1)}, bf16[128,768]{1,0:T(8,128)(2,1)S(1)}, u32[]{:S(2)}, u32[]{:S(2)}) %collective-permute-start.10) | collective-permute-done | bytes 196640 | tf_op jit(solution)/shard_map/ppermute | solution.py:680
  69.4 2.9 %fusion.5.x_ref = bf16[512,768]{1,0:T(8,128)(2,1)} fusion(s32[768]{0:T(1024)S(1)} %add.505, bf16[128,768]{1,0:T(8,128)(2,1)} %collective-permute-done.12, bf16[128,768]{1,0:T(8,128)(2,1)} %collective-permute-done.11, bf16[128,768]{1,0:T(8,128)(2,1)S(1)} %collective-permute-done.10, bf16[128,768]{1,0:T(8,128)(2,1)} %bitcast.2.x_ref), kind=kOutput, calls=%fused_computation.17 | convolution fusion | flops 608108544 | bytes 1575936 | tf_op jit(solution)/shard_map/dot_general | solution.py:44
  72.2 3.6 %project.1 = (bf16[512,192]{1,0:T(8,128)(2,1)}, bf16[512,384]{1,0:T(8,128)(2,1)}) custom-call(bf16[512,768]{1,0:T(8,128)(2,1)} %fusion.5.x_ref, bf16[768,1408]{1,0:T(8,128)(2,1)} %pad_maximum_fusion.table_ref, bf16[768,192]{1,0:T(8,128)(2,1)} %compare_convert_fusion.2.sel_ref), custom_call_target="tpu_custom_call" | custom-call | flops 100000000 | bytes 3244032 | tf_op jit(solution)/shard_map/project/pallas_call | solution.py:55
  81.5 6.2 %unfold_weights.1 = (bf16[768,576]{1,0:T(8,128)(2,1)}, bf16[768,768]{1,0:T(8,128)(2,1)}, f32[8,768]{1,0:T(8,128)}, f32[1,1536]{1,0:T(1,128)}) custom-call(bf16[768,1408]{1,0:T(8,128)(2,1)} %pad_maximum_fusion.table_ref, bf16[768,768]{1,0:T(8,128)(2,1)} %get-tuple-element.209.near_ref, bf16[768,768]{1,0:T(8,128)(2,1)} %get-tuple-element.208.line_ref, ...), custom_call_target="tpu_custom_call" | custom-call | flops 100000000 | bytes 6881280 | tf_op jit(solution)/shard_map/unfold_weights/pallas_call | solution.py:55
  93.8 3.2 %and_select_fusion.b_ref = f32[512,1024]{1,0:T(8,128)} fusion(s32[1024]{0:T(1024)S(1)} %bitcast.80, s32[1024]{0:T(1024)S(1)} %copy-done.24, s32[512]{0:T(512)S(1)} %copy-done.23, s32[512]{0:T(512)S(1)} %get-tuple-element.191, s32[512]{0:T(512)S(1)} %get-tuple-element.190, s32[512]{0:T(512)S(1)} %bitcast.82, s32[512]{0:T(512)S(1)} %bitcast.83, ...), kind=kLoop, calls=%fused_computation.14 | loop fusion | flops 8388608 | bytes 2121728 | tf_op jit(solution)/shard_map/jit(_where)/select_n | solution.py:826
  97.0 6.1 %attention_forward.1 = (bf16[128,192]{1,0:T(8,128)(2,1)}, bf16[128,192]{1,0:T(8,128)(2,1)}, bf16[128,192]{1,0:T(8,128)(2,1)}, bf16[128,192]{1,0:T(8,128)(2,1)}, f32[512,128]{1,0:T(8,128)}) custom-call(bf16[512,192]{1,0:T(8,128)(2,1)} %get-tuple-element.116.q_ref, bf16[1024,384]{1,0:T(8,128)(2,1)} %pad_maximum_fusion.4.kv_ref, f32[512,1024]{1,0:T(8,128)} %and_select_fusion.b_ref), custom_call_target="tpu_custom_call" | custom-call | flops 1610612736 | bytes 2097152 | tf_op jit(solution)/shard_map/attention_forward/pallas_call | solution.py:245
  107.6 4.7 %collective-permute-start.21 = (bf16[128,768]{1,0:T(8,128)(2,1)}, bf16[128,768]{1,0:T(8,128)(2,1)}, u32[]{:S(2)}, u32[]{:S(2)}) collective-permute-start(bf16[128,768]{1,0:T(8,128)(2,1)} %bitcast.2.x_ref), channel_id=1, source_target_pairs={{0,8},{1,9},{2,10},{3,11},{4,12},{5,13},{6,14},{7,15},{8,0},{9,1},... | collective-permute-start | bytes 589832 | tf_op jit(solution)/shard_map/ppermute | solution.py:661
  118.8 8.0 %ffn_forward.1 = (f32[256,768]{1,0:T(8,128)}, f32[256,768]{1,0:T(8,128)}, f32[256,128]{1,0:T(8,128)}, bf16[256,768]{1,0:T(8,128)(2,1)}, f32[256,1536]{1,0:T(8,12...) custom-call(s32[2]{0:T(128)} %pad_add_fusion.flag_ref, ...), custom_call_target="tpu_custom_call" | custom-call | flops 100000000 | bytes 7895048 | tf_op jit(solution)/shard_map/ffn_forward/pallas_call | solution.py:55
  129.7 7.8 %ffn_backward.1 = (bf16[128,768]{1,0:T(8,128)(2,1)}, f32[128,768]{1,0:T(8,128)}, bf16[128,768]{1,0:T(8,128)(2,1)}, bf16[256,768]{1,0:T(8,128)(2,1)}, bf16[256,15...) custom-call(s32[2]{0:T(128)} %pad_add_fusion.flag_ref, f32[256,768]{1,0:T(8,128)} %get-tuple-element.136.part_ref, ...), custom_call_target="tpu_custom_call" | custom-call | flops 100000000 | bytes 9854984 | tf_op jit(solution)/shard_map/ffn_backward/pallas_call | solution.py:55
  144.1 3.0 %branch_backward.1 = (f32[128,768]{1,0:T(8,128)}, bf16[128,768]{1,0:T(8,128)(2,1)}, f32[8,768]{1,0:T(8,128)}, bf16[128,192]{1,0:T(8,128)(2,1)}, bf16[128,192]{1,...) custom-call(f32[128,768]{1,0:T(8,128)} %get-tuple-element.141.keep_ref, bf16[128,768]{1,0:T(8,128)(2,1)} %copy-done.14, ...), custom_call_target="tpu_custom_call" | custom-call | flops 100000000 | bytes 2252800 | tf_op jit(solution)/shard_map/branch_backward/pallas_call | solution.py:55
  151.6 2.6 collective-permute-done.27.refs_1_
  156.6 9.1 %attention_backward.1 = (bf16[512,192]{1,0:T(8,128)(2,1)}, f32[512,384]{1,0:T(8,128)}, bf16[512,384]{1,0:T(8,128)(2,1)}) custom-call(bf16[512,192]{1,0:T(8,128)(2,1)} %get-tuple-element.116.q_ref, bf16[1024,384]{1,0:T(8,128)(2,1)} %pad_maximum_fusion.4.kv_ref, f32[512,1024]{1,0:T(8,128)} %and_select_fusion.b_ref, ...), custom_call_target="tpu_custom_call" | custom-call | flops 3019898880 | bytes 2097152 | tf_op jit(solution)/shard_map/attention_backward/pallas_call | solution.py:272
  170.8 7.3 %early_gradients.1 = (f32[384,1024]{1,0:T(8,128)}, bf16[384,1024]{1,0:T(8,128)(2,1)}, f32[512,768]{1,0:T(8,128)}) custom-call(bf16[512,768]{1,0:T(8,128)(2,1)} %fusion.5.x_ref, bf16[512,192]{1,0:T(8,128)(2,1)} %get-tuple-element.158.dq_ref, bf16[128,768]{1,0:T(8,128)(2,1)} %pad_maximum_fusion.7.att_ref, bf16[128,768]{1,0:T(8,128)(2,1)} %get-tuple-element.159.branch_ref, ...), custom_call_target="tpu_custom_call" | custom-call | flops 100000000 | bytes 7329792 | tf_op jit(solution)/shard_map/early_gradients/pallas_call | solution.py:55
  179.6 5.2 %collective-permute-done.34 = bf16[192,1536]{1,0:T(8,128)(2,1)S(1)} collective-permute-done((bf16[192,1536]{1,0:T(8,128)(2,1)S(1)}, bf16[192,1536]{1,0:T(8,128)(2,1)S(1)}, u32[]{:S(2)}, u32[]{:S(2)}) %collective-permute-start.34) | collective-permute-done | bytes 589856 | tf_op jit(solution)/shard_map/ppermute | solution.py:661
  186.0 4.3 %collective-permute-done.33.got_ref = bf16[512,384]{1,0:T(8,128)(2,1)S(1)} collective-permute-done((bf16[512,384]{1,0:T(8,128)(2,1)}, bf16[512,384]{1,0:T(8,128)(2,1)S(1)}, u32[]{:S(2)}, u32[]{:S(2)}) %collective-permute-start.33) | collective-permute-done | bytes 393248 | tf_op jit(solution)/shard_map/ppermute | solution.py:661
  191.1 6.2 %late_gradients.1 = (f32[384,1408]{1,0:T(8,128)}, bf16[384,1408]{1,0:T(8,128)(2,1)}, f32[128,768]{1,0:T(8,128)}, bf16[128,768]{1,0:T(8,128)(2,1)}, bf16[128,768]{1,0:T(8,128)(2,1)}, /*index=5*/bf16[128,768]{1,0:T(8,128)(2,1)}) custom-call(bf16[512,768]{1,0:T(8,128)(2,1)} %fusion.5.x_ref, f32[512,384]{1,0:T(8,128)} %get-tuple-element.165.own_ref, ...), custom_call_target="tpu_custom_call" | custom-call | flops 100000000 | bytes 7077888 | tf_op jit(solution)/shard_map/late_gradients/pallas_call | solution.py:55
  198.5 2.5 collective-permute-done.35
  208.5 3.5 %collective-permute-start.40 = (bf16[48,1536]{1,0:T(8,128)(2,1)S(1)}, bf16[48,1536]{1,0:T(8,128)(2,1)S(1)}, u32[]{:S(2)}, u32[]{:S(2)}) collective-permute-start(bf16[48,1536]{1,0:T(8,128)(2,1)S(1)} %get-tuple-element.196), channel_id=1, source_target_pairs={{0,6},{1,7},{2,0},{3,1},{4,2},{5,3},{6,4},{7,5},{8,14},{9,15},{10,... | collective-permute-start | bytes 442376 | tf_op jit(solution)/shard_map/ppermute | solution.py:680
  216.8 2.8 %collective-permute-start.50 = (bf16[96,768]{1,0:T(8,128)(2,1)S(1)}, bf16[96,768]{1,0:T(8,128)(2,1)S(1)}, u32[]{:S(2)}, u32[]{:S(2)}) collective-permute-start(bf16[96,768]{1,0:T(8,128)(2,1)S(1)} %get-tuple-element.193), channel_id=1, source_target_pairs={{0,6},{1,7},{2,0},{3,1},{4,2},{5,3},{6,4},{7,5},{8,14},{9,15},{10,... | collective-permute-start | bytes 442376 | tf_op jit(solution)/shard_map/ppermute | solution.py:680
  219.6 4.4 %collective-permute-start.49 = (bf16[96,768]{1,0:T(8,128)(2,1)S(1)}, bf16[96,768]{1,0:T(8,128)(2,1)S(1)}, u32[]{:S(2)}, u32[]{:S(2)}) collective-permute-start(bf16[96,768]{1,0:T(8,128)(2,1)S(1)} %get-tuple-element.194), channel_id=1, source_target_pairs={{0,4},{1,5},{2,6},{3,7},{4,0},{5,1},{6,2},{7,3},{8,12},{9,13},{10,... | collective-permute-start | bytes 442376 | tf_op jit(solution)/shard_map/ppermute | solution.py:680
  224.1 7.9 %collective-permute-done.39 = bf16[48,1536]{1,0:T(8,128)(2,1)S(1)} collective-permute-done((bf16[48,1536]{1,0:T(8,128)(2,1)S(1)}, bf16[48,1536]{1,0:T(8,128)(2,1)S(1)}, u32[]{:S(2)}, u32[]{:S(2)}) %collective-permute-start.39) | collective-permute-done | bytes 147488 | tf_op jit(solution)/shard_map/ppermute | solution.py:680
  233.7 2.6 collective-permute-start.42
  236.3 10.9 %collective-permute-done.49 = bf16[96,768]{1,0:T(8,128)(2,1)S(1)} collective-permute-done((bf16[96,768]{1,0:T(8,128)(2,1)S(1)}, bf16[96,768]{1,0:T(8,128)(2,1)S(1)}, u32[]{:S(2)}, u32[]{:S(2)}) %collective-permute-start.49) | collective-permute-done | bytes 147488 | tf_op jit(solution)/shard_map/ppermute | solution.py:680
  248.9 3.7 %collective-permute-start.44 = (bf16[24,1408]{1,0:T(8,128)(2,1)S(1)}, bf16[24,1408]{1,0:T(8,128)(2,1)S(1)}, u32[]{:S(2)}, u32[]{:S(2)}) collective-permute-start(bf16[24,1408]{1,0:T(8,128)(2,1)S(1)} %get-tuple-element.202), channel_id=1, source_target_pairs={{0,6},{1,7},{2,0},{3,1},{4,2},{5,3},{6,4},{7,5},{8,14},{9,15},{10,... | collective-permute-start | bytes 202760 | tf_op jit(solution)/shard_map/ppermute | solution.py:680
  (255 shorter events, 99.1 us)
Async XLA Ops:
  3.3 62.6 %collective-permute-start.12 = (bf16[128,768]{1,0:T(8,128)(2,1)}, bf16[128,768]{1,0:T(8,128)(2,1)}, u32[]{:S(2)}, u32[]{:S(2)}) collective-permute-start(bf16[128,768]{1,0:T(8,128)(2,1)} %bitcast.2.x_ref), channel_id=1, source_target_pairs={{0,6},{1,7},{2,0},{3,1},{4,2},{5,3},{6,4},{7,5},{8,14},{9,15},{10,... | collective-permute-start | bytes 589832 | tf_op jit(solution)/shard_map/ppermute | solution.py:680
  8.4 57.5 %collective-permute-start.11 = (bf16[128,768]{1,0:T(8,128)(2,1)}, bf16[128,768]{1,0:T(8,128)(2,1)}, u32[]{:S(2)}, u32[]{:S(2)}) collective-permute-start(bf16[128,768]{1,0:T(8,128)(2,1)} %bitcast.2.x_ref), channel_id=1, source_target_pairs={{0,4},{1,5},{2,6},{3,7},{4,0},{5,1},{6,2},{7,3},{8,12},{9,13},{10,... | collective-permute-start | bytes 589832 | tf_op jit(solution)/shard_map/ppermute | solution.py:680
  8.4 12.1 %collective-permute-start = (bf16[24,1408]{1,0:T(8,128)(2,1)}, bf16[24,1408]{1,0:T(8,128)(2,1)S(1)}, u32[]{:S(2)}, u32[]{:S(2)}) collective-permute-start(bf16[24,1408]{1,0:T(8,128)(2,1)} %get-tuple-element.102), channel_id=1, source_target_pairs={{0,2},{1,3},{2,4},{3,5},{4,6},{5,7},{6,0},{7,1},{8,10},{9,11},{10,... | collective-permute-start | bytes 202760 | tf_op jit(solution)/shard_map/ppermute | solution.py:680
  9.4 19.7 %collective-permute-start.1 = (bf16[24,1408]{1,0:T(8,128)(2,1)}, bf16[24,1408]{1,0:T(8,128)(2,1)S(1)}, u32[]{:S(2)}, u32[]{:S(2)}) collective-permute-start(bf16[24,1408]{1,0:T(8,128)(2,1)} %get-tuple-element.103), channel_id=1, source_target_pairs={{0,4},{1,5},{2,6},{3,7},{4,0},{5,1},{6,2},{7,3},{8,12},{9,13},{10,... | collective-permute-start | bytes 202760 | tf_op jit(solution)/shard_map/ppermute | solution.py:680
  11.4 17.8 %collective-permute-start.2 = (bf16[24,1408]{1,0:T(8,128)(2,1)}, bf16[24,1408]{1,0:T(8,128)(2,1)S(1)}, u32[]{:S(2)}, u32[]{:S(2)}) collective-permute-start(bf16[24,1408]{1,0:T(8,128)(2,1)} %get-tuple-element.104), channel_id=1, source_target_pairs={{0,6},{1,7},{2,0},{3,1},{4,2},{5,3},{6,4},{7,5},{8,14},{9,15},{10,... | collective-permute-start | bytes 202760 | tf_op jit(solution)/shard_map/ppermute | solution.py:680
  20.6 13.8 %collective-permute-start.4 = (bf16[1,96,768]{2,1,0:T(8,128)(2,1)S(1)}, bf16[1,96,768]{2,1,0:T(8,128)(2,1)S(1)}, u32[]{:S(2)}, u32[]{:S(2)}) collective-permute-start(bf16[1,96,768]{2,1,0:T(8,128)(2,1)S(1)} %bitcast.78), channel_id=1, source_target_pairs={{0,4},{1,5},{2,6},{3,7},{4,0},{5,1},{6,2},{7,3},{8,12},{9,13},{10,... | collective-permute-start | bytes 442376 | tf_op jit(solution)/shard_map/ppermute | solution.py:661
  41.0 9.6 %collective-permute-start.6 = (bf16[192,1408]{1,0:T(8,128)(2,1)S(1)}, bf16[192,1408]{1,0:T(8,128)(2,1)S(1)}, u32[]{:S(2)}, u32[]{:S(2)}) collective-permute-start(bf16[192,1408]{1,0:T(8,128)(2,1)S(1)} %pad_maximum_fusion.5), channel_id=1, source_target_pairs={{0,1},{1,0},{2,3},{3,2},{4,5},{5,4},{6,7},{7,6},{8,24},{9,25},{10,... | collective-permute-start | bytes 1622024 | tf_op jit(solution)/shard_map/ppermute | solution.py:661
  50.7 12.1 %collective-permute-start.9 = (bf16[384,1408]{1,0:T(8,128)(2,1)S(1)}, bf16[384,1408]{1,0:T(8,128)(2,1)}, u32[]{:S(2)}, u32[]{:S(2)}) collective-permute-start(bf16[384,1408]{1,0:T(8,128)(2,1)S(1)} %pad_maximum_fusion.3), channel_id=1, source_target_pairs={{0,8},{1,9},{2,10},{3,11},{4,12},{5,13},{6,14},{7,15},{8,0},{9,1},... | collective-permute-start | bytes 3244040 | tf_op jit(solution)/shard_map/ppermute | solution.py:661
  51.3 9.4 %collective-permute-start.13 = (bf16[2,48,1536]{2,1,0:T(8,128)(2,1)S(1)}, bf16[2,48,1536]{2,1,0:T(8,128)(2,1)S(1)}, u32[]{:S(2)}, u32[]{:S(2)}) collective-permute-start(bf16[2,48,1536]{2,1,0:T(8,128)(2,1)S(1)} %maximum_select_fusion.3), channel_id=1, source_target_pairs={{0,2},{1,3},{2,0},{3,1},{4,6},{5,7},{6,4},{7,5},{8,10},{9,11},{10,... | collective-permute-start | bytes 884744 | tf_op jit(solution)/shard_map/ppermute | solution.py:661
  51.6 10.0 %collective-permute-start.14 = (bf16[384,768]{1,0:T(8,128)(2,1)S(1)}, bf16[384,768]{1,0:T(8,128)(2,1)}, u32[]{:S(2)}, u32[]{:S(2)}) collective-permute-start(bf16[384,768]{1,0:T(8,128)(2,1)S(1)} %bitcast.74), channel_id=1, source_target_pairs={{0,16},{1,17},{2,18},{3,19},{4,20},{5,21},{6,22},{7,23},{8,9},{9,8... | collective-permute-start | bytes 1769480 | tf_op jit(solution)/shard_map/ppermute | solution.py:661
  75.9 15.1 %collective-permute-start.16 = (bf16[192,1536]{1,0:T(8,128)(2,1)S(1)}, bf16[192,1536]{1,0:T(8,128)(2,1)}, u32[]{:S(2)}, u32[]{:S(2)}) collective-permute-start(bf16[192,1536]{1,0:T(8,128)(2,1)S(1)} %bitcast.72), channel_id=1, source_target_pairs={{0,16},{1,17},{2,18},{3,19},{4,20},{5,21},{6,22},{7,23},{8,9},{9,8... | collective-permute-start | bytes 1769480 | tf_op jit(solution)/shard_map/ppermute | solution.py:661
  77.7 12.3 %collective-permute-start.15 = (bf16[512,384]{1,0:T(8,128)(2,1)}, bf16[512,384]{1,0:T(8,128)(2,1)S(1)}, u32[]{:S(2)}, u32[]{:S(2)}) collective-permute-start(bf16[512,384]{1,0:T(8,128)(2,1)} %get-tuple-element.123), channel_id=1, source_target_pairs={{0,1},{1,0},{2,3},{3,2},{4,5},{5,4},{6,7},{7,6},{8,9},{9,8},{10,11... | collective-permute-start | bytes 1179656 | tf_op jit(solution)/shard_map/ppermute | solution.py:661
  80.9 36.9 %collective-permute-start.23 = (bf16[768,768]{1,0:T(8,128)(2,1)S(1)}, bf16[768,768]{1,0:T(8,128)(2,1)S(1)}, u32[]{:S(2)}, u32[]{:S(2)}) collective-permute-start(bf16[768,768]{1,0:T(8,128)(2,1)S(1)} %pad_maximum_fusion.1.down_near_hbm), channel_id=1, source_target_pairs={{0,1},{1,0},{2,3},{3,2},{4,5},{5,4},{6,7},{7,6},{8,24},{9,25},{10,... | collective-permute-start | bytes 3538952 | tf_op jit(solution)/shard_map/ppermute | solution.py:661
  92.2 25.6 %collective-permute-start.22 = (bf16[384,1536]{1,0:T(8,128)(2,1)S(1)}, bf16[384,1536]{1,0:T(8,128)(2,1)}, u32[]{:S(2)}, u32[]{:S(2)}) collective-permute-start(bf16[384,1536]{1,0:T(8,128)(2,1)S(1)} %pad_maximum_fusion.2.in_near_hbm), channel_id=1, source_target_pairs={{0,1},{1,0},{2,3},{3,2},{4,5},{5,4},{6,7},{7,6},{8,24},{9,25},{10,... | collective-permute-start | bytes 3538952 | tf_op jit(solution)/shard_map/ppermute | solution.py:661
  107.6 9.3 %collective-permute-start.21 = (bf16[128,768]{1,0:T(8,128)(2,1)}, bf16[128,768]{1,0:T(8,128)(2,1)}, u32[]{:S(2)}, u32[]{:S(2)}) collective-permute-start(bf16[128,768]{1,0:T(8,128)(2,1)} %bitcast.2.x_ref), channel_id=1, source_target_pairs={{0,8},{1,9},{2,10},{3,11},{4,12},{5,13},{6,14},{7,15},{8,0},{9,1},... | collective-permute-start | bytes 589832 | tf_op jit(solution)/shard_map/ppermute | solution.py:661
  139.3 26.4 %collective-permute-start.31 = (bf16[384,1536]{1,0:T(8,128)(2,1)S(1)}, bf16[384,1536]{1,0:T(8,128)(2,1)}, u32[]{:S(2)}, u32[]{:S(2)}) collective-permute-start(bf16[384,1536]{1,0:T(8,128)(2,1)S(1)} %convolution_convert_fusion), channel_id=1, source_target_pairs={{0,1},{1,0},{2,3},{3,2},{4,5},{5,4},{6,7},{7,6},{8,24},{9,25},{10,... | collective-permute-start | bytes 3538952 | tf_op jit(solution)/shard_map/ppermute | solution.py:661
  141.3 26.9 %collective-permute-start.30 = (bf16[768,768]{1,0:T(8,128)(2,1)S(1)}, bf16[768,768]{1,0:T(8,128)(2,1)S(1)}, u32[]{:S(2)}, u32[]{:S(2)}) collective-permute-start(bf16[768,768]{1,0:T(8,128)(2,1)S(1)} %convolution_convert_fusion.2), channel_id=1, source_target_pairs={{0,1},{1,0},{2,3},{3,2},{4,5},{5,4},{6,7},{7,6},{8,24},{9,25},{10,... | collective-permute-start | bytes 3538952 | tf_op jit(solution)/shard_map/ppermute | solution.py:661
  147.1 8.8 %collective-permute-start.28 = (bf16[128,192]{1,0:T(8,128)(2,1)}, bf16[128,192]{1,0:T(8,128)(2,1)S(1)}, u32[]{:S(2)}, u32[]{:S(2)}) collective-permute-start(bf16[128,192]{1,0:T(8,128)(2,1)} %get-tuple-element.147), channel_id=1, source_target_pairs={{0,4},{1,5},{2,6},{3,7},{4,0},{5,1},{6,2},{7,3},{8,12},{9,13},{10,... | collective-permute-start | bytes 147464 | tf_op jit(solution)/shard_map/ppermute | solution.py:680
  168.5 11.0 %collective-permute-start.32 = (bf16[384,768]{1,0:T(8,128)(2,1)S(1)}, bf16[384,768]{1,0:T(8,128)(2,1)S(1)}, u32[]{:S(2)}, u32[]{:S(2)}) collective-permute-start(bf16[384,768]{1,0:T(8,128)(2,1)S(1)} %slice.155), channel_id=1, source_target_pairs={{0,16},{1,17},{2,18},{3,19},{4,20},{5,21},{6,22},{7,23},{8,9},{9,8... | collective-permute-start | bytes 1769480 | tf_op jit(solution)/shard_map/ppermute | solution.py:661
  169.0 15.8 %collective-permute-start.34 = (bf16[192,1536]{1,0:T(8,128)(2,1)S(1)}, bf16[192,1536]{1,0:T(8,128)(2,1)S(1)}, u32[]{:S(2)}, u32[]{:S(2)}) collective-permute-start(bf16[192,1536]{1,0:T(8,128)(2,1)S(1)} %slice.154), channel_id=1, source_target_pairs={{0,16},{1,17},{2,18},{3,19},{4,20},{5,21},{6,22},{7,23},{8,9},{9,8... | collective-permute-start | bytes 1769480 | tf_op jit(solution)/shard_map/ppermute | solution.py:661
  178.1 12.3 %collective-permute-start.33 = (bf16[512,384]{1,0:T(8,128)(2,1)}, bf16[512,384]{1,0:T(8,128)(2,1)S(1)}, u32[]{:S(2)}, u32[]{:S(2)}) collective-permute-start(bf16[512,384]{1,0:T(8,128)(2,1)} %get-tuple-element.166), channel_id=1, source_target_pairs={{0,1},{1,0},{2,3},{3,2},{4,5},{5,4},{6,7},{7,6},{8,9},{9,8},{10,11... | collective-permute-start | bytes 1179656 | tf_op jit(solution)/shard_map/ppermute | solution.py:661
  203.8 9.7 %collective-permute-start.36 = (bf16[192,1408]{1,0:T(8,128)(2,1)}, bf16[192,1408]{1,0:T(8,128)(2,1)}, u32[]{:S(2)}, u32[]{:S(2)}) collective-permute-start(bf16[192,1408]{1,0:T(8,128)(2,1)} %slice.156), channel_id=1, source_target_pairs={{0,1},{1,0},{2,3},{3,2},{4,5},{5,4},{6,7},{7,6},{8,24},{9,25},{10,... | collective-permute-start | bytes 1622024 | tf_op jit(solution)/shard_map/ppermute | solution.py:661
  205.3 43.6 %collective-permute-start.41 = (bf16[128,768]{1,0:T(8,128)(2,1)S(1)}, bf16[128,768]{1,0:T(8,128)(2,1)S(1)}, u32[]{:S(2)}, u32[]{:S(2)}) collective-permute-start(bf16[128,768]{1,0:T(8,128)(2,1)S(1)} %copy-done.35), channel_id=1, source_target_pairs={{0,6},{1,7},{2,0},{3,1},{4,2},{5,3},{6,4},{7,5},{8,14},{9,15},{10,... | collective-permute-start | bytes 589832 | tf_op jit(solution)/shard_map/ppermute | solution.py:680
  208.1 8.7 %collective-permute-start.38 = (bf16[48,1536]{1,0:T(8,128)(2,1)S(1)}, bf16[48,1536]{1,0:T(8,128)(2,1)S(1)}, u32[]{:S(2)}, u32[]{:S(2)}) collective-permute-start(bf16[48,1536]{1,0:T(8,128)(2,1)S(1)} %get-tuple-element.195), channel_id=1, source_target_pairs={{0,2},{1,3},{2,4},{3,5},{4,6},{5,7},{6,0},{7,1},{8,10},{9,11},{10,... | collective-permute-start | bytes 442376 | tf_op jit(solution)/shard_map/ppermute | solution.py:680
  208.5 11.1 %collective-permute-start.40 = (bf16[48,1536]{1,0:T(8,128)(2,1)S(1)}, bf16[48,1536]{1,0:T(8,128)(2,1)S(1)}, u32[]{:S(2)}, u32[]{:S(2)}) collective-permute-start(bf16[48,1536]{1,0:T(8,128)(2,1)S(1)} %get-tuple-element.196), channel_id=1, source_target_pairs={{0,6},{1,7},{2,0},{3,1},{4,2},{5,3},{6,4},{7,5},{8,14},{9,15},{10,... | collective-permute-start | bytes 442376 | tf_op jit(solution)/shard_map/ppermute | solution.py:680
  212.0 20.0 %collective-permute-start.39 = (bf16[48,1536]{1,0:T(8,128)(2,1)S(1)}, bf16[48,1536]{1,0:T(8,128)(2,1)S(1)}, u32[]{:S(2)}, u32[]{:S(2)}) collective-permute-start(bf16[48,1536]{1,0:T(8,128)(2,1)S(1)} %get-tuple-element.197), channel_id=1, source_target_pairs={{0,4},{1,5},{2,6},{3,7},{4,0},{5,1},{6,2},{7,3},{8,12},{9,13},{10,... | collective-permute-start | bytes 442376 | tf_op jit(solution)/shard_map/ppermute | solution.py:680
  213.5 20.2 %collective-permute-start.48 = (bf16[96,768]{1,0:T(8,128)(2,1)S(1)}, bf16[96,768]{1,0:T(8,128)(2,1)S(1)}, u32[]{:S(2)}, u32[]{:S(2)}) collective-permute-start(bf16[96,768]{1,0:T(8,128)(2,1)S(1)} %get-tuple-element.192), channel_id=1, source_target_pairs={{0,2},{1,3},{2,4},{3,5},{4,6},{5,7},{6,0},{7,1},{8,10},{9,11},{10,... | collective-permute-start | bytes 442376 | tf_op jit(solution)/shard_map/ppermute | solution.py:680
  216.8 19.4 %collective-permute-start.50 = (bf16[96,768]{1,0:T(8,128)(2,1)S(1)}, bf16[96,768]{1,0:T(8,128)(2,1)S(1)}, u32[]{:S(2)}, u32[]{:S(2)}) collective-permute-start(bf16[96,768]{1,0:T(8,128)(2,1)S(1)} %get-tuple-element.193), channel_id=1, source_target_pairs={{0,6},{1,7},{2,0},{3,1},{4,2},{5,3},{6,4},{7,5},{8,14},{9,15},{10,... | collective-permute-start | bytes 442376 | tf_op jit(solution)/shard_map/ppermute | solution.py:680
  219.6 27.5 %collective-permute-start.49 = (bf16[96,768]{1,0:T(8,128)(2,1)S(1)}, bf16[96,768]{1,0:T(8,128)(2,1)S(1)}, u32[]{:S(2)}, u32[]{:S(2)}) collective-permute-start(bf16[96,768]{1,0:T(8,128)(2,1)S(1)} %get-tuple-element.194), channel_id=1, source_target_pairs={{0,4},{1,5},{2,6},{3,7},{4,0},{5,1},{6,2},{7,3},{8,12},{9,13},{10,... | collective-permute-start | bytes 442376 | tf_op jit(solution)/shard_map/ppermute | solution.py:680
  232.0 16.0 %collective-permute-start.37 = (bf16[96,1408]{1,0:T(8,128)(2,1)S(1)}, bf16[96,1408]{1,0:T(8,128)(2,1)S(1)}, u32[]{:S(2)}, u32[]{:S(2)}) collective-permute-start(bf16[96,1408]{1,0:T(8,128)(2,1)S(1)} %slice.157), channel_id=1, source_target_pairs={{0,16},{1,17},{2,18},{3,19},{4,20},{5,21},{6,22},{7,23},{8,9},{9,8... | collective-permute-start | bytes 811016 | tf_op jit(solution)/shard_map/ppermute | solution.py:661
  233.7 18.9 %collective-permute-start.42 = (bf16[128,768]{1,0:T(8,128)(2,1)S(1)}, bf16[128,768]{1,0:T(8,128)(2,1)S(1)}, u32[]{:S(2)}, u32[]{:S(2)}) collective-permute-start(bf16[128,768]{1,0:T(8,128)(2,1)S(1)} %copy-done.34), channel_id=1, source_target_pairs={{0,4},{1,5},{2,6},{3,7},{4,0},{5,1},{6,2},{7,3},{8,12},{9,13},{10,... | collective-permute-start | bytes 589832 | tf_op jit(solution)/shard_map/ppermute | solution.py:680
  236.3 16.3 %collective-permute-start.43 = (bf16[128,768]{1,0:T(8,128)(2,1)S(1)}, bf16[128,768]{1,0:T(8,128)(2,1)S(1)}, u32[]{:S(2)}, u32[]{:S(2)}) collective-permute-start(bf16[128,768]{1,0:T(8,128)(2,1)S(1)} %copy-done.33), channel_id=1, source_target_pairs={{0,2},{1,3},{2,4},{3,5},{4,6},{5,7},{6,0},{7,1},{8,10},{9,11},{10,... | collective-permute-start | bytes 589832 | tf_op jit(solution)/shard_map/ppermute | solution.py:680
  (64 other events, 433.0 us)

commit v2 on v1

--- a/solution.py
+++ b/solution.py
@@ -101,7 +101,24 @@
     return chosen
 
 
-def pack_kernel(unit_ids, place_ref, qkv_ref, out_ref, in_ref, vec_ref, ffn_ref, gain_ref, shift_ref, *outs):
+def crossed(number):
+    return (number % 2) * 2 + number // 2
+
+
+def pack_kernel(
+    unit_ids,
+    place_ref,
+    qkv_ref,
+    out_ref,
+    in_ref,
+    x_ref,
+    cot_ref,
+    vec_ref,
+    ffn_ref,
+    gain_ref,
+    shift_ref,
+    *outs,
+):
     core, group = place_ref[0], place_ref[1]
     rows, width = out_ref.shape
     columns = width // HEAD_GROUPS
@@ -114,41 +131,59 @@
     turned.append(spread_rows(ffn_ref[...].astype(f32), rows, ffn_ref.shape[1] // rows))
     small = jnp.concatenate(turned, axis=1).astype(bf16)
     for k in range(HEAD_GROUPS):
-        chosen = pick(by_group, (group + k) % HEAD_GROUPS)
+        chosen = pick(by_group, group ^ crossed(k))
         rest = outs[k].shape[1] - 3 * columns - width - small.shape[1]
-        outs[k][...] = jnp.concatenate(
-            [chosen, out_ref[...], small, jnp.zeros((rows, rest), bf16)], axis=1
+        outs[k][:, : 2 * columns] = chosen[:, : 2 * columns]
+        outs[k][:, 2 * columns : 2 * columns + width] = out_ref[...]
+        outs[k][:, 2 * columns + width :] = jnp.concatenate(
+            [chosen[:, 2 * columns :], small, jnp.zeros((rows, rest), bf16)], axis=1
         )
     each = ffn_ref.shape[1]
     units = [
         jnp.concatenate([in_ref[:, i * each : (i + 1) * each] for i in ids], axis=1) for ids in unit_ids
     ]
     outs[HEAD_GROUPS][...] = jnp.where(core == 0, units[0], units[1])
-    outs[HEAD_GROUPS + 1][...] = jnp.where(core == 0, units[1], units[0])
-
-
-def qkv_kernel(x_ref, table_ref, sel_ref, q_ref, pair_ref):
-    columns = sel_ref.shape[1]
-    width = x_ref.shape[1]
-    mixed = dot(x_ref[...], table_ref[:, : 3 * columns])
-    small = table_ref[:, 3 * columns + width : 3 * columns + width + 4]
-    biases = dot(small, sel_ref[...], 0, 0)
-    keys = mixed[:, :columns]
-    values = mixed[:, columns : 2 * columns] + biases[1:2]
-    pair_ref[...] = jnp.concatenate([keys, values], axis=1).astype(bf16)
-    q_ref[...] = ((mixed[:, 2 * columns :] + biases[0:1]) * HD ** (-0.5)).astype(bf16)
-
-
-def unfold_kernel(small_each, table_ref, near_ref, line_ref, unit_ref, qkv_ref, out_ref, par_ref, ffn_ref):
-    columns = qkv_ref.shape[1]
+    far = jnp.where(core == 0, units[1], units[0])
+    far_ref = outs[HEAD_GROUPS + 1]
+    tokens = x_ref.shape[0]
+    top = far_ref.shape[0] - 2 * tokens
+    blank = jnp.zeros((top - 2 * rows, width), bf16)
+    far_ref[:top] = jnp.concatenate([far[:, :width], far[:, width:], blank][: 3 if top > 2 * rows else 2])
+    far_ref[top : top + tokens] = x_ref[...]
+    far_ref[top + tokens :] = cot_ref[...]
+
+
+def unfold_kernel(
+    small_each, table_ref, far_ref, near_ref, line_ref, unit_ref, qkv_ref, out_ref, par_ref, ffn_ref
+):
+    columns = qkv_ref.shape[1] // 3
     width = out_ref.shape[1]
-    qkv_ref[...] = dot(near_ref[...], table_ref[:, :columns]).astype(bf16)
-    out_ref[...] = dot(line_ref[...], table_ref[:, columns : columns + width]).astype(bf16)
-    small = table_ref[:, columns + width : columns + width + 8 + small_each]
-    par_ref[...] = dot(small[:, :8], near_ref[...], 0, 1)
+    start, at = 2 * columns, 2 * columns + width
+    near = near_ref[...]
+    both = lambda i, j: jnp.concatenate([table_ref[:, i:j], far_ref[:, i:j]], axis=0)
+    rest = both(at, table_ref.shape[1])
+    qkv_ref[:, :start] = dot(near, both(0, start)).astype(bf16)
+    qkv_ref[:, start:] = dot(near, rest[:, :columns]).astype(bf16)
+    out_ref[...] = dot(line_ref[...], both(start, at)).astype(bf16)
+    small = rest[:, columns : columns + 8 + small_each]
+    par_ref[...] = dot(small[:, :8], near, 0, 1)
     by_slot = dot(small[:, 8:], unit_ref[...], 0, 0)
     slot = iota(by_slot.shape, 1) % small_each == iota(by_slot.shape, 0)
     ffn_ref[...] = jnp.sum(jnp.where(slot, by_slot, 0.0), axis=0, keepdims=True)
+
+
+def qkv_kernel(x_ref, table_ref, far_ref, sel_ref, q_ref, pair_ref):
+    columns = q_ref.shape[1]
+    width = x_ref.shape[1]
+    half = width // 2
+    start, at = 2 * columns, 2 * columns + width
+    pairs = dot(x_ref[:, :half], table_ref[:, :start]) + dot(x_ref[:, half:], far_ref[:, :start])
+    rest = jnp.concatenate([table_ref[:, at:], far_ref[:, at:]], axis=0)
+    biases = dot(rest[:, columns : columns + 8], sel_ref[...], 0, 0)
+    values = pairs[:, columns:] + biases[1:2]
+    pair_ref[...] = jnp.concatenate([pairs[:, :columns], values], axis=1).astype(bf16)
+    queries = dot(x_ref[...], rest[:, :columns]) + biases[0:1]
+    q_ref[...] = (queries * HD ** (-0.5)).astype(bf16)
 
 
 def head_mask(shape, head):
@@ -316,7 +351,7 @@
     att_ref,
     att_far_ref,
     x_ref,
-    x_far_ref,
+    far_ref,
     par_ref,
     ffn_ref,
     out_hbm,
@@ -354,7 +389,9 @@
     )
     flags = [flag_ref[i] for i in range(flag_count)]
     attended = jnp.concatenate([att_ref[...], att_far_ref[...]], axis=0)
-    tokens = jnp.concatenate([x_ref[...], x_far_ref[...]], axis=0).astype(f32)
+    rows = x_ref.shape[0]
+    top = far_ref.shape[0] - 2 * rows
+    tokens = jnp.concatenate([x_ref[...], far_ref[top : top + rows]], axis=0).astype(f32)
     waits[0].wait()
     branch = dot(attended, out_ref[...]) + par_ref[2:3]
     normed, inverse = normalize(tokens + branch)
@@ -395,7 +432,7 @@
     got_ref,
     first_ref,
     cot_ref,
-    cot_far_ref,
+    far_ref,
     hidden_ref,
     par_ref,
     mix_hbm,
@@ -433,7 +470,7 @@
     normed, inverse = normalize(first_ref[...] + part_ref[...] + other + par_ref[3:4])
     gain = par_ref[5:6]
     output_ref[...] = (normed[:rows] * gain + par_ref[7:8]).astype(bf16)
-    out_grad = jnp.concatenate([cot_ref[...], cot_far_ref[...]], axis=0).astype(f32)
+    out_grad = jnp.concatenate([cot_ref[...], far_ref[far_ref.shape[0] - rows :]], axis=0).astype(f32)
     d_two = norm_back(out_grad, normed, inverse, gain)
     d_second = d_two.astype(bf16)
     second_ref[...] = d_second
@@ -489,74 +526,89 @@
         piece[...] = d_attended[:, k * columns : (k + 1) * columns]
 
 
-def early_grads_kernel(
+def branch_grads_kernel(
     small_each,
-    x_ref,
-    dq_ref,
     att_ref,
     branch_ref,
     sums_ref,
     sums_two_ref,
     ffn_ref,
-    sel_ref,
     near_ref,
     line_ref,
     unit_ref,
+    keep_ref,
+    send_ref,
+    small_ref,
+):
+    attended = dot(att_ref[...], line_ref[...]).astype(bf16)
+    outs = dot(attended, branch_ref[...], 0, 0)
+    half = outs.shape[0] // 2
+    keep_ref[...] = outs[:half]
+    send_ref[...] = outs[half:].astype(bf16)
+    first, second = sums_ref[...], sums_two_ref[...]
+    blank = jnp.zeros((2, first.shape[1]), f32)
+    vectors = jnp.concatenate(
+        [blank, first[2:3], second[2:3], first[0:1], second[0:1], first[1:2], second[1:2]], axis=0
+    )
+    vectors = dot(near_ref[...], vectors.astype(bf16), 0, 1)
+    units = ffn_ref.shape[1]
+    slot = iota((8, units), 1) % small_each == iota((8, units), 0)
+    by_slot = jnp.where(slot, ffn_ref[...], 0.0).astype(bf16)
+    ffn = dot(unit_ref[...], by_slot, 1, 1)
+    small_ref[...] = jnp.concatenate([vectors, ffn], axis=1)
+
+
+def query_grads_kernel(x_ref, dq_ref, sel_ref, qkv_ref, grad_ref, bias_ref, back_ref):
+    columns = dq_ref.shape[1]
+    d_query = dq_ref[...]
+    back_ref[...] = dot(d_query, qkv_ref[:, 2 * columns :], 1, 1)
+    grad_ref[...] = dot(x_ref[...], d_query, 0, 0)
+    sums = jnp.concatenate([column_sum(d_query.astype(f32)), jnp.zeros((7, columns), f32)], axis=0)
+    bias_ref[...] = dot(sel_ref[...], sums.astype(bf16), 1, 1)
+
+
+def pair_grads_kernel(
+    x_ref,
+    own_ref,
+    got_ref,
+    sel_ref,
     qkv_ref,
+    out_ref,
+    out_send_ref,
+    small_ref,
+    query_ref,
+    bias_ref,
+    query_back_ref,
     keep_ref,
     send_ref,
     back_ref,
+    back_send_ref,
 ):
-    columns = dq_ref.shape[1]
-    d_query = dq_ref[...]
-    back_ref[...] = dot(d_query, qkv_ref[:, 2 * columns :], 1, 1)
-    queries = dot(x_ref[...], d_query, 0, 0)
-    attended = dot(att_ref[...], line_ref[...]).astype(bf16)
-    outs = dot(attended, branch_ref[...], 0, 0)
-    sums = jnp.concatenate([column_sum(d_query.astype(f32)), jnp.zeros((7, columns), f32)], axis=0)
-    biases = dot(sel_ref[...], sums.astype(bf16), 1, 1)[:, :2]
-    first, second = sums_ref[...], sums_two_ref[...]
-    vectors = jnp.concatenate(
-        [first[2:3], second[2:3], first[0:1], second[0:1], first[1:2], second[1:2], first[3:5]], axis=0
-    )
-    vectors = dot(near_ref[...], vectors.astype(bf16), 0, 1)[:, :6]
-    units = ffn_ref.shape[1]
-    slot = iota((8, units), 1) % small_each == iota((8, units), 0)
-    by_slot = jnp.where(slot, ffn_ref[...], 0.0).astype(bf16)
-    ffn = dot(unit_ref[...], by_slot, 1, 1)[:, :small_each]
-    total = [queries, outs, biases, vectors, ffn]
-    rest = keep_ref.shape[1] - sum(a.shape[1] for a in total)
-    total = jnp.concatenate([*total, jnp.zeros((queries.shape[0], rest), f32)], axis=1)
-    half = total.shape[0] // 2
-    keep_ref[...] = total[:half]
-    send_ref[...] = total[half:].astype(bf16)
-
-
-def late_grads_kernel(
-    x_ref, own_ref, got_ref, sel_ref, qkv_ref, early_ref, early_send_ref, early_back_ref, *outs
-):
-    keep_ref, send_ref, back_ref, *back_pieces = outs
     pair_columns = own_ref.shape[1]
     columns = pair_columns // 2
+    width = x_ref.shape[1]
     d_pairs = (own_ref[...] + got_ref[...].astype(f32)).astype(bf16)
-    grad_back = early_back_ref[...] + dot(d_pairs, qkv_ref[:, :pair_columns], 1, 1)
+    grad_back = query_back_ref[...] + dot(d_pairs, qkv_ref[:, :pair_columns], 1, 1)
     rows = back_ref.shape[0]
     back_ref[...] = grad_back[:rows]
-    for k, piece in enumerate(back_pieces):
-        piece[...] = grad_back[(k + 1) * rows : (k + 2) * rows].astype(bf16)
+    back_send_ref[...] = grad_back[rows:].astype(bf16)
     pairs = dot(x_ref[...], d_pairs, 0, 0)
     sums = [jnp.zeros((1, columns), f32), column_sum(d_pairs[:, columns:].astype(f32))]
     sums = jnp.concatenate([*sums, jnp.zeros((6, columns), f32)], axis=0)
-    bias = dot(sel_ref[...], sums.astype(bf16), 1, 1)[:, 1:2]
-    half = pairs.shape[0] // 2
-    width = x_ref.shape[1]
-    at = columns + width + 1
-    lane = iota(early_ref.shape, 1)
+    bias = dot(sel_ref[...], sums.astype(bf16), 1, 1)
+    small = small_ref[...]
+    vectors = small[:, :8] + bias + bias_ref[...]
+    at = pair_columns + width
+    rest = keep_ref.shape[1] - at - columns - 16
+    last = [query_ref[...], vectors, small[:, 8:], jnp.zeros((width, rest), f32)]
+    last = jnp.concatenate(last, axis=1)
+    half = width // 2
     keep_ref[:, :pair_columns] = pairs[:half]
-    keep_ref[:, pair_columns:] = early_ref[...] + jnp.where(lane == at, bias[:half], 0.0)
+    keep_ref[:, pair_columns:at] = out_ref[...]
+    keep_ref[:, at:] = last[:half]
     send_ref[:, :pair_columns] = pairs[half:].astype(bf16)
-    late = early_send_ref[...].astype(f32) + jnp.where(lane == at, bias[half:], 0.0)
-    send_ref[:, pair_columns:] = late.astype(bf16)
+    send_ref[:, pair_columns:at] = out_send_ref[...]
+    send_ref[:, at:] = last[half:].astype(bf16)
 
 
 def finish_kernel(small_each, place_ref, own_ref, *refs):
@@ -566,14 +618,17 @@
     rows, width = out_ref.shape
     columns = width // HEAD_GROUPS
     line = [own_ref[...]] + [piece[...].astype(f32) for piece in pieces]
+    at = 2 * columns + width
     for g in range(HEAD_GROUPS):
-        mine = pick([a[:, : 3 * columns] for a in line], (g - group) % HEAD_GROUPS)
-        for kind, at in enumerate((2, 0, 1)):
+        source = crossed(group ^ g)
+        pairs = pick([a[:, : 2 * columns] for a in line], source)
+        queries = pick([a[:, at : at + columns] for a in line], source)
+        for kind, mine in enumerate((queries, pairs[:, :columns], pairs[:, columns:])):
             start = kind * width + g * columns
-            qkv_ref[:, start : start + columns] = mine[:, at * columns : (at + 1) * columns]
-    rest = sum(a[:, 3 * columns :] for a in line[1:]) + line[0][:, 3 * columns :]
-    out_ref[...] = rest[:, :width]
-    small = rest[:, width : width + 8 + small_each]
+            qkv_ref[:, start : start + columns] = mine
+    out_ref[...] = sum(a[:, 2 * columns : at] for a in line)
+    rest = sum(a[:, at:] for a in line)
+    small = rest[:, columns : columns + 8 + small_each]
     same_row = (iota((rows, rows), 0) == iota((rows, rows), 1)).astype(f32)
     turned = exact(small[:, :8], same_row, 0, 0)
     vec_ref[...] = turned[:4]
@@ -632,11 +687,11 @@
             pairs.append((device, self.device(at)))
         return pairs
 
-    def shift(self, by):
+    def cross(self, by):
         pairs = []
         for device in range(self.count):
             at = self.place(device)
-            at["g"] = (at["g"] + by) % HEAD_GROUPS
+            at["g"] ^= by
             pairs.append((device, self.device(at)))
         return pairs
 
@@ -675,9 +730,9 @@
     return total
 
 
-def line_send(grid, pieces, sign):
+def line_swap(grid, pieces):
     return [
-        lax.ppermute(piece, BOTH, grid.shift(sign * (k + 1))) for k, piece in enumerate(pieces)
+        lax.ppermute(piece, BOTH, grid.cross(crossed(k + 1))) for k, piece in enumerate(pieces)
     ]
 
 
@@ -732,14 +787,17 @@
         ]
         unit_ids.append(np.array(ids))
 
-    *packets, own_units, far_units = call(
+    far_top = -(-2 * rows_each // 16) * 16
+    *packets, own_units, far_pack = call(
         functools.partial(pack_kernel, unit_ids),
         [((rows_each, table_width), bf16)] * groups
-        + [((rows_each, ff_half), bf16)] * 2,
+        + [((rows_each, ff_half), bf16), ((far_top + 2 * local_len, width), bf16)],
         place,
         w_qkv,
         w_out,
         w_in,
+        tokens,
+        cot,
         vec_bias,
         ffn_bias.reshape(1, ff_each),
         norm_gain,
@@ -747,11 +805,11 @@
         name="pack_weights",
         scratch=(),
     )
-    got_packets = line_send(grid, packets[1:], 1)
+    got_packets = line_swap(grid, packets[1:])
 
     plane_x = [coords["x"] ^ jnp.asarray(masks[c]["x"]) for c in range(2)]
     plane_q = [part ^ jnp.asarray(masks[c]["q"]) for c in range(2)]
-    line_groups = (group - jnp.arange(groups, dtype=jnp.int32)) % groups
+    line_groups = group ^ jnp.asarray(group_order, jnp.int32)
     row = jnp.arange(rows_each, dtype=jnp.int32)
     row_ids = jnp.arange(width, dtype=jnp.int32)
     by_core = lambda c, pair: jnp.where(c == 0, pair[0], pair[1])
@@ -765,9 +823,18 @@
             for c in (core, 1 - core)
         ]
     )
+    line_bits = same(grid.group_bits)
+    x_half = gather_near(grid, tokens, line_bits[:1])
+    got_pack = chip_swap(far_pack)
+    got_units = jnp.concatenate([got_pack[:rows_each], got_pack[rows_each : 2 * rows_each]], axis=1)
+    table = jnp.concatenate([packets[0], *got_packets], axis=0)
+    units = jnp.concatenate([own_units, got_units], axis=0)[None]
+    table, x_half, units, near_ids, line_groups, segments = tie(
+        table, x_half, units, near_ids, line_groups, segments
+    )
     near_rows = (near_ids[..., None] * rows_each + row).reshape(width)
     to_near = (row_ids[:, None] == near_rows[None, :]).astype(bf16)
-    line_rows = (row_ids + group * columns) % width
+    line_rows = jnp.repeat(line_groups, columns) * columns + row_ids % columns
     line_near = (line_rows[:, None] == near_rows[None, :]).astype(bf16)
     group_rows = group * columns + jnp.arange(columns, dtype=jnp.int32)
     near_group = (near_rows[:, None] == group_rows[None, :]).astype(bf16)
@@ -825,6 +892,8 @@
         near = near | (key_block == picked)
     mask_bias = jnp.where(near & (query_seg == key_seg), 0.0, masked_score).astype(f32)
 
+    steps = len(grid.plane_bits)
+
     def group_step(held, entry):
         axis, bit = grid.group_bits[entry]
         got = swap(grid, held, ((axis, bit), (axis, bit)))
@@ -836,34 +905,35 @@
             held = jnp.concatenate([held, swap(grid, held, pair)], axis=0)
         return held
 
-    got_units = chip_swap(far_units)
+    x_far_half = swap(grid, x_half, line_bits[1])
+    table = gather_near(grid, table, grid.plane_bits[: steps // 2])
     down = group_step(w_down[None], 0)
-    packet, sent_tokens = tie(packets[0], tokens)
-    got_tokens = line_send(grid, [sent_tokens] * (groups - 1), 1)
-    table = jnp.concatenate([packet, *got_packets], axis=0)
-    units = jnp.concatenate([own_units, got_units], axis=0)[None]
-    table, units, down = tie(table, units, down)
-    down, units = group_step(down, 1), group_step(units, 0)
-    table = gather_near(grid, table, grid.plane_bits)
-    table, units, down = tie(table, units, down)
+    table, down, x_far_half, to_near, near_group, mask_bias = tie(
+        table, down, x_far_half, to_near, near_group, mask_bias
+    )
+    x_near = dot(jnp.concatenate([x_half, x_far_half]), to_near).astype(bf16)
+    table = gather_near(grid, table, grid.plane_bits[steps // 2 :])
+    down = group_step(down, 1)
+    units = group_step(units, 0)
+    table, down, units, x_near, line_near, near_unit, to_piece = tie(
+        table, down, units, x_near, line_near, near_unit, to_piece
+    )
+    table_far = swap(grid, table, grid.core_bit[0])
+    down_near = plane_gather(down.reshape(-1, width))
     units = group_step(units, 1)
-    down_near = plane_gather(down.reshape(-1, width))
-    table = gather_near(grid, table, grid.core_bit)
-    table, *got_tokens = tie(table, *got_tokens)
-    x_line = jnp.concatenate([tokens, *got_tokens], axis=0)
-    x_near = dot(x_line, to_near).astype(bf16)
 
     query, own_pairs = call(
         qkv_kernel,
         [((line_len, columns), bf16), ((line_len, 2 * columns), bf16)],
         x_near,
         table,
+        table_far,
         near_group,
         name="project",
     )
-    own_pairs, units, down_near = tie(own_pairs, units, down_near)
+    own_pairs, units, down_near, table_far = tie(own_pairs, units, down_near, table_far)
+    in_near = plane_gather(units.reshape(-1, ff_half))
     down_far = swap(grid, down_near, grid.plane_bits[-1])
-    x_far, cot_far = chip_swap(tokens), chip_swap(cot)
     qkv_slice, out_line, params, ffn_row = call(
         functools.partial(unfold_kernel, small_each),
         [
@@ -873,23 +943,22 @@
             ((1, ff_half), f32),
         ],
         table,
+        table_far,
         to_near,
         line_near,
         near_unit,
         name="unfold_weights",
     )
     ffn_row = outer_swap(ffn_row)
-    kept_pairs, out_line, params, to_piece = tie(own_pairs, out_line, params, to_piece)
+    kept_pairs, out_line, params, qkv_slice = tie(own_pairs, out_line, params, qkv_slice)
     pairs = jnp.concatenate([kept_pairs, swap(grid, own_pairs, part_bits[0])], axis=0)
     pairs = gather_near(grid, pairs, part_bits[1:])
-
-    in_near = plane_gather(units.reshape(-1, ff_half))
     pairs, in_near = tie(pairs, in_near)
     in_far = swap(grid, in_near, grid.plane_bits[-1])
     in_near, in_far = outer_swap(in_near), outer_swap(in_far)
 
     att_pieces, logs = attention_forward(query, pairs, mask_bias)
-    got_att = line_send(grid, att_pieces[1:], -1)
+    got_att = line_swap(grid, att_pieces[1:])
     attended = jnp.concatenate([att_pieces[0], *got_att], axis=1)
     attended_far = chip_swap(attended)
 
@@ -912,7 +981,7 @@
         attended,
         attended_far,
         tokens,
-        x_far,
+        got_pack,
         params,
         ffn_row,
         out_line,
@@ -944,7 +1013,7 @@
         part_got,
         first,
         cot,
-        cot_far,
+        got_pack,
         hidden,
         params,
         to_piece,
@@ -958,6 +1027,7 @@
         + [pltpu.SemaphoreType.DMA((5,))],
     )
     first_got = chip_swap(first_send)
+    first_got, d_hidden, d_second = tie(first_got, d_hidden, d_second)
     down_send = dot(active[:, width:], d_second, 0, 0).astype(bf16)
     down_keep = dot(active[:, :width], d_second, 0, 0).astype(bf16)
     d_hidden, ffn_sums = outer_swap(d_hidden), outer_swap(ffn_sums)
@@ -975,7 +1045,7 @@
         out_line,
         name="branch_backward",
     )
-    got_d_att = line_send(grid, d_pieces[1:], 1)
+    got_d_att = line_swap(grid, d_pieces[1:])
 
     def far_sum(keep, send):
         return keep.astype(f32) + swap(grid, send, grid.plane_bits[-1]).astype(f32)
@@ -984,17 +1054,34 @@
     in_total = far_sum(in_keep, in_send)
 
     def line_sum(total):
-        total = total.reshape(groups, -1, total.shape[1])
-        piece = lambda k: lax.dynamic_index_in_dim(
-            total, group_slot((group + k) % groups), 0, keepdims=False
-        )
-        got = line_send(grid, [piece(k).astype(bf16) for k in range(1, groups)], 1)
-        return sum((g.astype(f32) for g in got), piece(0))
+        for axis, bit in reversed(grid.group_bits):
+            size = total.shape[0] // 2
+            upper = (group >> bit) & 1
+            keep = lax.dynamic_slice_in_dim(total, upper * size, size, 0)
+            send = lax.dynamic_slice_in_dim(total, (1 - upper) * size, size, 0)
+            got = swap(grid, send.astype(bf16), ((axis, bit), (axis, bit)))
+            total = keep + got.astype(f32)
+        return total
+
+    small_sums = call(
+        functools.partial(branch_grads_kernel, small_each),
+        [((width // 2, width), f32), ((width // 2, width), bf16), ((width, 16), f32)],
+        attended,
+        d_branch,
+        sums_one,
+        sums_two,
+        ffn_sums,
+        to_near,
+        line_near,
+        near_unit,
+        name="branch_gradients",
+    )
+    d_pieces[0], *small_sums = tie(d_pieces[0], *small_sums)
 
     d_query, pairs_own, pairs_send = attention_backward(
         query, pairs, mask_bias, [d_pieces[0], *got_d_att], logs
     )
-    pairs_own, pairs_send, down_total, in_total = tie(pairs_own, pairs_send, down_total, in_total)
+    pairs_own, down_total, in_total = tie(pairs_own, down_total, in_total)
     down_total = reduce_near(grid, down_total, grid.plane_bits[:-1])
     in_total = reduce_near(grid, in_total, grid.plane_bits[:-1])
     if parts == 2:
@@ -1003,51 +1090,37 @@
         pairs_all = jnp.concatenate([pairs_own, pairs_send.astype(f32)])
         pairs_own = reduce_near(grid, pairs_all, part_bits)
         pairs_got = jnp.zeros(pairs_own.shape, bf16)
-    early_width = table_width - 2 * columns
-    early, early_send, early_back = call(
-        functools.partial(early_grads_kernel, small_each),
-        [
-            ((width // 2, early_width), f32),
-            ((width // 2, early_width), bf16),
-            ((line_len, width), f32),
-        ],
+    query_grads = call(
+        query_grads_kernel,
+        [((width, columns), f32), ((width, 8), f32), ((line_len, width), f32)],
         x_near,
         d_query,
-        attended,
-        d_branch,
-        sums_one,
-        sums_two,
-        ffn_sums,
         near_group,
-        to_near,
-        line_near,
-        near_unit,
         qkv_slice,
-        name="early_gradients",
-    )
-    pairs_own, down_total, early = tie(pairs_own, down_total, early)
-    grad_keep, grad_send, back_own, *back_pieces = call(
-        late_grads_kernel,
+        name="query_gradients",
+    )
+    grad_keep, grad_send, back_keep, back_send = call(
+        pair_grads_kernel,
         [
             ((width // 2, table_width), f32),
             ((width // 2, table_width), bf16),
-            ((local_len, width), f32),
-        ]
-        + [((local_len, width), bf16)] * (groups - 1),
+            ((line_len // 2, width), f32),
+            ((line_len // 2, width), bf16),
+        ],
         x_near,
         pairs_own,
         pairs_got,
         near_group,
         qkv_slice,
-        early,
-        early_send,
-        early_back,
-        name="late_gradients",
-    )
-    grad_send, in_total = tie(grad_send, in_total)
+        *small_sums,
+        *query_grads,
+        name="pair_gradients",
+    )
+    grad_send, down_total, in_total = tie(grad_send, down_total, in_total)
     sum_down = line_sum(down_total)
     in_pairs = line_sum(in_total)
-    got_back = line_send(grid, back_pieces, -1)
+    back = back_keep + swap(grid, back_send, line_bits[1]).astype(f32)
+    back = reduce_near(grid, back, line_bits[:1])
     total = grad_keep + chip_swap(grad_send).astype(f32)
     total = reduce_near(grid, total, grid.plane_bits)
     total, in_pairs, d_one = tie(total, in_pairs, d_one)
@@ -1061,10 +1134,10 @@
         name="order_units",
     )
 
-    got_total = line_send(
-        grid, [total[k * rows_each : (k + 1) * rows_each].astype(bf16) for k in range(1, groups)], -1
-    )
-    input_grad = d_one + sum((g.astype(f32) for g in got_back), back_own)
+    got_total = line_swap(
+        grid, [total[k * rows_each : (k + 1) * rows_each].astype(bf16) for k in range(1, groups)]
+    )
+    input_grad = d_one + back
     sum_qkv, sum_out, sum_vec, sum_ffn, sum_gain, sum_shift = call(
         functools.partial(finish_kernel, small_each),
         [

time: 261 us -> 242 us (0.927)
  starting transfers between devices: 74.7 us -> 60 us
  other arithmetic: 30 us -> 20.8 us
  waiting for transfers between devices: 72 us -> 75.8 us
  Pallas kernels: 63.2 us -> 66.2 us
    ppermute x27 -> x33, waiting for transfers between devices: 40.2 us -> 62.7 us  [swap(): return lax.ppermute(held, BOTH, grid.flip(bits))]
    ppermute x24 -> x12, starting transfers between devices: 37.9 us -> 17.7 us  [line_swap(): lax.ppermute(piece, BOTH, grid.cross(crossed(k + 1)))]
    ppermute x24 -> x12, waiting for transfers between devices: 31.8 us -> 13.1 us  [line_swap(): lax.ppermute(piece, BOTH, grid.cross(crossed(k + 1)))]
    ppermute x27 -> x33, starting transfers between devices: 36.8 us -> 42.3 us  [swap(): return lax.ppermute(held, BOTH, grid.flip(bits))]
    concatenate x3, other arithmetic: 3.29 us -> 0.15 us  [gather_near(): held = jnp.concatenate([held, swap(grid, held, pair)], axis=0)]
    pallas_call x10 -> x11, Pallas kernels: 48 us -> 50.7 us  [call(): pl.pallas_call(body, in_specs=specs, out_specs=[pl.BlockSpec(memory_space...]
    unnamed x89 -> x69, local copies, waits for them, and re-layouts: 5.43 us -> 6.05 us
  transfers between devices with their start and end apart: 51 -> 45, of which waited for: 24 -> 21; matrix products, arithmetic and copies ran while one was open for 14% -> 12% of each run, Pallas kernels for 13% -> 19%
where the time goes in v2:
time: 242 us; the launch traced here: 241 us
  waiting for transfers between devices  75.8 us (31%)
  Pallas kernels  66.2 us (27%)
  starting transfers between devices  60 us (25%)
  other arithmetic  20.8 us (9%)
  local copies, waits for them, and re-layouts  11 us (5%)
  matrix products  6.19 us (3%)
    ppermute x33, waiting for transfers between devices, swap(): return lax.ppermute(held, BOTH, grid.flip(bits))  62.7 us
    pallas_call x11, Pallas kernels, call(): pl.pallas_call(body, in_specs=specs, out_specs=[pl.BlockSpec(memory_space...  50.7 us
    ppermute x33, starting transfers between devices, swap(): return lax.ppermute(held, BOTH, grid.flip(bits))  42.3 us
    ppermute x12, starting transfers between devices, line_swap(): lax.ppermute(piece, BOTH, grid.cross(crossed(k + 1)))  17.7 us
    ppermute x12, waiting for transfers between devices, line_swap(): lax.ppermute(piece, BOTH, grid.cross(crossed(k + 1)))  13.1 us
    pallas_call x1, Pallas kernels, attention_backward(): pl.pallas_call(backward_kernel, grid=(rows // tile,), in_specs=[pl.BlockS...  9.38 us
    dot_general x5, matrix products, dot(): lax.dot_general(left, right, (((left_dim,), (right_dim,)), ((), ())), pre...  6.19 us
    pallas_call x1, Pallas kernels, attention_forward(): pl.pallas_call(forward_kernel, grid=(rows // tile,), in_specs=[pl.BlockSp...  6.12 us
  transfers between devices with their start and end apart: 45, of which 21 were waited for; matrix products, arithmetic and copies ran while one was open for 12% of the time, Pallas kernels for 19%

profile of v2, /device:TPU:0, one launch (start us, length us, event | category | flops | bytes accessed | tf_op | source)
XLA Modules:
  0.0 241.4 jit_solution(4969873229349084276)
XLA Ops:
  0.6 4.1 %collective-permute-start.6 = (bf16[1,96,768]{2,1,0:T(8,128)(2,1)}, bf16[1,96,768]{2,1,0:T(8,128)(2,1)S(1)}, u32[]{:S(2)}, u32[]{:S(2)}) collective-permute-start(bf16[1,96,768]{2,1,0:T(8,128)(2,1)} %bitcast.53), channel_id=1, source_target_pairs={{0,4},{1,5},{2,6},{3,7},{4,0},{5,1},{6,2},{7,3},{8,12},{9,13},{10,... | collective-permute-start | bytes 442376 | tf_op jit(solution)/shard_map/ppermute | solution.py:716
  5.4 2.5 %pack_weights.1 = (bf16[24,1408]{1,0:T(8,128)(2,1)}, bf16[24,1408]{1,0:T(8,128)(2,1)}, bf16[24,1408]{1,0:T(8,128)(2,1)}, bf16[24,1408]{1,0:T(8,128)(2,1)}, bf16[...) custom-call(s32[2]{0:T(128)} %pad_add_fusion.2.place_ref, bf16[24,2304]{1,0:T(8,128)(2,1)} %qkv_ref.1, ...), custom_call_target="tpu_custom_call" | custom-call | flops 100000000 | bytes 688712 | tf_op jit(solution)/shard_map/pack_weights/pallas_call | solution.py:55
  7.9 2.9 %collective-permute-start = (bf16[24,1408]{1,0:T(8,128)(2,1)}, bf16[24,1408]{1,0:T(8,128)(2,1)S(1)}, u32[]{:S(2)}, u32[]{:S(2)}) collective-permute-start(bf16[24,1408]{1,0:T(8,128)(2,1)} %get-tuple-element.114), channel_id=1, source_target_pairs={{0,4},{1,5},{2,6},{3,7},{4,0},{5,1},{6,2},{7,3},{8,12},{9,13},{10,... | collective-permute-start | bytes 202760 | tf_op jit(solution)/shard_map/ppermute | solution.py:735
  18.8 6.6 %collective-permute-done = bf16[24,1408]{1,0:T(8,128)(2,1)S(1)} collective-permute-done((bf16[24,1408]{1,0:T(8,128)(2,1)}, bf16[24,1408]{1,0:T(8,128)(2,1)S(1)}, u32[]{:S(2)}, u32[]{:S(2)}) %collective-permute-start) | collective-permute-done | bytes 67616 | tf_op jit(solution)/shard_map/ppermute | solution.py:735
  36.3 3.2 %and_select_fusion.b_ref = f32[512,1024]{1,0:T(8,128)} fusion(s32[1024]{0:T(1024)S(1)} %bitcast.55, s32[1024]{0:T(1024)S(1)} %get-tuple-element.240, s32[512]{0:T(512)S(1)} %slice_bitcast_fusion, s32[512]{0:T(512)S(1)} %get-tuple-element.217, s32[512]{0:T(512)S(1)} %get-tuple-element.216, s32[512]{0:T(512)S(1)} %bitcast.57, s32[512]{0:T(512)S(1)} %bitcast.58, ...), kind=kLoop, calls=%fused_computation.12 | loop fusion | flops 8388608 | bytes 2121728 | tf_op jit(solution)/shard_map/jit(_where)/select_n | solution.py:893
  42.0 4.1 %collective-permute-done.7 = bf16[256,768]{1,0:T(8,128)(2,1)S(1)} collective-permute-done((bf16[256,768]{1,0:T(8,128)(2,1)S(1)}, bf16[256,768]{1,0:T(8,128)(2,1)S(1)}, u32[]{:S(2)}, u32[]{:S(2)}) %collective-permute-start.7) | collective-permute-done | bytes 393248 | tf_op jit(solution)/shard_map/ppermute | solution.py:716
  48.6 5.1 %collective-permute-done.9 = bf16[2,96,768]{2,1,0:T(8,128)(2,1)S(1)} collective-permute-done((bf16[2,96,768]{2,1,0:T(8,128)(2,1)S(1)}, bf16[2,96,768]{2,1,0:T(8,128)(2,1)S(1)}, u32[]{:S(2)}, u32[]{:S(2)}) %collective-permute-start.9) | collective-permute-done | bytes 294944 | tf_op jit(solution)/shard_map/ppermute | solution.py:716
  57.2 2.0 collective-permute-start.12
  59.2 6.3 %collective-permute-done.12 = bf16[2,48,1536]{2,1,0:T(8,128)(2,1)S(1)} collective-permute-done((bf16[2,48,1536]{2,1,0:T(8,128)(2,1)S(1)}, bf16[2,48,1536]{2,1,0:T(8,128)(2,1)S(1)}, u32[]{:S(2)}, u32[]{:S(2)}) %collective-permute-start.12) | collective-permute-done | bytes 294944 | tf_op jit(solution)/shard_map/ppermute | solution.py:716
  66.8 3.6 %project.1 = (bf16[512,192]{1,0:T(8,128)(2,1)}, bf16[512,384]{1,0:T(8,128)(2,1)}) custom-call(bf16[512,768]{1,0:T(8,128)(2,1)} %convolution_convert_fusion.4.x_ref, bf16[384,1408]{1,0:T(8,128)(2,1)} %copy-done.3, bf16[384,1408]{1,0:T(8,128)(2,1)} %copy-done.5, bf16[768,192]{1,0:T(8,128)(2,1)} %compare_convert_fusion.2.sel_ref), custom_call_target="tpu_custom_call" | custom-call | flops 100000000 | bytes 3244032 | tf_op jit(solution)/shard_map/project/pallas_call | solution.py:55
  73.0 6.2 %unfold_weights.1 = (bf16[768,576]{1,0:T(8,128)(2,1)}, bf16[768,768]{1,0:T(8,128)(2,1)}, f32[8,768]{1,0:T(8,128)}, f32[1,1536]{1,0:T(1,128)}) custom-call(bf16[384,1408]{1,0:T(8,128)(2,1)} %copy-done.3, bf16[384,1408]{1,0:T(8,128)(2,1)} %copy-done.5, bf16[768,768]{1,0:T(8,128)(2,1)} %copy-done.2, bf16[768,768]{1,0:T(8,128)(2,1)} %get-tuple-element.138.line_ref, ...), custom_call_target="tpu_custom_call" | custom-call | flops 100000000 | bytes 6881280 | tf_op jit(solution)/shard_map/unfold_weights/pallas_call | solution.py:55
  80.1 4.0 %collective-permute-done.14 = bf16[512,384]{1,0:T(8,128)(2,1)S(1)} collective-permute-done((bf16[512,384]{1,0:T(8,128)(2,1)}, bf16[512,384]{1,0:T(8,128)(2,1)S(1)}, u32[]{:S(2)}, u32[]{:S(2)}) %collective-permute-start.14) | collective-permute-done | bytes 393248 | tf_op jit(solution)/shard_map/ppermute | solution.py:716
  86.4 6.1 %attention_forward.1 = (bf16[128,192]{1,0:T(8,128)(2,1)}, bf16[128,192]{1,0:T(8,128)(2,1)}, bf16[128,192]{1,0:T(8,128)(2,1)}, bf16[128,192]{1,0:T(8,128)(2,1)}, f32[512,128]{1,0:T(8,128)}) custom-call(bf16[512,192]{1,0:T(8,128)(2,1)} %get-tuple-element.132.q_ref, bf16[1024,384]{1,0:T(8,128)(2,1)} %pad_maximum_fusion.3.kv_ref, f32[512,1024]{1,0:T(8,128)} %and_select_fusion.b_ref), custom_call_target="tpu_custom_call" | custom-call | flops 1610612736 | bytes 2097152 | tf_op jit(solution)/shard_map/attention_forward/pallas_call | solution.py:280
  92.5 2.3 collective-permute-start.16
  94.8 2.1 collective-permute-start.18
  102.8 6.1 %collective-permute-start.19 = (bf16[128,768]{1,0:T(8,128)(2,1)}, bf16[128,768]{1,0:T(8,128)(2,1)}, u32[]{:S(2)}, u32[]{:S(2)}) collective-permute-start(bf16[128,768]{1,0:T(8,128)(2,1)} %pad_maximum_fusion.7.att_ref), channel_id=1, source_target_pairs={{0,8},{1,9},{2,10},{3,11},{4,12},{5,13},{6,14},{7,15},{8,0},{9,1},... | collective-permute-start | bytes 589832 | tf_op jit(solution)/shard_map/ppermute | solution.py:716
  110.3 2.3 collective-permute-done.20.in_far_hbm
  112.6 7.9 %ffn_forward.1 = (f32[256,768]{1,0:T(8,128)}, f32[256,768]{1,0:T(8,128)}, f32[256,128]{1,0:T(8,128)}, bf16[256,768]{1,0:T(8,128)(2,1)}, f32[256,1536]{1,0:T(8,12...) custom-call(s32[2]{0:T(128)} %pad_add_fusion.1.flag_ref, ...), custom_call_target="tpu_custom_call" | custom-call | flops 100000000 | bytes 8165384 | tf_op jit(solution)/shard_map/ffn_forward/pallas_call | solution.py:55
  123.3 7.9 %ffn_backward.1 = (bf16[128,768]{1,0:T(8,128)(2,1)}, f32[128,768]{1,0:T(8,128)}, bf16[128,768]{1,0:T(8,128)(2,1)}, bf16[256,768]{1,0:T(8,128)(2,1)}, bf16[256,15...) custom-call(s32[2]{0:T(128)} %pad_add_fusion.1.flag_ref, f32[256,768]{1,0:T(8,128)} %get-tuple-element.157.part_ref, ...), custom_call_target="tpu_custom_call" | custom-call | flops 100000000 | bytes 10125320 | tf_op jit(solution)/shard_map/ffn_backward/pallas_call | solution.py:55
  138.7 3.0 %branch_backward.1 = (f32[128,768]{1,0:T(8,128)}, bf16[128,768]{1,0:T(8,128)(2,1)}, f32[8,768]{1,0:T(8,128)}, bf16[128,192]{1,0:T(8,128)(2,1)}, bf16[128,192]{1,...) custom-call(f32[128,768]{1,0:T(8,128)} %get-tuple-element.162.keep_ref, bf16[128,768]{1,0:T(8,128)(2,1)} %copy-done.18, ...), custom_call_target="tpu_custom_call" | custom-call | flops 100000000 | bytes 2252800 | tf_op jit(solution)/shard_map/branch_backward/pallas_call | solution.py:55
  141.7 2.4 %collective-permute-start.24 = (bf16[128,192]{1,0:T(8,128)(2,1)}, bf16[128,192]{1,0:T(8,128)(2,1)S(1)}, u32[]{:S(2)}, u32[]{:S(2)}) collective-permute-start(bf16[128,192]{1,0:T(8,128)(2,1)} %get-tuple-element.178), channel_id=1, source_target_pairs={{0,4},{1,5},{2,6},{3,7},{4,0},{5,1},{6,2},{7,3},{8,12},{9,13},{10,... | collective-permute-start | bytes 147464 | tf_op jit(solution)/shard_map/ppermute | solution.py:735
  146.6 5.2 %branch_gradients.1 = (f32[384,768]{1,0:T(8,128)}, bf16[384,768]{1,0:T(8,128)(2,1)}, f32[768,16]{1,0:T(8,128)}) custom-call(bf16[128,768]{1,0:T(8,128)(2,1)} %pad_maximum_fusion.7.att_ref, bf16[128,768]{1,0:T(8,128)(2,1)} %get-tuple-element.170.branch_ref, f32[8,768]{1,0:T(8,128)} %get-tuple-element.171.sums_ref, f32[8,768]{1,0:T(8,128)} %get-tuple-element.172.sums_two_ref, ...), custom_call_target="tpu_custom_call" | custom-call | flops 100000000 | bytes 5167104 | tf_op jit(solution)/shard_map/branch_gradients/pallas_call | solution.py:55
  152.5 9.4 %attention_backward.1 = (bf16[512,192]{1,0:T(8,128)(2,1)}, f32[512,384]{1,0:T(8,128)}, bf16[512,384]{1,0:T(8,128)(2,1)}) custom-call(bf16[512,192]{1,0:T(8,128)(2,1)} %get-tuple-element.132.q_ref, bf16[1024,384]{1,0:T(8,128)(2,1)} %pad_maximum_fusion.3.kv_ref, f32[512,1024]{1,0:T(8,128)} %and_select_fusion.b_ref, ...), custom_call_target="tpu_custom_call" | custom-call | flops 3019898880 | bytes 2097152 | tf_op jit(solution)/shard_map/attention_backward/pallas_call | solution.py:307
  168.3 4.0 %query_gradients.1 = (f32[768,192]{1,0:T(8,128)}, f32[768,8]{1,0:T(8,128)}, f32[512,768]{1,0:T(8,128)}) custom-call(bf16[512,768]{1,0:T(8,128)(2,1)} %convolution_convert_fusion.4.x_ref, bf16[512,192]{1,0:T(8,128)(2,1)} %get-tuple-element.193.dq_ref, bf16[768,192]{1,0:T(8,128)(2,1)} %compare_convert_fusion.2.sel_ref, bf16[768,576]{1,0:T(8,128)(2,1)} %get-tuple-element.189.qkv_ref), custom_call_target="tpu_custom_call" | custom-call | flops 100000000 | bytes 2162688 | tf_op jit(solution)/shard_map/query_gradients/pallas_call | solution.py:55
  172.3 5.6 %collective-permute-done.29.got_ref = bf16[512,384]{1,0:T(8,128)(2,1)S(1)} collective-permute-done((bf16[512,384]{1,0:T(8,128)(2,1)S(1)}, bf16[512,384]{1,0:T(8,128)(2,1)S(1)}, u32[]{:S(2)}, u32[]{:S(2)}) %collective-permute-start.29) | collective-permute-done | bytes 393248 | tf_op jit(solution)/shard_map/ppermute | solution.py:716
  178.6 6.7 %pair_gradients.1 = (f32[384,1408]{1,0:T(8,128)}, bf16[384,1408]{1,0:T(8,128)(2,1)}, f32[256,768]{1,0:T(8,128)}, bf16[256,768]{1,0:T(8,128)(2,1)}) custom-call(bf16[512,768]{1,0:T(8,128)(2,1)} %convolution_convert_fusion.4.x_ref, f32[512,384]{1,0:T(8,128)} %get-tuple-element.187.own_ref, bf16[512,384]{1,0:T(8,128)(2,1)} %copy-done.12, ...), custom_call_target="tpu_custom_call" | custom-call | flops 100000000 | bytes 7151616 | tf_op jit(solution)/shard_map/pair_gradients/pallas_call | solution.py:55
  187.2 2.6 %collective-permute-start.32 = (bf16[384,1408]{1,0:T(8,128)(2,1)}, bf16[384,1408]{1,0:T(8,128)(2,1)S(1)}, u32[]{:S(2)}, u32[]{:S(2)}) collective-permute-start(bf16[384,1408]{1,0:T(8,128)(2,1)} %get-tuple-element.201), channel_id=1, source_target_pairs={{0,8},{1,9},{2,10},{3,11},{4,12},{5,13},{6,14},{7,15},{8,0},{9,1},... | collective-permute-start | bytes 3244040 | tf_op jit(solution)/shard_map/ppermute | solution.py:716
  190.2 5.4 %collective-permute-done.37 = bf16[256,768]{1,0:T(8,128)(2,1)} collective-permute-done((bf16[256,768]{1,0:T(8,128)(2,1)}, bf16[256,768]{1,0:T(8,128)(2,1)}, u32[]{:S(2)}, u32[]{:S(2)}) %collective-permute-start.37) | collective-permute-done | bytes 393248 | tf_op jit(solution)/shard_map/ppermute | solution.py:716
  199.6 4.3 %collective-permute-done.43 = bf16[192,768]{1,0:T(8,128)(2,1)S(1)} collective-permute-done((bf16[192,768]{1,0:T(8,128)(2,1)S(1)}, bf16[192,768]{1,0:T(8,128)(2,1)S(1)}, u32[]{:S(2)}, u32[]{:S(2)}) %collective-permute-start.43) | collective-permute-done | bytes 294944 | tf_op jit(solution)/shard_map/ppermute | solution.py:716
  206.2 7.7 %collective-permute-done.35 = bf16[96,1536]{1,0:T(8,128)(2,1)S(1)} collective-permute-done((bf16[96,1536]{1,0:T(8,128)(2,1)S(1)}, bf16[96,1536]{1,0:T(8,128)(2,1)S(1)}, u32[]{:S(2)}, u32[]{:S(2)}) %collective-permute-start.35) | collective-permute-done | bytes 294944 | tf_op jit(solution)/shard_map/ppermute | solution.py:716
  214.9 10.3 %collective-permute-done.36 = bf16[48,1536]{1,0:T(8,128)(2,1)S(1)} collective-permute-done((bf16[48,1536]{1,0:T(8,128)(2,1)S(1)}, bf16[48,1536]{1,0:T(8,128)(2,1)S(1)}, u32[]{:S(2)}, u32[]{:S(2)}) %collective-permute-start.36) | collective-permute-done | bytes 147488 | tf_op jit(solution)/shard_map/ppermute | solution.py:716
  228.2 2.5 %collective-permute-start.39 = (bf16[24,1408]{1,0:T(8,128)(2,1)S(1)}, bf16[24,1408]{1,0:T(8,128)(2,1)S(1)}, u32[]{:S(2)}, u32[]{:S(2)}) collective-permute-start(bf16[24,1408]{1,0:T(8,128)(2,1)S(1)} %get-tuple-element.224), channel_id=1, source_target_pairs={{0,4},{1,5},{2,6},{3,7},{4,0},{5,1},{6,2},{7,3},{8,12},{9,13},{10,... | collective-permute-start | bytes 202760 | tf_op jit(solution)/shard_map/ppermute | solution.py:735
  (235 shorter events, 85.6 us)
Async XLA Ops:
  0.6 24.9 %collective-permute-start.6 = (bf16[1,96,768]{2,1,0:T(8,128)(2,1)}, bf16[1,96,768]{2,1,0:T(8,128)(2,1)S(1)}, u32[]{:S(2)}, u32[]{:S(2)}) collective-permute-start(bf16[1,96,768]{2,1,0:T(8,128)(2,1)} %bitcast.53), channel_id=1, source_target_pairs={{0,4},{1,5},{2,6},{3,7},{4,0},{5,1},{6,2},{7,3},{8,12},{9,13},{10,... | collective-permute-start | bytes 442376 | tf_op jit(solution)/shard_map/ppermute | solution.py:716
  4.7 20.9 %collective-permute-start.3 = (bf16[128,768]{1,0:T(8,128)(2,1)}, bf16[128,768]{1,0:T(8,128)(2,1)S(1)}, u32[]{:S(2)}, u32[]{:S(2)}) collective-permute-start(bf16[128,768]{1,0:T(8,128)(2,1)} %bitcast.47), channel_id=1, source_target_pairs={{0,4},{1,5},{2,6},{3,7},{4,0},{5,1},{6,2},{7,3},{8,12},{9,13},{10,... | collective-permute-start | bytes 589832 | tf_op jit(solution)/shard_map/ppermute | solution.py:716
  7.9 17.6 %collective-permute-start = (bf16[24,1408]{1,0:T(8,128)(2,1)}, bf16[24,1408]{1,0:T(8,128)(2,1)S(1)}, u32[]{:S(2)}, u32[]{:S(2)}) collective-permute-start(bf16[24,1408]{1,0:T(8,128)(2,1)} %get-tuple-element.114), channel_id=1, source_target_pairs={{0,4},{1,5},{2,6},{3,7},{4,0},{5,1},{6,2},{7,3},{8,12},{9,13},{10,... | collective-permute-start | bytes 202760 | tf_op jit(solution)/shard_map/ppermute | solution.py:735
  10.8 14.7 %collective-permute-start.1 = (bf16[24,1408]{1,0:T(8,128)(2,1)}, bf16[24,1408]{1,0:T(8,128)(2,1)S(1)}, u32[]{:S(2)}, u32[]{:S(2)}) collective-permute-start(bf16[24,1408]{1,0:T(8,128)(2,1)} %get-tuple-element.115), channel_id=1, source_target_pairs={{0,2},{1,3},{2,0},{3,1},{4,6},{5,7},{6,4},{7,5},{8,10},{9,11},{10,... | collective-permute-start | bytes 202760 | tf_op jit(solution)/shard_map/ppermute | solution.py:735
  12.4 13.1 %collective-permute-start.2 = (bf16[24,1408]{1,0:T(8,128)(2,1)}, bf16[24,1408]{1,0:T(8,128)(2,1)S(1)}, u32[]{:S(2)}, u32[]{:S(2)}) collective-permute-start(bf16[24,1408]{1,0:T(8,128)(2,1)} %get-tuple-element.116), channel_id=1, source_target_pairs={{0,6},{1,7},{2,4},{3,5},{4,2},{5,3},{6,0},{7,1},{8,14},{9,15},{10,... | collective-permute-start | bytes 202760 | tf_op jit(solution)/shard_map/ppermute | solution.py:735
  29.4 17.5 %collective-permute-start.10 = (bf16[1,48,1536]{2,1,0:T(8,128)(2,1)S(1)}, bf16[1,48,1536]{2,1,0:T(8,128)(2,1)S(1)}, u32[]{:S(2)}, u32[]{:S(2)}) collective-permute-start(bf16[1,48,1536]{2,1,0:T(8,128)(2,1)S(1)} %maximum_bitcast_fusion), channel_id=1, source_target_pairs={{0,4},{1,5},{2,6},{3,7},{4,0},{5,1},{6,2},{7,3},{8,12},{9,13},{10,... | collective-permute-start | bytes 442376 | tf_op jit(solution)/shard_map/ppermute | solution.py:716
  31.1 10.8 %collective-permute-start.5 = (bf16[96,1408]{1,0:T(8,128)(2,1)S(1)}, bf16[96,1408]{1,0:T(8,128)(2,1)S(1)}, u32[]{:S(2)}, u32[]{:S(2)}) collective-permute-start(bf16[96,1408]{1,0:T(8,128)(2,1)S(1)} %pad_maximum_fusion.6), channel_id=1, source_target_pairs={{0,16},{1,17},{2,18},{3,19},{4,20},{5,21},{6,22},{7,23},{8,9},{9,8... | collective-permute-start | bytes 811016 | tf_op jit(solution)/shard_map/ppermute | solution.py:716
  32.6 13.5 %collective-permute-start.7 = (bf16[256,768]{1,0:T(8,128)(2,1)S(1)}, bf16[256,768]{1,0:T(8,128)(2,1)S(1)}, u32[]{:S(2)}, u32[]{:S(2)}) collective-permute-start(bf16[256,768]{1,0:T(8,128)(2,1)S(1)} %pad_maximum_fusion.5), channel_id=1, source_target_pairs={{0,2},{1,3},{2,0},{3,1},{4,6},{5,7},{6,4},{7,5},{8,10},{9,11},{10,... | collective-permute-start | bytes 1179656 | tf_op jit(solution)/shard_map/ppermute | solution.py:716
  46.1 9.4 %collective-permute-start.8 = (bf16[192,1408]{1,0:T(8,128)(2,1)S(1)}, bf16[192,1408]{1,0:T(8,128)(2,1)S(1)}, u32[]{:S(2)}, u32[]{:S(2)}) collective-permute-start(bf16[192,1408]{1,0:T(8,128)(2,1)S(1)} %pad_maximum_fusion.4), channel_id=1, source_target_pairs={{0,1},{1,0},{2,3},{3,2},{4,5},{5,4},{6,7},{7,6},{8,24},{9,25},{10,... | collective-permute-start | bytes 1622024 | tf_op jit(solution)/shard_map/ppermute | solution.py:716
  55.5 10.3 %collective-permute-start.11 = (bf16[384,1408]{1,0:T(8,128)(2,1)S(1)}, bf16[384,1408]{1,0:T(8,128)(2,1)S(1)}, u32[]{:S(2)}, u32[]{:S(2)}) collective-permute-start(bf16[384,1408]{1,0:T(8,128)(2,1)S(1)} %pad_maximum_fusion.2.table_ref), channel_id=1, source_target_pairs={{0,8},{1,9},{2,10},{3,11},{4,12},{5,13},{6,14},{7,15},{8,0},{9,1},... | collective-permute-start | bytes 3244040 | tf_op jit(solution)/shard_map/ppermute | solution.py:716
  55.6 10.1 %collective-permute-start.13 = (bf16[384,768]{1,0:T(8,128)(2,1)S(1)}, bf16[384,768]{1,0:T(8,128)(2,1)S(1)}, u32[]{:S(2)}, u32[]{:S(2)}) collective-permute-start(bf16[384,768]{1,0:T(8,128)(2,1)S(1)} %bitcast.45), channel_id=1, source_target_pairs={{0,16},{1,17},{2,18},{3,19},{4,20},{5,21},{6,22},{7,23},{8,9},{9,8... | collective-permute-start | bytes 1769480 | tf_op jit(solution)/shard_map/ppermute | solution.py:716
  57.2 8.4 %collective-permute-start.12 = (bf16[2,48,1536]{2,1,0:T(8,128)(2,1)S(1)}, bf16[2,48,1536]{2,1,0:T(8,128)(2,1)S(1)}, u32[]{:S(2)}, u32[]{:S(2)}) collective-permute-start(bf16[2,48,1536]{2,1,0:T(8,128)(2,1)S(1)} %maximum_select_fusion.3), channel_id=1, source_target_pairs={{0,2},{1,3},{2,0},{3,1},{4,6},{5,7},{6,4},{7,5},{8,10},{9,11},{10,... | collective-permute-start | bytes 884744 | tf_op jit(solution)/shard_map/ppermute | solution.py:716
  70.4 14.7 %collective-permute-start.15 = (bf16[192,1536]{1,0:T(8,128)(2,1)S(1)}, bf16[192,1536]{1,0:T(8,128)(2,1)S(1)}, u32[]{:S(2)}, u32[]{:S(2)}) collective-permute-start(bf16[192,1536]{1,0:T(8,128)(2,1)S(1)} %bitcast.43), channel_id=1, source_target_pairs={{0,16},{1,17},{2,18},{3,19},{4,20},{5,21},{6,22},{7,23},{8,9},{9,8... | collective-permute-start | bytes 1769480 | tf_op jit(solution)/shard_map/ppermute | solution.py:716
  71.9 12.3 %collective-permute-start.14 = (bf16[512,384]{1,0:T(8,128)(2,1)}, bf16[512,384]{1,0:T(8,128)(2,1)S(1)}, u32[]{:S(2)}, u32[]{:S(2)}) collective-permute-start(bf16[512,384]{1,0:T(8,128)(2,1)} %get-tuple-element.143), channel_id=1, source_target_pairs={{0,1},{1,0},{2,3},{3,2},{4,5},{5,4},{6,7},{7,6},{8,9},{9,8},{10,11... | collective-permute-start | bytes 1179656 | tf_op jit(solution)/shard_map/ppermute | solution.py:716
  79.2 31.1 %collective-permute-start.21 = (bf16[768,768]{1,0:T(8,128)(2,1)S(1)}, bf16[768,768]{1,0:T(8,128)(2,1)S(1)}, u32[]{:S(2)}, u32[]{:S(2)}) collective-permute-start(bf16[768,768]{1,0:T(8,128)(2,1)S(1)} %pad_maximum_fusion.down_near_hbm), channel_id=1, source_target_pairs={{0,1},{1,0},{2,3},{3,2},{4,5},{5,4},{6,7},{7,6},{8,24},{9,25},{10,... | collective-permute-start | bytes 3538952 | tf_op jit(solution)/shard_map/ppermute | solution.py:716
  85.2 27.4 %collective-permute-start.20 = (bf16[384,1536]{1,0:T(8,128)(2,1)S(1)}, bf16[384,1536]{1,0:T(8,128)(2,1)}, u32[]{:S(2)}, u32[]{:S(2)}) collective-permute-start(bf16[384,1536]{1,0:T(8,128)(2,1)S(1)} %pad_maximum_fusion.1.in_near_hbm), channel_id=1, source_target_pairs={{0,1},{1,0},{2,3},{3,2},{4,5},{5,4},{6,7},{7,6},{8,24},{9,25},{10,... | collective-permute-start | bytes 3538952 | tf_op jit(solution)/shard_map/ppermute | solution.py:716
  134.6 27.3 %collective-permute-start.28 = (bf16[384,1536]{1,0:T(8,128)(2,1)S(1)}, bf16[384,1536]{1,0:T(8,128)(2,1)}, u32[]{:S(2)}, u32[]{:S(2)}) collective-permute-start(bf16[384,1536]{1,0:T(8,128)(2,1)S(1)} %convolution_convert_fusion), channel_id=1, source_target_pairs={{0,1},{1,0},{2,3},{3,2},{4,5},{5,4},{6,7},{7,6},{8,24},{9,25},{10,... | collective-permute-start | bytes 3538952 | tf_op jit(solution)/shard_map/ppermute | solution.py:716
  136.6 27.1 %collective-permute-start.27 = (bf16[768,768]{1,0:T(8,128)(2,1)S(1)}, bf16[768,768]{1,0:T(8,128)(2,1)S(1)}, u32[]{:S(2)}, u32[]{:S(2)}) collective-permute-start(bf16[768,768]{1,0:T(8,128)(2,1)S(1)} %convolution_convert_fusion.2), channel_id=1, source_target_pairs={{0,1},{1,0},{2,3},{3,2},{4,5},{5,4},{6,7},{7,6},{8,24},{9,25},{10,... | collective-permute-start | bytes 3538952 | tf_op jit(solution)/shard_map/ppermute | solution.py:716
  141.7 10.1 %collective-permute-start.24 = (bf16[128,192]{1,0:T(8,128)(2,1)}, bf16[128,192]{1,0:T(8,128)(2,1)S(1)}, u32[]{:S(2)}, u32[]{:S(2)}) collective-permute-start(bf16[128,192]{1,0:T(8,128)(2,1)} %get-tuple-element.178), channel_id=1, source_target_pairs={{0,4},{1,5},{2,6},{3,7},{4,0},{5,1},{6,2},{7,3},{8,12},{9,13},{10,... | collective-permute-start | bytes 147464 | tf_op jit(solution)/shard_map/ppermute | solution.py:735
  164.0 22.9 %collective-permute-start.31 = (bf16[192,1536]{1,0:T(8,128)(2,1)S(1)}, bf16[192,1536]{1,0:T(8,128)(2,1)S(1)}, u32[]{:S(2)}, u32[]{:S(2)}) collective-permute-start(bf16[192,1536]{1,0:T(8,128)(2,1)S(1)} %slice.181), channel_id=1, source_target_pairs={{0,16},{1,17},{2,18},{3,19},{4,20},{5,21},{6,22},{7,23},{8,9},{9,8... | collective-permute-start | bytes 1769480 | tf_op jit(solution)/shard_map/ppermute | solution.py:716
  165.8 12.1 %collective-permute-start.29 = (bf16[512,384]{1,0:T(8,128)(2,1)S(1)}, bf16[512,384]{1,0:T(8,128)(2,1)S(1)}, u32[]{:S(2)}, u32[]{:S(2)}) collective-permute-start(bf16[512,384]{1,0:T(8,128)(2,1)S(1)} %copy-done.27), channel_id=1, source_target_pairs={{0,1},{1,0},{2,3},{3,2},{4,5},{5,4},{6,7},{7,6},{8,9},{9,8},{10,11... | collective-permute-start | bytes 1179656 | tf_op jit(solution)/shard_map/ppermute | solution.py:716
  167.4 19.6 %collective-permute-start.30 = (bf16[384,768]{1,0:T(8,128)(2,1)S(1)}, bf16[384,768]{1,0:T(8,128)(2,1)S(1)}, u32[]{:S(2)}, u32[]{:S(2)}) collective-permute-start(bf16[384,768]{1,0:T(8,128)(2,1)S(1)} %slice.182), channel_id=1, source_target_pairs={{0,16},{1,17},{2,18},{3,19},{4,20},{5,21},{6,22},{7,23},{8,9},{9,8... | collective-permute-start | bytes 1769480 | tf_op jit(solution)/shard_map/ppermute | solution.py:716
  185.3 10.4 %collective-permute-start.37 = (bf16[256,768]{1,0:T(8,128)(2,1)}, bf16[256,768]{1,0:T(8,128)(2,1)}, u32[]{:S(2)}, u32[]{:S(2)}) collective-permute-start(bf16[256,768]{1,0:T(8,128)(2,1)} %get-tuple-element.206), channel_id=1, source_target_pairs={{0,2},{1,3},{2,0},{3,1},{4,6},{5,7},{6,4},{7,5},{8,10},{9,11},{10,... | collective-permute-start | bytes 1179656 | tf_op jit(solution)/shard_map/ppermute | solution.py:716
  187.2 16.9 %collective-permute-start.32 = (bf16[384,1408]{1,0:T(8,128)(2,1)}, bf16[384,1408]{1,0:T(8,128)(2,1)S(1)}, u32[]{:S(2)}, u32[]{:S(2)}) collective-permute-start(bf16[384,1408]{1,0:T(8,128)(2,1)} %get-tuple-element.201), channel_id=1, source_target_pairs={{0,8},{1,9},{2,10},{3,11},{4,12},{5,13},{6,14},{7,15},{8,0},{9,1},... | collective-permute-start | bytes 3244040 | tf_op jit(solution)/shard_map/ppermute | solution.py:716
  189.9 14.0 %collective-permute-start.43 = (bf16[192,768]{1,0:T(8,128)(2,1)S(1)}, bf16[192,768]{1,0:T(8,128)(2,1)S(1)}, u32[]{:S(2)}, u32[]{:S(2)}) collective-permute-start(bf16[192,768]{1,0:T(8,128)(2,1)S(1)} %dynamic-slice_convert_fusion), channel_id=1, source_target_pairs={{0,2},{1,3},{2,0},{3,1},{4,6},{5,7},{6,4},{7,5},{8,10},{9,11},{10,... | collective-permute-start | bytes 884744 | tf_op jit(solution)/shard_map/ppermute | solution.py:716
  197.0 35.6 %collective-permute-start.38 = (bf16[128,768]{1,0:T(8,128)(2,1)S(1)}, bf16[128,768]{1,0:T(8,128)(2,1)S(1)}, u32[]{:S(2)}, u32[]{:S(2)}) collective-permute-start(bf16[128,768]{1,0:T(8,128)(2,1)S(1)} %slice.185), channel_id=1, source_target_pairs={{0,4},{1,5},{2,6},{3,7},{4,0},{5,1},{6,2},{7,3},{8,12},{9,13},{10,... | collective-permute-start | bytes 589832 | tf_op jit(solution)/shard_map/ppermute | solution.py:716
  199.0 15.0 %collective-permute-start.35 = (bf16[96,1536]{1,0:T(8,128)(2,1)S(1)}, bf16[96,1536]{1,0:T(8,128)(2,1)S(1)}, u32[]{:S(2)}, u32[]{:S(2)}) collective-permute-start(bf16[96,1536]{1,0:T(8,128)(2,1)S(1)} %dynamic-slice_convert_fusion.1), channel_id=1, source_target_pairs={{0,2},{1,3},{2,0},{3,1},{4,6},{5,7},{6,4},{7,5},{8,10},{9,11},{10,... | collective-permute-start | bytes 884744 | tf_op jit(solution)/shard_map/ppermute | solution.py:716
  203.9 21.4 %collective-permute-start.44 = (bf16[96,768]{1,0:T(8,128)(2,1)S(1)}, bf16[96,768]{1,0:T(8,128)(2,1)S(1)}, u32[]{:S(2)}, u32[]{:S(2)}) collective-permute-start(bf16[96,768]{1,0:T(8,128)(2,1)S(1)} %dynamic-slice_convert_fusion.2), channel_id=1, source_target_pairs={{0,4},{1,5},{2,6},{3,7},{4,0},{5,1},{6,2},{7,3},{8,12},{9,13},{10,... | collective-permute-start | bytes 442376 | tf_op jit(solution)/shard_map/ppermute | solution.py:716
  204.4 10.2 %collective-permute-start.33 = (bf16[192,1408]{1,0:T(8,128)(2,1)S(1)}, bf16[192,1408]{1,0:T(8,128)(2,1)S(1)}, u32[]{:S(2)}, u32[]{:S(2)}) collective-permute-start(bf16[192,1408]{1,0:T(8,128)(2,1)S(1)} %slice.183), channel_id=1, source_target_pairs={{0,1},{1,0},{2,3},{3,2},{4,5},{5,4},{6,7},{7,6},{8,24},{9,25},{10,... | collective-permute-start | bytes 1622024 | tf_op jit(solution)/shard_map/ppermute | solution.py:716
  214.1 11.2 %collective-permute-start.36 = (bf16[48,1536]{1,0:T(8,128)(2,1)S(1)}, bf16[48,1536]{1,0:T(8,128)(2,1)S(1)}, u32[]{:S(2)}, u32[]{:S(2)}) collective-permute-start(bf16[48,1536]{1,0:T(8,128)(2,1)S(1)} %dynamic-slice_convert_fusion.3), channel_id=1, source_target_pairs={{0,4},{1,5},{2,6},{3,7},{4,0},{5,1},{6,2},{7,3},{8,12},{9,13},{10,... | collective-permute-start | bytes 442376 | tf_op jit(solution)/shard_map/ppermute | solution.py:716
  214.7 11.4 %collective-permute-start.34 = (bf16[96,1408]{1,0:T(8,128)(2,1)S(1)}, bf16[96,1408]{1,0:T(8,128)(2,1)S(1)}, u32[]{:S(2)}, u32[]{:S(2)}) collective-permute-start(bf16[96,1408]{1,0:T(8,128)(2,1)S(1)} %slice.184), channel_id=1, source_target_pairs={{0,16},{1,17},{2,18},{3,19},{4,20},{5,21},{6,22},{7,23},{8,9},{9,8... | collective-permute-start | bytes 811016 | tf_op jit(solution)/shard_map/ppermute | solution.py:716
  228.2 8.1 %collective-permute-start.39 = (bf16[24,1408]{1,0:T(8,128)(2,1)S(1)}, bf16[24,1408]{1,0:T(8,128)(2,1)S(1)}, u32[]{:S(2)}, u32[]{:S(2)}) collective-permute-start(bf16[24,1408]{1,0:T(8,128)(2,1)S(1)} %get-tuple-element.224), channel_id=1, source_target_pairs={{0,4},{1,5},{2,6},{3,7},{4,0},{5,1},{6,2},{7,3},{8,12},{9,13},{10,... | collective-permute-start | bytes 202760 | tf_op jit(solution)/shard_map/ppermute | solution.py:735
  (47 other events, 278.7 us)

commit v3 on v2

--- a/solution.py
+++ b/solution.py
@@ -823,14 +823,25 @@
             for c in (core, 1 - core)
         ]
     )
+    def group_step(held, entry):
+        axis, bit = grid.group_bits[entry]
+        got = swap(grid, held, ((axis, bit), (axis, bit)))
+        upper = (group >> bit) & 1 == 1
+        return jnp.where(upper, jnp.concatenate([got, held]), jnp.concatenate([held, got]))
+
+    def plane_gather(held):
+        for pair in grid.plane_bits[:-1]:
+            held = jnp.concatenate([held, swap(grid, held, pair)], axis=0)
+        return held
+
     line_bits = same(grid.group_bits)
-    x_half = gather_near(grid, tokens, line_bits[:1])
     got_pack = chip_swap(far_pack)
     got_units = jnp.concatenate([got_pack[:rows_each], got_pack[rows_each : 2 * rows_each]], axis=1)
     table = jnp.concatenate([packets[0], *got_packets], axis=0)
     units = jnp.concatenate([own_units, got_units], axis=0)[None]
-    table, x_half, units, near_ids, line_groups, segments = tie(
-        table, x_half, units, near_ids, line_groups, segments
+    down = group_step(w_down[None], 0)
+    table, units, down, sent_tokens, near_ids, line_groups, segments = tie(
+        table, units, down, tokens, near_ids, line_groups, segments
     )
     near_rows = (near_ids[..., None] * rows_each + row).reshape(width)
     to_near = (row_ids[:, None] == near_rows[None, :]).astype(bf16)
@@ -894,29 +905,16 @@
 
     steps = len(grid.plane_bits)
 
-    def group_step(held, entry):
-        axis, bit = grid.group_bits[entry]
-        got = swap(grid, held, ((axis, bit), (axis, bit)))
-        upper = (group >> bit) & 1 == 1
-        return jnp.where(upper, jnp.concatenate([got, held]), jnp.concatenate([held, got]))
-
-    def plane_gather(held):
-        for pair in grid.plane_bits[:-1]:
-            held = jnp.concatenate([held, swap(grid, held, pair)], axis=0)
-        return held
-
+    x_half = gather_near(grid, sent_tokens, line_bits[:1])
+    table = gather_near(grid, table, grid.plane_bits[: steps // 2])
+    down = group_step(down, 1)
+    table, x_half, down, units = tie(table, x_half, down, units)
     x_far_half = swap(grid, x_half, line_bits[1])
-    table = gather_near(grid, table, grid.plane_bits[: steps // 2])
-    down = group_step(w_down[None], 0)
-    table, down, x_far_half, to_near, near_group, mask_bias = tie(
-        table, down, x_far_half, to_near, near_group, mask_bias
-    )
+    table = gather_near(grid, table, grid.plane_bits[steps // 2 :])
+    units = group_step(units, 0)
     x_near = dot(jnp.concatenate([x_half, x_far_half]), to_near).astype(bf16)
-    table = gather_near(grid, table, grid.plane_bits[steps // 2 :])
-    down = group_step(down, 1)
-    units = group_step(units, 0)
-    table, down, units, x_near, line_near, near_unit, to_piece = tie(
-        table, down, units, x_near, line_near, near_unit, to_piece
+    table, units, down, x_near, mask_bias, to_near, near_group, line_near, near_unit, to_piece = tie(
+        table, units, down, x_near, mask_bias, to_near, near_group, line_near, near_unit, to_piece
     )
     table_far = swap(grid, table, grid.core_bit[0])
     down_near = plane_gather(down.reshape(-1, width))
@@ -931,7 +929,7 @@
         near_group,
         name="project",
     )
-    own_pairs, units, down_near, table_far = tie(own_pairs, units, down_near, table_far)
+    own_pairs, table_far = tie(own_pairs, table_far)
     in_near = plane_gather(units.reshape(-1, ff_half))
     down_far = swap(grid, down_near, grid.plane_bits[-1])
     qkv_slice, out_line, params, ffn_row = call(

time: 242 us -> 234 us (0.967)
  starting transfers between devices: 60 us -> 49 us
  waiting for transfers between devices: 75.8 us -> 78.8 us
    ppermute x33, starting transfers between devices: 42.3 us -> 31.4 us  [swap(): return lax.ppermute(held, BOTH, grid.flip(bits))]
    ppermute x33, waiting for transfers between devices: 62.7 us -> 70.1 us  [swap(): return lax.ppermute(held, BOTH, grid.flip(bits))]
    ppermute x12, waiting for transfers between devices: 13.1 us -> 8.67 us  [line_swap(): lax.ppermute(piece, BOTH, grid.cross(crossed(k + 1)))]
    unnamed x69 -> x63, local copies, waits for them, and re-layouts: 6.05 us -> 5.27 us
  transfers between devices with their start and end apart: 45 -> 45, of which waited for: 21 -> 20; matrix products, arithmetic and copies ran while one was open for 12% -> 13% of each run, Pallas kernels for 19% -> 21%
where the time goes in v3:
time: 234 us; the launch traced here: 233 us
  waiting for transfers between devices  78.8 us (34%)
  Pallas kernels  66.6 us (28%)
  starting transfers between devices  49 us (21%)
  other arithmetic  20.9 us (9%)
  local copies, waits for them, and re-layouts  10.3 us (4%)
  matrix products  6.24 us (3%)
    ppermute x33, waiting for transfers between devices, swap(): return lax.ppermute(held, BOTH, grid.flip(bits))  70.1 us
    pallas_call x11, Pallas kernels, call(): pl.pallas_call(body, in_specs=specs, out_specs=[pl.BlockSpec(memory_space...  51.1 us
    ppermute x33, starting transfers between devices, swap(): return lax.ppermute(held, BOTH, grid.flip(bits))  31.4 us
    ppermute x12, starting transfers between devices, line_swap(): lax.ppermute(piece, BOTH, grid.cross(crossed(k + 1)))  17.6 us
    pallas_call x1, Pallas kernels, attention_backward(): pl.pallas_call(backward_kernel, grid=(rows // tile,), in_specs=[pl.BlockS...  9.36 us
    ppermute x12, waiting for transfers between devices, line_swap(): lax.ppermute(piece, BOTH, grid.cross(crossed(k + 1)))  8.67 us
    dot_general x5, matrix products, dot(): lax.dot_general(left, right, (((left_dim,), (right_dim,)), ((), ())), pre...  6.24 us
    pallas_call x1, Pallas kernels, attention_forward(): pl.pallas_call(forward_kernel, grid=(rows // tile,), in_specs=[pl.BlockSp...  6.12 us
  transfers between devices with their start and end apart: 45, of which 20 were waited for; matrix products, arithmetic and copies ran while one was open for 13% of the time, Pallas kernels for 21%

profile of v3, /device:TPU:0, one launch (start us, length us, event | category | flops | bytes accessed | tf_op | source)
XLA Modules:
  0.0 233.2 jit_solution(13870343184127266786)
XLA Ops:
  0.7 4.1 %collective-permute-start.4 = (bf16[1,96,768]{2,1,0:T(8,128)(2,1)}, bf16[1,96,768]{2,1,0:T(8,128)(2,1)S(1)}, u32[]{:S(2)}, u32[]{:S(2)}) collective-permute-start(bf16[1,96,768]{2,1,0:T(8,128)(2,1)} %bitcast.52), channel_id=1, source_target_pairs={{0,4},{1,5},{2,6},{3,7},{4,0},{5,1},{6,2},{7,3},{8,12},{9,13},{10,... | collective-permute-start | bytes 442376 | tf_op jit(solution)/shard_map/ppermute | solution.py:716
  5.4 2.4 %pack_weights.1 = (bf16[24,1408]{1,0:T(8,128)(2,1)}, bf16[24,1408]{1,0:T(8,128)(2,1)}, bf16[24,1408]{1,0:T(8,128)(2,1)}, bf16[24,1408]{1,0:T(8,128)(2,1)}, bf16[...) custom-call(s32[2]{0:T(128)} %pad_add_fusion.2.place_ref, bf16[24,2304]{1,0:T(8,128)(2,1)} %qkv_ref.1, ...), custom_call_target="tpu_custom_call" | custom-call | flops 100000000 | bytes 688712 | tf_op jit(solution)/shard_map/pack_weights/pallas_call | solution.py:55
  9.8 2.5 %collective-permute-start.2 = (bf16[24,1408]{1,0:T(8,128)(2,1)}, bf16[24,1408]{1,0:T(8,128)(2,1)S(1)}, u32[]{:S(2)}, u32[]{:S(2)}) collective-permute-start(bf16[24,1408]{1,0:T(8,128)(2,1)} %get-tuple-element.116), channel_id=1, source_target_pairs={{0,6},{1,7},{2,4},{3,5},{4,2},{5,3},{6,0},{7,1},{8,14},{9,15},{10,... | collective-permute-start | bytes 202760 | tf_op jit(solution)/shard_map/ppermute | solution.py:735
  19.6 3.3 %collective-permute-start.6 = (bf16[128,768]{1,0:T(8,128)(2,1)S(1)}, bf16[128,768]{1,0:T(8,128)(2,1)S(1)}, u32[]{:S(2)}, u32[]{:S(2)}) collective-permute-start(bf16[128,768]{1,0:T(8,128)(2,1)S(1)} %bitcast.48), channel_id=1, source_target_pairs={{0,4},{1,5},{2,6},{3,7},{4,0},{5,1},{6,2},{7,3},{8,12},{9,13},{10,... | collective-permute-start | bytes 589832 | tf_op jit(solution)/shard_map/ppermute | solution.py:716
  27.0 3.2 %and_select_fusion.b_ref = f32[512,1024]{1,0:T(8,128)} fusion(s32[1024]{0:T(1024)S(1)} %bitcast.54, s32[1024]{0:T(1024)S(1)} %get-tuple-element.240, s32[512]{0:T(512)S(1)} %slice_bitcast_fusion, s32[512]{0:T(512)S(1)} %get-tuple-element.217, s32[512]{0:T(512)S(1)} %get-tuple-element.216, s32[512]{0:T(512)S(1)} %bitcast.56, s32[512]{0:T(512)S(1)} %bitcast.57, ...), kind=kLoop, calls=%fused_computation.13 | loop fusion | flops 8388608 | bytes 2121728 | tf_op jit(solution)/shard_map/jit(_where)/select_n | solution.py:904
  32.4 4.1 %collective-permute-done.7 = bf16[2,96,768]{2,1,0:T(8,128)(2,1)S(1)} collective-permute-done((bf16[2,96,768]{2,1,0:T(8,128)(2,1)S(1)}, bf16[2,96,768]{2,1,0:T(8,128)(2,1)S(1)}, u32[]{:S(2)}, u32[]{:S(2)}) %collective-permute-start.7) | collective-permute-done | bytes 294944 | tf_op jit(solution)/shard_map/ppermute | solution.py:716
  39.5 5.2 %collective-permute-done.9 = bf16[1,48,1536]{2,1,0:T(8,128)(2,1)S(1)} collective-permute-done((bf16[1,48,1536]{2,1,0:T(8,128)(2,1)S(1)}, bf16[1,48,1536]{2,1,0:T(8,128)(2,1)S(1)}, u32[]{:S(2)}, u32[]{:S(2)}) %collective-permute-start.9) | collective-permute-done | bytes 147488 | tf_op jit(solution)/shard_map/ppermute | solution.py:716
  44.7 5.0 %collective-permute-done.10 = bf16[256,768]{1,0:T(8,128)(2,1)S(1)} collective-permute-done((bf16[256,768]{1,0:T(8,128)(2,1)S(1)}, bf16[256,768]{1,0:T(8,128)(2,1)S(1)}, u32[]{:S(2)}, u32[]{:S(2)}) %collective-permute-start.10) | collective-permute-done | bytes 393248 | tf_op jit(solution)/shard_map/ppermute | solution.py:716
  52.0 2.4 %collective-permute-start.20 = (bf16[384,768]{1,0:T(8,128)(2,1)S(1)}, bf16[384,768]{1,0:T(8,128)(2,1)S(1)}, u32[]{:S(2)}, u32[]{:S(2)}) collective-permute-start(bf16[384,768]{1,0:T(8,128)(2,1)S(1)} %bitcast.42), channel_id=1, source_target_pairs={{0,16},{1,17},{2,18},{3,19},{4,20},{5,21},{6,22},{7,23},{8,9},{9,8... | collective-permute-start | bytes 1769480 | tf_op jit(solution)/shard_map/ppermute | solution.py:716
  54.4 6.7 %collective-permute-done.13 = bf16[2,48,1536]{2,1,0:T(8,128)(2,1)S(1)} collective-permute-done((bf16[2,48,1536]{2,1,0:T(8,128)(2,1)S(1)}, bf16[2,48,1536]{2,1,0:T(8,128)(2,1)S(1)}, u32[]{:S(2)}, u32[]{:S(2)}) %collective-permute-start.13) | collective-permute-done | bytes 294944 | tf_op jit(solution)/shard_map/ppermute | solution.py:716
  61.2 2.4 %collective-permute-start.14 = (bf16[192,1536]{1,0:T(8,128)(2,1)S(1)}, bf16[192,1536]{1,0:T(8,128)(2,1)S(1)}, u32[]{:S(2)}, u32[]{:S(2)}) collective-permute-start(bf16[192,1536]{1,0:T(8,128)(2,1)S(1)} %bitcast.44), channel_id=1, source_target_pairs={{0,16},{1,17},{2,18},{3,19},{4,20},{5,21},{6,22},{7,23},{8,9},{9,8... | collective-permute-start | bytes 1769480 | tf_op jit(solution)/shard_map/ppermute | solution.py:716
  64.6 3.6 %project.1 = (bf16[512,192]{1,0:T(8,128)(2,1)}, bf16[512,384]{1,0:T(8,128)(2,1)}) custom-call(bf16[512,768]{1,0:T(8,128)(2,1)} %fusion.5.x_ref, bf16[384,1408]{1,0:T(8,128)(2,1)} %copy-done.2, bf16[384,1408]{1,0:T(8,128)(2,1)} %copy-done.4, bf16[768,192]{1,0:T(8,128)(2,1)} %compare_convert_fusion.2.sel_ref), custom_call_target="tpu_custom_call" | custom-call | flops 100000000 | bytes 3244032 | tf_op jit(solution)/shard_map/project/pallas_call | solution.py:55
  72.6 6.6 %unfold_weights.1 = (bf16[768,576]{1,0:T(8,128)(2,1)}, bf16[768,768]{1,0:T(8,128)(2,1)}, f32[8,768]{1,0:T(8,128)}, f32[1,1536]{1,0:T(1,128)}) custom-call(bf16[384,1408]{1,0:T(8,128)(2,1)} %copy-done.2, bf16[384,1408]{1,0:T(8,128)(2,1)} %copy-done.4, bf16[768,768]{1,0:T(8,128)(2,1)} %get-tuple-element.137.near_ref, ...), custom_call_target="tpu_custom_call" | custom-call | flops 100000000 | bytes 6881280 | tf_op jit(solution)/shard_map/unfold_weights/pallas_call | solution.py:55
  80.2 6.1 %attention_forward.1 = (bf16[128,192]{1,0:T(8,128)(2,1)}, bf16[128,192]{1,0:T(8,128)(2,1)}, bf16[128,192]{1,0:T(8,128)(2,1)}, bf16[128,192]{1,0:T(8,128)(2,1)}, f32[512,128]{1,0:T(8,128)}) custom-call(bf16[512,192]{1,0:T(8,128)(2,1)} %get-tuple-element.133.q_ref, bf16[1024,384]{1,0:T(8,128)(2,1)} %pad_maximum_fusion.3.kv_ref, f32[512,1024]{1,0:T(8,128)} %and_select_fusion.b_ref), custom_call_target="tpu_custom_call" | custom-call | flops 1610612736 | bytes 2097152 | tf_op jit(solution)/shard_map/attention_forward/pallas_call | solution.py:280
  90.7 3.0 %collective-permute-done.15 = bf16[128,192]{1,0:T(8,128)(2,1)S(1)} collective-permute-done((bf16[128,192]{1,0:T(8,128)(2,1)}, bf16[128,192]{1,0:T(8,128)(2,1)S(1)}, u32[]{:S(2)}, u32[]{:S(2)}) %collective-permute-start.15) | collective-permute-done | bytes 49184 | tf_op jit(solution)/shard_map/ppermute | solution.py:735
  99.9 3.7 %collective-permute-done.19.in_far_hbm = bf16[384,1536]{1,0:T(8,128)(2,1)} collective-permute-done((bf16[384,1536]{1,0:T(8,128)(2,1)S(1)}, bf16[384,1536]{1,0:T(8,128)(2,1)}, u32[]{:S(2)}, u32[]{:S(2)}) %collective-permute-start.19) | collective-permute-done | bytes 1179680 | tf_op jit(solution)/shard_map/ppermute | solution.py:716
  103.7 7.9 %ffn_forward.1 = (f32[256,768]{1,0:T(8,128)}, f32[256,768]{1,0:T(8,128)}, f32[256,128]{1,0:T(8,128)}, bf16[256,768]{1,0:T(8,128)(2,1)}, f32[256,1536]{1,0:T(8,12...) custom-call(s32[2]{0:T(128)} %pad_add_fusion.1.flag_ref, ...), custom_call_target="tpu_custom_call" | custom-call | flops 100000000 | bytes 8165384 | tf_op jit(solution)/shard_map/ffn_forward/pallas_call | solution.py:55
  114.4 7.9 %ffn_backward.1 = (bf16[128,768]{1,0:T(8,128)(2,1)}, f32[128,768]{1,0:T(8,128)}, bf16[128,768]{1,0:T(8,128)(2,1)}, bf16[256,768]{1,0:T(8,128)(2,1)}, bf16[256,15...) custom-call(s32[2]{0:T(128)} %pad_add_fusion.1.flag_ref, f32[256,768]{1,0:T(8,128)} %get-tuple-element.157.part_ref, ...), custom_call_target="tpu_custom_call" | custom-call | flops 100000000 | bytes 10125320 | tf_op jit(solution)/shard_map/ffn_backward/pallas_call | solution.py:55
  129.8 3.0 %branch_backward.1 = (f32[128,768]{1,0:T(8,128)}, bf16[128,768]{1,0:T(8,128)(2,1)}, f32[8,768]{1,0:T(8,128)}, bf16[128,192]{1,0:T(8,128)(2,1)}, bf16[128,192]{1,...) custom-call(f32[128,768]{1,0:T(8,128)} %get-tuple-element.162.keep_ref, bf16[128,768]{1,0:T(8,128)(2,1)} %copy-done.17, ...), custom_call_target="tpu_custom_call" | custom-call | flops 100000000 | bytes 2252800 | tf_op jit(solution)/shard_map/branch_backward/pallas_call | solution.py:55
  134.9 2.3 collective-permute-start.26
  137.8 5.2 %branch_gradients.1 = (f32[384,768]{1,0:T(8,128)}, bf16[384,768]{1,0:T(8,128)(2,1)}, f32[768,16]{1,0:T(8,128)}) custom-call(bf16[128,768]{1,0:T(8,128)(2,1)} %pad_maximum_fusion.7.att_ref, bf16[128,768]{1,0:T(8,128)(2,1)} %get-tuple-element.170.branch_ref, f32[8,768]{1,0:T(8,128)} %get-tuple-element.171.sums_ref, f32[8,768]{1,0:T(8,128)} %get-tuple-element.172.sums_two_ref, ...), custom_call_target="tpu_custom_call" | custom-call | flops 100000000 | bytes 5167104 | tf_op jit(solution)/shard_map/branch_gradients/pallas_call | solution.py:55
  143.7 9.4 %attention_backward.1 = (bf16[512,192]{1,0:T(8,128)(2,1)}, f32[512,384]{1,0:T(8,128)}, bf16[512,384]{1,0:T(8,128)(2,1)}) custom-call(bf16[512,192]{1,0:T(8,128)(2,1)} %get-tuple-element.133.q_ref, bf16[1024,384]{1,0:T(8,128)(2,1)} %pad_maximum_fusion.3.kv_ref, f32[512,1024]{1,0:T(8,128)} %and_select_fusion.b_ref, ...), custom_call_target="tpu_custom_call" | custom-call | flops 3019898880 | bytes 2097152 | tf_op jit(solution)/shard_map/attention_backward/pallas_call | solution.py:307
  155.2 2.4 %collective-permute-start.31 = (bf16[192,1536]{1,0:T(8,128)(2,1)S(1)}, bf16[192,1536]{1,0:T(8,128)(2,1)S(1)}, u32[]{:S(2)}, u32[]{:S(2)}) collective-permute-start(bf16[192,1536]{1,0:T(8,128)(2,1)S(1)} %slice.181), channel_id=1, source_target_pairs={{0,16},{1,17},{2,18},{3,19},{4,20},{5,21},{6,22},{7,23},{8,9},{9,8... | collective-permute-start | bytes 1769480 | tf_op jit(solution)/shard_map/ppermute | solution.py:716
  158.6 4.0 %query_gradients.1 = (f32[768,192]{1,0:T(8,128)}, f32[768,8]{1,0:T(8,128)}, f32[512,768]{1,0:T(8,128)}) custom-call(bf16[512,768]{1,0:T(8,128)(2,1)} %fusion.5.x_ref, bf16[512,192]{1,0:T(8,128)(2,1)} %get-tuple-element.193.dq_ref, bf16[768,192]{1,0:T(8,128)(2,1)} %compare_convert_fusion.2.sel_ref, bf16[768,576]{1,0:T(8,128)(2,1)} %get-tuple-element.189.qkv_ref), custom_call_target="tpu_custom_call" | custom-call | flops 100000000 | bytes 2162688 | tf_op jit(solution)/shard_map/query_gradients/pallas_call | solution.py:55
  162.5 7.1 %collective-permute-done.29.got_ref = bf16[512,384]{1,0:T(8,128)(2,1)S(1)} collective-permute-done((bf16[512,384]{1,0:T(8,128)(2,1)S(1)}, bf16[512,384]{1,0:T(8,128)(2,1)S(1)}, u32[]{:S(2)}, u32[]{:S(2)}) %collective-permute-start.29) | collective-permute-done | bytes 393248 | tf_op jit(solution)/shard_map/ppermute | solution.py:716
  170.4 6.6 %pair_gradients.1 = (f32[384,1408]{1,0:T(8,128)}, bf16[384,1408]{1,0:T(8,128)(2,1)}, f32[256,768]{1,0:T(8,128)}, bf16[256,768]{1,0:T(8,128)(2,1)}) custom-call(bf16[512,768]{1,0:T(8,128)(2,1)} %fusion.5.x_ref, f32[512,384]{1,0:T(8,128)} %get-tuple-element.187.own_ref, bf16[512,384]{1,0:T(8,128)(2,1)} %copy-done.11, ...), custom_call_target="tpu_custom_call" | custom-call | flops 100000000 | bytes 7151616 | tf_op jit(solution)/shard_map/pair_gradients/pallas_call | solution.py:55
  177.3 2.5 %collective-permute-start.32 = (bf16[384,1408]{1,0:T(8,128)(2,1)}, bf16[384,1408]{1,0:T(8,128)(2,1)S(1)}, u32[]{:S(2)}, u32[]{:S(2)}) collective-permute-start(bf16[384,1408]{1,0:T(8,128)(2,1)} %get-tuple-element.201), channel_id=1, source_target_pairs={{0,8},{1,9},{2,10},{3,11},{4,12},{5,13},{6,14},{7,15},{8,0},{9,1},... | collective-permute-start | bytes 3244040 | tf_op jit(solution)/shard_map/ppermute | solution.py:716
  181.6 6.2 %collective-permute-done.37 = bf16[256,768]{1,0:T(8,128)(2,1)} collective-permute-done((bf16[256,768]{1,0:T(8,128)(2,1)}, bf16[256,768]{1,0:T(8,128)(2,1)}, u32[]{:S(2)}, u32[]{:S(2)}) %collective-permute-start.37) | collective-permute-done | bytes 393248 | tf_op jit(solution)/shard_map/ppermute | solution.py:716
  190.9 3.5 %collective-permute-done.43 = bf16[192,768]{1,0:T(8,128)(2,1)S(1)} collective-permute-done((bf16[192,768]{1,0:T(8,128)(2,1)S(1)}, bf16[192,768]{1,0:T(8,128)(2,1)S(1)}, u32[]{:S(2)}, u32[]{:S(2)}) %collective-permute-start.43) | collective-permute-done | bytes 294944 | tf_op jit(solution)/shard_map/ppermute | solution.py:716
  195.4 12.3 %collective-permute-done.35 = bf16[96,1536]{1,0:T(8,128)(2,1)S(1)} collective-permute-done((bf16[96,1536]{1,0:T(8,128)(2,1)S(1)}, bf16[96,1536]{1,0:T(8,128)(2,1)S(1)}, u32[]{:S(2)}, u32[]{:S(2)}) %collective-permute-start.35) | collective-permute-done | bytes 294944 | tf_op jit(solution)/shard_map/ppermute | solution.py:716
  208.1 9.5 %collective-permute-done.36 = bf16[48,1536]{1,0:T(8,128)(2,1)S(1)} collective-permute-done((bf16[48,1536]{1,0:T(8,128)(2,1)S(1)}, bf16[48,1536]{1,0:T(8,128)(2,1)S(1)}, u32[]{:S(2)}, u32[]{:S(2)}) %collective-permute-start.36) | collective-permute-done | bytes 147488 | tf_op jit(solution)/shard_map/ppermute | solution.py:716
  220.5 2.5 %collective-permute-start.39 = (bf16[24,1408]{1,0:T(8,128)(2,1)S(1)}, bf16[24,1408]{1,0:T(8,128)(2,1)S(1)}, u32[]{:S(2)}, u32[]{:S(2)}) collective-permute-start(bf16[24,1408]{1,0:T(8,128)(2,1)S(1)} %get-tuple-element.224), channel_id=1, source_target_pairs={{0,4},{1,5},{2,6},{3,7},{4,0},{5,1},{6,2},{7,3},{8,12},{9,13},{10,... | collective-permute-start | bytes 202760 | tf_op jit(solution)/shard_map/ppermute | solution.py:735
  (228 shorter events, 75.1 us)
Async XLA Ops:
  0.7 17.5 %collective-permute-start.4 = (bf16[1,96,768]{2,1,0:T(8,128)(2,1)}, bf16[1,96,768]{2,1,0:T(8,128)(2,1)S(1)}, u32[]{:S(2)}, u32[]{:S(2)}) collective-permute-start(bf16[1,96,768]{2,1,0:T(8,128)(2,1)} %bitcast.52), channel_id=1, source_target_pairs={{0,4},{1,5},{2,6},{3,7},{4,0},{5,1},{6,2},{7,3},{8,12},{9,13},{10,... | collective-permute-start | bytes 442376 | tf_op jit(solution)/shard_map/ppermute | solution.py:716
  7.9 9.4 %collective-permute-start = (bf16[24,1408]{1,0:T(8,128)(2,1)}, bf16[24,1408]{1,0:T(8,128)(2,1)S(1)}, u32[]{:S(2)}, u32[]{:S(2)}) collective-permute-start(bf16[24,1408]{1,0:T(8,128)(2,1)} %get-tuple-element.114), channel_id=1, source_target_pairs={{0,4},{1,5},{2,6},{3,7},{4,0},{5,1},{6,2},{7,3},{8,12},{9,13},{10,... | collective-permute-start | bytes 202760 | tf_op jit(solution)/shard_map/ppermute | solution.py:735
  7.9 9.3 %collective-permute-start.1 = (bf16[24,1408]{1,0:T(8,128)(2,1)}, bf16[24,1408]{1,0:T(8,128)(2,1)S(1)}, u32[]{:S(2)}, u32[]{:S(2)}) collective-permute-start(bf16[24,1408]{1,0:T(8,128)(2,1)} %get-tuple-element.115), channel_id=1, source_target_pairs={{0,2},{1,3},{2,0},{3,1},{4,6},{5,7},{6,4},{7,5},{8,10},{9,11},{10,... | collective-permute-start | bytes 202760 | tf_op jit(solution)/shard_map/ppermute | solution.py:735
  19.6 12.8 %collective-permute-start.6 = (bf16[128,768]{1,0:T(8,128)(2,1)S(1)}, bf16[128,768]{1,0:T(8,128)(2,1)S(1)}, u32[]{:S(2)}, u32[]{:S(2)}) collective-permute-start(bf16[128,768]{1,0:T(8,128)(2,1)S(1)} %bitcast.48), channel_id=1, source_target_pairs={{0,4},{1,5},{2,6},{3,7},{4,0},{5,1},{6,2},{7,3},{8,12},{9,13},{10,... | collective-permute-start | bytes 589832 | tf_op jit(solution)/shard_map/ppermute | solution.py:716
  22.8 9.5 %collective-permute-start.5 = (bf16[96,1408]{1,0:T(8,128)(2,1)S(1)}, bf16[96,1408]{1,0:T(8,128)(2,1)S(1)}, u32[]{:S(2)}, u32[]{:S(2)}) collective-permute-start(bf16[96,1408]{1,0:T(8,128)(2,1)S(1)} %pad_maximum_fusion.6), channel_id=1, source_target_pairs={{0,16},{1,17},{2,18},{3,19},{4,20},{5,21},{6,22},{7,23},{8,9},{9,8... | collective-permute-start | bytes 811016 | tf_op jit(solution)/shard_map/ppermute | solution.py:716
  24.3 12.2 %collective-permute-start.7 = (bf16[2,96,768]{2,1,0:T(8,128)(2,1)S(1)}, bf16[2,96,768]{2,1,0:T(8,128)(2,1)S(1)}, u32[]{:S(2)}, u32[]{:S(2)}) collective-permute-start(bf16[2,96,768]{2,1,0:T(8,128)(2,1)S(1)} %maximum_select_fusion.2), channel_id=1, source_target_pairs={{0,2},{1,3},{2,0},{3,1},{4,6},{5,7},{6,4},{7,5},{8,10},{9,11},{10,... | collective-permute-start | bytes 884744 | tf_op jit(solution)/shard_map/ppermute | solution.py:716
  36.7 13.0 %collective-permute-start.10 = (bf16[256,768]{1,0:T(8,128)(2,1)S(1)}, bf16[256,768]{1,0:T(8,128)(2,1)S(1)}, u32[]{:S(2)}, u32[]{:S(2)}) collective-permute-start(bf16[256,768]{1,0:T(8,128)(2,1)S(1)} %pad_maximum_fusion.5), channel_id=1, source_target_pairs={{0,2},{1,3},{2,0},{3,1},{4,6},{5,7},{6,4},{7,5},{8,10},{9,11},{10,... | collective-permute-start | bytes 1179656 | tf_op jit(solution)/shard_map/ppermute | solution.py:716
  37.5 14.0 %collective-permute-start.8 = (bf16[192,1408]{1,0:T(8,128)(2,1)S(1)}, bf16[192,1408]{1,0:T(8,128)(2,1)S(1)}, u32[]{:S(2)}, u32[]{:S(2)}) collective-permute-start(bf16[192,1408]{1,0:T(8,128)(2,1)S(1)} %pad_maximum_fusion.4), channel_id=1, source_target_pairs={{0,1},{1,0},{2,3},{3,2},{4,5},{5,4},{6,7},{7,6},{8,24},{9,25},{10,... | collective-permute-start | bytes 1622024 | tf_op jit(solution)/shard_map/ppermute | solution.py:716
  51.6 12.0 %collective-permute-start.11 = (bf16[384,1408]{1,0:T(8,128)(2,1)S(1)}, bf16[384,1408]{1,0:T(8,128)(2,1)S(1)}, u32[]{:S(2)}, u32[]{:S(2)}) collective-permute-start(bf16[384,1408]{1,0:T(8,128)(2,1)S(1)} %pad_maximum_fusion.2.table_ref), channel_id=1, source_target_pairs={{0,8},{1,9},{2,10},{3,11},{4,12},{5,13},{6,14},{7,15},{8,0},{9,1},... | collective-permute-start | bytes 3244040 | tf_op jit(solution)/shard_map/ppermute | solution.py:716
  51.7 9.4 %collective-permute-start.13 = (bf16[2,48,1536]{2,1,0:T(8,128)(2,1)S(1)}, bf16[2,48,1536]{2,1,0:T(8,128)(2,1)S(1)}, u32[]{:S(2)}, u32[]{:S(2)}) collective-permute-start(bf16[2,48,1536]{2,1,0:T(8,128)(2,1)S(1)} %maximum_select_fusion.3), channel_id=1, source_target_pairs={{0,2},{1,3},{2,0},{3,1},{4,6},{5,7},{6,4},{7,5},{8,10},{9,11},{10,... | collective-permute-start | bytes 884744 | tf_op jit(solution)/shard_map/ppermute | solution.py:716
  52.0 16.3 %collective-permute-start.20 = (bf16[384,768]{1,0:T(8,128)(2,1)S(1)}, bf16[384,768]{1,0:T(8,128)(2,1)S(1)}, u32[]{:S(2)}, u32[]{:S(2)}) collective-permute-start(bf16[384,768]{1,0:T(8,128)(2,1)S(1)} %bitcast.42), channel_id=1, source_target_pairs={{0,16},{1,17},{2,18},{3,19},{4,20},{5,21},{6,22},{7,23},{8,9},{9,8... | collective-permute-start | bytes 1769480 | tf_op jit(solution)/shard_map/ppermute | solution.py:716
  61.2 11.3 %collective-permute-start.14 = (bf16[192,1536]{1,0:T(8,128)(2,1)S(1)}, bf16[192,1536]{1,0:T(8,128)(2,1)S(1)}, u32[]{:S(2)}, u32[]{:S(2)}) collective-permute-start(bf16[192,1536]{1,0:T(8,128)(2,1)S(1)} %bitcast.44), channel_id=1, source_target_pairs={{0,16},{1,17},{2,18},{3,19},{4,20},{5,21},{6,22},{7,23},{8,9},{9,8... | collective-permute-start | bytes 1769480 | tf_op jit(solution)/shard_map/ppermute | solution.py:716
  68.3 11.0 %collective-permute-start.12 = (bf16[512,384]{1,0:T(8,128)(2,1)}, bf16[512,384]{1,0:T(8,128)(2,1)S(1)}, u32[]{:S(2)}, u32[]{:S(2)}) collective-permute-start(bf16[512,384]{1,0:T(8,128)(2,1)} %get-tuple-element.143), channel_id=1, source_target_pairs={{0,1},{1,0},{2,3},{3,2},{4,5},{5,4},{6,7},{7,6},{8,9},{9,8},{10,11... | collective-permute-start | bytes 1179656 | tf_op jit(solution)/shard_map/ppermute | solution.py:716
  68.4 31.5 %collective-permute-start.21 = (bf16[768,768]{1,0:T(8,128)(2,1)S(1)}, bf16[768,768]{1,0:T(8,128)(2,1)S(1)}, u32[]{:S(2)}, u32[]{:S(2)}) collective-permute-start(bf16[768,768]{1,0:T(8,128)(2,1)S(1)} %pad_maximum_fusion.1.down_near_hbm), channel_id=1, source_target_pairs={{0,1},{1,0},{2,3},{3,2},{4,5},{5,4},{6,7},{7,6},{8,24},{9,25},{10,... | collective-permute-start | bytes 3538952 | tf_op jit(solution)/shard_map/ppermute | solution.py:716
  80.2 23.4 %collective-permute-start.19 = (bf16[384,1536]{1,0:T(8,128)(2,1)S(1)}, bf16[384,1536]{1,0:T(8,128)(2,1)}, u32[]{:S(2)}, u32[]{:S(2)}) collective-permute-start(bf16[384,1536]{1,0:T(8,128)(2,1)S(1)} %pad_maximum_fusion.in_near_hbm), channel_id=1, source_target_pairs={{0,1},{1,0},{2,3},{3,2},{4,5},{5,4},{6,7},{7,6},{8,24},{9,25},{10,... | collective-permute-start | bytes 3538952 | tf_op jit(solution)/shard_map/ppermute | solution.py:716
  125.7 27.3 %collective-permute-start.28 = (bf16[384,1536]{1,0:T(8,128)(2,1)S(1)}, bf16[384,1536]{1,0:T(8,128)(2,1)}, u32[]{:S(2)}, u32[]{:S(2)}) collective-permute-start(bf16[384,1536]{1,0:T(8,128)(2,1)S(1)} %convolution_convert_fusion), channel_id=1, source_target_pairs={{0,1},{1,0},{2,3},{3,2},{4,5},{5,4},{6,7},{7,6},{8,24},{9,25},{10,... | collective-permute-start | bytes 3538952 | tf_op jit(solution)/shard_map/ppermute | solution.py:716
  126.6 28.2 %collective-permute-start.27 = (bf16[768,768]{1,0:T(8,128)(2,1)S(1)}, bf16[768,768]{1,0:T(8,128)(2,1)S(1)}, u32[]{:S(2)}, u32[]{:S(2)}) collective-permute-start(bf16[768,768]{1,0:T(8,128)(2,1)S(1)} %convolution_convert_fusion.2), channel_id=1, source_target_pairs={{0,1},{1,0},{2,3},{3,2},{4,5},{5,4},{6,7},{7,6},{8,24},{9,25},{10,... | collective-permute-start | bytes 3538952 | tf_op jit(solution)/shard_map/ppermute | solution.py:716
  132.9 10.1 %collective-permute-start.24 = (bf16[128,192]{1,0:T(8,128)(2,1)}, bf16[128,192]{1,0:T(8,128)(2,1)S(1)}, u32[]{:S(2)}, u32[]{:S(2)}) collective-permute-start(bf16[128,192]{1,0:T(8,128)(2,1)} %get-tuple-element.178), channel_id=1, source_target_pairs={{0,4},{1,5},{2,6},{3,7},{4,0},{5,1},{6,2},{7,3},{8,12},{9,13},{10,... | collective-permute-start | bytes 147464 | tf_op jit(solution)/shard_map/ppermute | solution.py:735
  133.8 9.2 %collective-permute-start.25 = (bf16[128,192]{1,0:T(8,128)(2,1)}, bf16[128,192]{1,0:T(8,128)(2,1)S(1)}, u32[]{:S(2)}, u32[]{:S(2)}) collective-permute-start(bf16[128,192]{1,0:T(8,128)(2,1)} %get-tuple-element.179), channel_id=1, source_target_pairs={{0,2},{1,3},{2,0},{3,1},{4,6},{5,7},{6,4},{7,5},{8,10},{9,11},{10,... | collective-permute-start | bytes 147464 | tf_op jit(solution)/shard_map/ppermute | solution.py:735
  134.9 8.1 %collective-permute-start.26 = (bf16[128,192]{1,0:T(8,128)(2,1)}, bf16[128,192]{1,0:T(8,128)(2,1)S(1)}, u32[]{:S(2)}, u32[]{:S(2)}) collective-permute-start(bf16[128,192]{1,0:T(8,128)(2,1)} %get-tuple-element.180), channel_id=1, source_target_pairs={{0,6},{1,7},{2,4},{3,5},{4,2},{5,3},{6,0},{7,1},{8,14},{9,15},{10,... | collective-permute-start | bytes 147464 | tf_op jit(solution)/shard_map/ppermute | solution.py:735
  155.2 21.9 %collective-permute-start.31 = (bf16[192,1536]{1,0:T(8,128)(2,1)S(1)}, bf16[192,1536]{1,0:T(8,128)(2,1)S(1)}, u32[]{:S(2)}, u32[]{:S(2)}) collective-permute-start(bf16[192,1536]{1,0:T(8,128)(2,1)S(1)} %slice.181), channel_id=1, source_target_pairs={{0,16},{1,17},{2,18},{3,19},{4,20},{5,21},{6,22},{7,23},{8,9},{9,8... | collective-permute-start | bytes 1769480 | tf_op jit(solution)/shard_map/ppermute | solution.py:716
  157.6 12.1 %collective-permute-start.29 = (bf16[512,384]{1,0:T(8,128)(2,1)S(1)}, bf16[512,384]{1,0:T(8,128)(2,1)S(1)}, u32[]{:S(2)}, u32[]{:S(2)}) collective-permute-start(bf16[512,384]{1,0:T(8,128)(2,1)S(1)} %copy-done.24), channel_id=1, source_target_pairs={{0,1},{1,0},{2,3},{3,2},{4,5},{5,4},{6,7},{7,6},{8,9},{9,8},{10,11... | collective-permute-start | bytes 1179656 | tf_op jit(solution)/shard_map/ppermute | solution.py:716
  157.9 19.3 %collective-permute-start.30 = (bf16[384,768]{1,0:T(8,128)(2,1)S(1)}, bf16[384,768]{1,0:T(8,128)(2,1)S(1)}, u32[]{:S(2)}, u32[]{:S(2)}) collective-permute-start(bf16[384,768]{1,0:T(8,128)(2,1)S(1)} %slice.182), channel_id=1, source_target_pairs={{0,16},{1,17},{2,18},{3,19},{4,20},{5,21},{6,22},{7,23},{8,9},{9,8... | collective-permute-start | bytes 1769480 | tf_op jit(solution)/shard_map/ppermute | solution.py:716
  177.0 10.8 %collective-permute-start.37 = (bf16[256,768]{1,0:T(8,128)(2,1)}, bf16[256,768]{1,0:T(8,128)(2,1)}, u32[]{:S(2)}, u32[]{:S(2)}) collective-permute-start(bf16[256,768]{1,0:T(8,128)(2,1)} %get-tuple-element.206), channel_id=1, source_target_pairs={{0,2},{1,3},{2,0},{3,1},{4,6},{5,7},{6,4},{7,5},{8,10},{9,11},{10,... | collective-permute-start | bytes 1179656 | tf_op jit(solution)/shard_map/ppermute | solution.py:716
  177.3 17.2 %collective-permute-start.32 = (bf16[384,1408]{1,0:T(8,128)(2,1)}, bf16[384,1408]{1,0:T(8,128)(2,1)S(1)}, u32[]{:S(2)}, u32[]{:S(2)}) collective-permute-start(bf16[384,1408]{1,0:T(8,128)(2,1)} %get-tuple-element.201), channel_id=1, source_target_pairs={{0,8},{1,9},{2,10},{3,11},{4,12},{5,13},{6,14},{7,15},{8,0},{9,1},... | collective-permute-start | bytes 3244040 | tf_op jit(solution)/shard_map/ppermute | solution.py:716
  179.8 14.5 %collective-permute-start.43 = (bf16[192,768]{1,0:T(8,128)(2,1)S(1)}, bf16[192,768]{1,0:T(8,128)(2,1)S(1)}, u32[]{:S(2)}, u32[]{:S(2)}) collective-permute-start(bf16[192,768]{1,0:T(8,128)(2,1)S(1)} %dynamic-slice_convert_fusion), channel_id=1, source_target_pairs={{0,2},{1,3},{2,0},{3,1},{4,6},{5,7},{6,4},{7,5},{8,10},{9,11},{10,... | collective-permute-start | bytes 884744 | tf_op jit(solution)/shard_map/ppermute | solution.py:716
  189.1 34.5 %collective-permute-start.38 = (bf16[128,768]{1,0:T(8,128)(2,1)S(1)}, bf16[128,768]{1,0:T(8,128)(2,1)S(1)}, u32[]{:S(2)}, u32[]{:S(2)}) collective-permute-start(bf16[128,768]{1,0:T(8,128)(2,1)S(1)} %slice.185), channel_id=1, source_target_pairs={{0,4},{1,5},{2,6},{3,7},{4,0},{5,1},{6,2},{7,3},{8,12},{9,13},{10,... | collective-permute-start | bytes 589832 | tf_op jit(solution)/shard_map/ppermute | solution.py:716
  189.2 18.4 %collective-permute-start.35 = (bf16[96,1536]{1,0:T(8,128)(2,1)S(1)}, bf16[96,1536]{1,0:T(8,128)(2,1)S(1)}, u32[]{:S(2)}, u32[]{:S(2)}) collective-permute-start(bf16[96,1536]{1,0:T(8,128)(2,1)S(1)} %dynamic-slice_convert_fusion.1), channel_id=1, source_target_pairs={{0,2},{1,3},{2,0},{3,1},{4,6},{5,7},{6,4},{7,5},{8,10},{9,11},{10,... | collective-permute-start | bytes 884744 | tf_op jit(solution)/shard_map/ppermute | solution.py:716
  194.4 23.2 %collective-permute-start.44 = (bf16[96,768]{1,0:T(8,128)(2,1)S(1)}, bf16[96,768]{1,0:T(8,128)(2,1)S(1)}, u32[]{:S(2)}, u32[]{:S(2)}) collective-permute-start(bf16[96,768]{1,0:T(8,128)(2,1)S(1)} %dynamic-slice_convert_fusion.2), channel_id=1, source_target_pairs={{0,4},{1,5},{2,6},{3,7},{4,0},{5,1},{6,2},{7,3},{8,12},{9,13},{10,... | collective-permute-start | bytes 442376 | tf_op jit(solution)/shard_map/ppermute | solution.py:716
  194.8 13.0 %collective-permute-start.33 = (bf16[192,1408]{1,0:T(8,128)(2,1)S(1)}, bf16[192,1408]{1,0:T(8,128)(2,1)S(1)}, u32[]{:S(2)}, u32[]{:S(2)}) collective-permute-start(bf16[192,1408]{1,0:T(8,128)(2,1)S(1)} %slice.183), channel_id=1, source_target_pairs={{0,1},{1,0},{2,3},{3,2},{4,5},{5,4},{6,7},{7,6},{8,24},{9,25},{10,... | collective-permute-start | bytes 1622024 | tf_op jit(solution)/shard_map/ppermute | solution.py:716
  207.8 9.8 %collective-permute-start.36 = (bf16[48,1536]{1,0:T(8,128)(2,1)S(1)}, bf16[48,1536]{1,0:T(8,128)(2,1)S(1)}, u32[]{:S(2)}, u32[]{:S(2)}) collective-permute-start(bf16[48,1536]{1,0:T(8,128)(2,1)S(1)} %dynamic-slice_convert_fusion.3), channel_id=1, source_target_pairs={{0,4},{1,5},{2,6},{3,7},{4,0},{5,1},{6,2},{7,3},{8,12},{9,13},{10,... | collective-permute-start | bytes 442376 | tf_op jit(solution)/shard_map/ppermute | solution.py:716
  208.0 10.3 %collective-permute-start.34 = (bf16[96,1408]{1,0:T(8,128)(2,1)S(1)}, bf16[96,1408]{1,0:T(8,128)(2,1)S(1)}, u32[]{:S(2)}, u32[]{:S(2)}) collective-permute-start(bf16[96,1408]{1,0:T(8,128)(2,1)S(1)} %slice.184), channel_id=1, source_target_pairs={{0,16},{1,17},{2,18},{3,19},{4,20},{5,21},{6,22},{7,23},{8,9},{9,8... | collective-permute-start | bytes 811016 | tf_op jit(solution)/shard_map/ppermute | solution.py:716
  (44 other events, 262.2 us)

commit v4 on v3

--- a/solution.py
+++ b/solution.py
@@ -191,19 +191,23 @@
     return (lane >= head * HD) & (lane < (head + 1) * HD)
 
 
-def split_pairs(pair_ref, k_ref, v_ref):
+def split_pairs(pair_refs, k_ref, v_ref):
     width = k_ref.shape[1]
-    k_ref[...] = pair_ref[:, :width]
-    v_ref[...] = pair_ref[:, width:]
-
-
-def forward_kernel(q_ref, kv_ref, b_ref, *refs):
+    start = 0
+    for ref in pair_refs:
+        end = start + ref.shape[0]
+        k_ref[start:end] = ref[:, :width]
+        v_ref[start:end] = ref[:, width:]
+        start = end
+
+
+def forward_kernel(q_ref, kv_ref, far_ref, b_ref, *refs):
     *o_refs, l_ref, k_ref, v_ref = refs
     step = pl.program_id(0)
 
     @pl.when(step == 0)
     def _():
-        split_pairs(kv_ref, k_ref, v_ref)
+        split_pairs((kv_ref, far_ref), k_ref, v_ref)
 
     query, keys, values, bias = q_ref[...], k_ref[...], v_ref[...], b_ref[...]
     rows, width = query.shape
@@ -230,23 +234,26 @@
             o_ref[...] = low[start : start + piece]
 
 
-def backward_kernel(q_ref, kv_ref, b_ref, *refs):
-    pieces, refs = refs[:HEAD_GROUPS], refs[HEAD_GROUPS:]
-    l_ref, dq_ref, own_ref, send_ref, k_ref, v_ref, d_ref, dk_ref, dv_ref = refs
+def backward_kernel(q_ref, kv_ref, far_ref, b_ref, *refs):
+    pieces, att_refs, refs = refs[:HEAD_GROUPS], refs[HEAD_GROUPS : 2 * HEAD_GROUPS], refs[2 * HEAD_GROUPS :]
+    l_ref, dq_ref, own_ref, send_ref, k_ref, v_ref, d_ref, o_ref, dk_ref, dv_ref = refs
     step = pl.program_id(0)
     rows, width = q_ref.shape
 
     @pl.when(step == 0)
     def _():
-        split_pairs(kv_ref, k_ref, v_ref)
+        split_pairs((kv_ref, far_ref), k_ref, v_ref)
         dk_ref[...] = jnp.zeros(dk_ref.shape, f32)
         dv_ref[...] = jnp.zeros(dv_ref.shape, f32)
         piece = pieces[0].shape[0]
         for k, ref in enumerate(pieces):
             d_ref[k * piece : (k + 1) * piece] = ref[...]
+            o_ref[k * piece : (k + 1) * piece] = att_refs[k][...]
 
     query, keys, values, bias = q_ref[...], k_ref[...], v_ref[...], b_ref[...]
-    d_att = d_ref[pl.ds(pl.multiple_of(step * rows, rows), rows)]
+    here = pl.ds(pl.multiple_of(step * rows, rows), rows)
+    d_att = d_ref[here]
+    products = d_att.astype(f32) * o_ref[here].astype(f32)
     logs = l_ref[...]
     d_query = jnp.zeros(query.shape, f32)
     for head in range(width // HD):
@@ -256,7 +263,7 @@
         scores = dot(q_head, keys, 1, 1) + bias
         weights = jnp.exp(scores - logs[:, head : head + 1])
         d_probs = dot(d_head, values, 1, 1)
-        delta = jnp.sum(weights * d_probs, axis=1, keepdims=True)
+        delta = jnp.sum(jnp.where(mine, products, 0.0), axis=1, keepdims=True)
         d_scores = (weights * (d_probs - delta)).astype(bf16)
         d_query = d_query + jnp.where(mine, dot(d_scores, keys), 0.0)
         dk_ref[...] += dot(d_scores, q_head, 0, 0)
@@ -274,7 +281,7 @@
 
 def attention_forward(query, pairs, bias):
     rows, width = query.shape
-    key_rows = pairs.shape[0]
+    key_rows = sum(a.shape[0] for a in pairs)
     tile = min(rows, SCORE_CELLS // key_rows)
     piece = rows // HEAD_GROUPS
     results = pl.pallas_call(
@@ -282,7 +289,7 @@
         grid=(rows // tile,),
         in_specs=[
             pl.BlockSpec((tile, width), lambda i: (i, 0)),
-            pl.BlockSpec((key_rows, 2 * width), lambda i: (0, 0)),
+            *[pl.BlockSpec(a.shape, lambda i: (0, 0)) for a in pairs],
             pl.BlockSpec((tile, key_rows), lambda i: (i, 0)),
         ],
         out_specs=[pl.BlockSpec((piece, width), lambda i: (0, 0))] * HEAD_GROUPS
@@ -295,13 +302,13 @@
             flops=16 * rows * key_rows * width, bytes_accessed=4 * rows * key_rows, transcendentals=0
         ),
         name="attention_forward",
-    )(query, pairs, bias)
+    )(query, *pairs, bias)
     return results[:-1], results[-1]
 
 
-def attention_backward(query, pairs, bias, d_pieces, logs):
+def attention_backward(query, pairs, bias, d_pieces, att_pieces, logs):
     rows, width = query.shape
-    key_rows = pairs.shape[0]
+    key_rows = sum(a.shape[0] for a in pairs)
     tile = min(rows, SCORE_CELLS // key_rows)
     fixed = lambda n: pl.BlockSpec((n, 2 * width), lambda i: (0, 0))
     return pl.pallas_call(
@@ -309,10 +316,10 @@
         grid=(rows // tile,),
         in_specs=[
             pl.BlockSpec((tile, width), lambda i: (i, 0)),
-            fixed(key_rows),
+            *[pl.BlockSpec(a.shape, lambda i: (0, 0)) for a in pairs],
             pl.BlockSpec((tile, key_rows), lambda i: (i, 0)),
         ]
-        + [pl.BlockSpec(d_pieces[0].shape, lambda i: (0, 0))] * HEAD_GROUPS
+        + [pl.BlockSpec(d_pieces[0].shape, lambda i: (0, 0))] * (2 * HEAD_GROUPS)
         + [pl.BlockSpec((tile, 128), lambda i: (i, 0))],
         out_specs=[
             pl.BlockSpec((tile, width), lambda i: (i, 0)),
@@ -325,14 +332,14 @@
             jax.ShapeDtypeStruct((key_rows - rows, 2 * width), bf16),
         ],
         scratch_shapes=[pltpu.VMEM((key_rows, width), bf16)] * 2
-        + [pltpu.VMEM((rows, width), bf16)]
+        + [pltpu.VMEM((rows, width), bf16)] * 2
         + [pltpu.VMEM((key_rows, width), f32)] * 2,
         compiler_params=pltpu.CompilerParams(vmem_limit_bytes=56 * 1024 * 1024),
         cost_estimate=pl.CostEstimate(
             flops=30 * rows * key_rows * width, bytes_accessed=4 * rows * key_rows, transcendentals=0
         ),
         name="attention_backward",
-    )(query, pairs, bias, *d_pieces, logs)
+    )(query, *pairs, bias, *d_pieces, *att_pieces, logs)
 
 
 def swap_blocks(a, flags, block):
@@ -526,59 +533,52 @@
         piece[...] = d_attended[:, k * columns : (k + 1) * columns]
 
 
-def branch_grads_kernel(
+def branch_grads_kernel(att_ref, branch_ref, line_ref, out_ref):
+    attended = dot(att_ref[...], line_ref[...]).astype(bf16)
+    out_ref[...] = dot(attended, branch_ref[...], 0, 0).astype(bf16)
+
+
+def query_grads_kernel(
     small_each,
-    att_ref,
-    branch_ref,
+    x_ref,
+    dq_ref,
+    sel_ref,
     sums_ref,
     sums_two_ref,
     ffn_ref,
     near_ref,
-    line_ref,
     unit_ref,
-    keep_ref,
-    send_ref,
-    small_ref,
+    last_ref,
 ):
-    attended = dot(att_ref[...], line_ref[...]).astype(bf16)
-    outs = dot(attended, branch_ref[...], 0, 0)
-    half = outs.shape[0] // 2
-    keep_ref[...] = outs[:half]
-    send_ref[...] = outs[half:].astype(bf16)
+    columns = dq_ref.shape[1]
+    d_query = dq_ref[...]
+    queries = dot(x_ref[...], d_query, 0, 0)
+    sums = jnp.concatenate([column_sum(d_query.astype(f32)), jnp.zeros((7, columns), f32)], axis=0)
+    bias = dot(sel_ref[...], sums.astype(bf16), 1, 1)
     first, second = sums_ref[...], sums_two_ref[...]
     blank = jnp.zeros((2, first.shape[1]), f32)
     vectors = jnp.concatenate(
         [blank, first[2:3], second[2:3], first[0:1], second[0:1], first[1:2], second[1:2]], axis=0
     )
-    vectors = dot(near_ref[...], vectors.astype(bf16), 0, 1)
+    vectors = dot(near_ref[...], vectors.astype(bf16), 0, 1) + bias
     units = ffn_ref.shape[1]
     slot = iota((8, units), 1) % small_each == iota((8, units), 0)
     by_slot = jnp.where(slot, ffn_ref[...], 0.0).astype(bf16)
     ffn = dot(unit_ref[...], by_slot, 1, 1)
-    small_ref[...] = jnp.concatenate([vectors, ffn], axis=1)
-
-
-def query_grads_kernel(x_ref, dq_ref, sel_ref, qkv_ref, grad_ref, bias_ref, back_ref):
-    columns = dq_ref.shape[1]
-    d_query = dq_ref[...]
-    back_ref[...] = dot(d_query, qkv_ref[:, 2 * columns :], 1, 1)
-    grad_ref[...] = dot(x_ref[...], d_query, 0, 0)
-    sums = jnp.concatenate([column_sum(d_query.astype(f32)), jnp.zeros((7, columns), f32)], axis=0)
-    bias_ref[...] = dot(sel_ref[...], sums.astype(bf16), 1, 1)
+    rest = last_ref.shape[1] - columns - 16
+    last = [queries, vectors, ffn, jnp.zeros((queries.shape[0], rest), f32)]
+    last_ref[...] = jnp.concatenate(last, axis=1)
 
 
 def pair_grads_kernel(
     x_ref,
     own_ref,
     got_ref,
+    dq_ref,
     sel_ref,
     qkv_ref,
     out_ref,
-    out_send_ref,
-    small_ref,
-    query_ref,
-    bias_ref,
-    query_back_ref,
+    last_ref,
     keep_ref,
     send_ref,
     back_ref,
@@ -587,28 +587,24 @@
     pair_columns = own_ref.shape[1]
     columns = pair_columns // 2
     width = x_ref.shape[1]
+    half = width // 2
+    at = pair_columns + width
     d_pairs = (own_ref[...] + got_ref[...].astype(f32)).astype(bf16)
-    grad_back = query_back_ref[...] + dot(d_pairs, qkv_ref[:, :pair_columns], 1, 1)
+    pairs = dot(x_ref[...], d_pairs, 0, 0).astype(bf16)
+    sums = [jnp.zeros((1, columns), f32), column_sum(d_pairs[:, columns:].astype(f32))]
+    sums = jnp.concatenate([*sums, jnp.zeros((6, columns), f32)], axis=0)
+    bias = dot(sel_ref[...], sums.astype(bf16), 1, 1)[:, 1:2]
+    last = last_ref[...]
+    last = (last + jnp.where(iota(last.shape, 1) == columns + 1, bias, 0.0)).astype(bf16)
+    for ref, rows in ((send_ref, slice(half, width)), (keep_ref, slice(0, half))):
+        ref[:, :pair_columns] = pairs[rows]
+        ref[:, pair_columns:at] = out_ref[rows]
+        ref[:, at:] = last[rows]
+    grad_back = dot(dq_ref[...], qkv_ref[:, pair_columns:], 1, 1)
+    grad_back = grad_back + dot(d_pairs, qkv_ref[:, :pair_columns], 1, 1)
     rows = back_ref.shape[0]
     back_ref[...] = grad_back[:rows]
     back_send_ref[...] = grad_back[rows:].astype(bf16)
-    pairs = dot(x_ref[...], d_pairs, 0, 0)
-    sums = [jnp.zeros((1, columns), f32), column_sum(d_pairs[:, columns:].astype(f32))]
-    sums = jnp.concatenate([*sums, jnp.zeros((6, columns), f32)], axis=0)
-    bias = dot(sel_ref[...], sums.astype(bf16), 1, 1)
-    small = small_ref[...]
-    vectors = small[:, :8] + bias + bias_ref[...]
-    at = pair_columns + width
-    rest = keep_ref.shape[1] - at - columns - 16
-    last = [query_ref[...], vectors, small[:, 8:], jnp.zeros((width, rest), f32)]
-    last = jnp.concatenate(last, axis=1)
-    half = width // 2
-    keep_ref[:, :pair_columns] = pairs[:half]
-    keep_ref[:, pair_columns:at] = out_ref[...]
-    keep_ref[:, at:] = last[:half]
-    send_ref[:, :pair_columns] = pairs[half:].astype(bf16)
-    send_ref[:, pair_columns:at] = out_send_ref[...]
-    send_ref[:, at:] = last[half:].astype(bf16)
 
 
 def finish_kernel(small_each, place_ref, own_ref, *refs):
@@ -949,9 +945,11 @@
     )
     ffn_row = outer_swap(ffn_row)
     kept_pairs, out_line, params, qkv_slice = tie(own_pairs, out_line, params, qkv_slice)
-    pairs = jnp.concatenate([kept_pairs, swap(grid, own_pairs, part_bits[0])], axis=0)
-    pairs = gather_near(grid, pairs, part_bits[1:])
-    pairs, in_near = tie(pairs, in_near)
+    far_pairs = swap(grid, own_pairs, part_bits[0])
+    if parts > 2:
+        far_pairs = gather_near(grid, jnp.concatenate([kept_pairs, far_pairs]), part_bits[1:])[line_len:]
+    kept_pairs, far_pairs, in_near = tie(kept_pairs, far_pairs, in_near)
+    pairs = (kept_pairs, far_pairs)
     in_far = swap(grid, in_near, grid.plane_bits[-1])
     in_near, in_far = outer_swap(in_near), outer_swap(in_far)
 
@@ -1061,26 +1059,20 @@
             total = keep + got.astype(f32)
         return total
 
-    small_sums = call(
-        functools.partial(branch_grads_kernel, small_each),
-        [((width // 2, width), f32), ((width // 2, width), bf16), ((width, 16), f32)],
+    (grad_out,) = call(
+        branch_grads_kernel,
+        [((width, width), bf16)],
         attended,
         d_branch,
-        sums_one,
-        sums_two,
-        ffn_sums,
-        to_near,
         line_near,
-        near_unit,
         name="branch_gradients",
     )
-    d_pieces[0], *small_sums = tie(d_pieces[0], *small_sums)
+    d_pieces[0], grad_out = tie(d_pieces[0], grad_out)
 
     d_query, pairs_own, pairs_send = attention_backward(
-        query, pairs, mask_bias, [d_pieces[0], *got_d_att], logs
-    )
-    pairs_own, down_total, in_total = tie(pairs_own, down_total, in_total)
-    down_total = reduce_near(grid, down_total, grid.plane_bits[:-1])
+        query, pairs, mask_bias, [d_pieces[0], *got_d_att], att_pieces, logs
+    )
+    pairs_own, in_total = tie(pairs_own, in_total)
     in_total = reduce_near(grid, in_total, grid.plane_bits[:-1])
     if parts == 2:
         pairs_got = swap(grid, pairs_send, part_bits[0])
@@ -1088,19 +1080,26 @@
         pairs_all = jnp.concatenate([pairs_own, pairs_send.astype(f32)])
         pairs_own = reduce_near(grid, pairs_all, part_bits)
         pairs_got = jnp.zeros(pairs_own.shape, bf16)
-    query_grads = call(
-        query_grads_kernel,
-        [((width, columns), f32), ((width, 8), f32), ((line_len, width), f32)],
+    last_columns = table_width - 2 * columns - width
+    (last_grads,) = call(
+        functools.partial(query_grads_kernel, small_each),
+        [((width, last_columns), f32)],
         x_near,
         d_query,
         near_group,
-        qkv_slice,
+        sums_one,
+        sums_two,
+        ffn_sums,
+        to_near,
+        near_unit,
         name="query_gradients",
     )
+    last_grads, down_total = tie(last_grads, down_total)
+    down_total = reduce_near(grid, down_total, grid.plane_bits[:-1])
     grad_keep, grad_send, back_keep, back_send = call(
         pair_grads_kernel,
         [
-            ((width // 2, table_width), f32),
+            ((width // 2, table_width), bf16),
             ((width // 2, table_width), bf16),
             ((line_len // 2, width), f32),
             ((line_len // 2, width), bf16),
@@ -1108,10 +1107,11 @@
         x_near,
         pairs_own,
         pairs_got,
+        d_query,
         near_group,
         qkv_slice,
-        *small_sums,
-        *query_grads,
+        grad_out,
+        last_grads,
         name="pair_gradients",
     )
     grad_send, down_total, in_total = tie(grad_send, down_total, in_total)
@@ -1119,7 +1119,7 @@
     in_pairs = line_sum(in_total)
     back = back_keep + swap(grid, back_send, line_bits[1]).astype(f32)
     back = reduce_near(grid, back, line_bits[:1])
-    total = grad_keep + chip_swap(grad_send).astype(f32)
+    total = grad_keep.astype(f32) + chip_swap(grad_send).astype(f32)
     total = reduce_near(grid, total, grid.plane_bits)
     total, in_pairs, d_one = tie(total, in_pairs, d_one)
     in_got = chip_swap(in_pairs[rows_each:])

time: 234 us -> 224 us (0.957)
  waiting for transfers between devices: 78.8 us -> 67.5 us
  starting transfers between devices: 49 us -> 53.8 us
  Pallas kernels: 66.6 us -> 63.7 us
    ppermute x33, waiting for transfers between devices: 70.1 us -> 59.2 us  [swap(): return lax.ppermute(held, BOTH, grid.flip(bits))]
    ppermute x33, starting transfers between devices: 31.4 us -> 36.2 us  [swap(): return lax.ppermute(held, BOTH, grid.flip(bits))]
    unnamed x63 -> x57, local copies, waits for them, and re-layouts: 5.27 us -> 5.33 us
  transfers between devices with their start and end apart: 45 -> 45, of which waited for: 20 -> 21; matrix products, arithmetic and copies ran while one was open for 13% -> 13% of each run, Pallas kernels for 21% -> 21%
where the time goes in v4:
time: 224 us; the launch traced here: 223 us
  waiting for transfers between devices  67.5 us (30%)
  Pallas kernels  63.7 us (28%)
  starting transfers between devices  53.8 us (24%)
  other arithmetic  20.8 us (9%)
  local copies, waits for them, and re-layouts  11.2 us (5%)
  matrix products  4.96 us (2%)
    ppermute x33, waiting for transfers between devices, swap(): return lax.ppermute(held, BOTH, grid.flip(bits))  59.2 us
    pallas_call x11, Pallas kernels, call(): pl.pallas_call(body, in_specs=specs, out_specs=[pl.BlockSpec(memory_space...  49.1 us
    ppermute x33, starting transfers between devices, swap(): return lax.ppermute(held, BOTH, grid.flip(bits))  36.2 us
    ppermute x12, starting transfers between devices, line_swap(): lax.ppermute(piece, BOTH, grid.cross(crossed(k + 1)))  17.7 us
    pallas_call x1, Pallas kernels, attention_backward(): pl.pallas_call(backward_kernel, grid=(rows // tile,), in_specs=[pl.BlockS...  8.39 us
    ppermute x12, waiting for transfers between devices, line_swap(): lax.ppermute(piece, BOTH, grid.cross(crossed(k + 1)))  8.28 us
    pallas_call x1, Pallas kernels, attention_forward(): pl.pallas_call(forward_kernel, grid=(rows // tile,), in_specs=[pl.BlockSp...  6.13 us
    unnamed x57, local copies, waits for them, and re-layouts  5.33 us
  transfers between devices with their start and end apart: 45, of which 21 were waited for; matrix products, arithmetic and copies ran while one was open for 13% of the time, Pallas kernels for 21%

profile of v4, /device:TPU:0, one launch (start us, length us, event | category | flops | bytes accessed | tf_op | source)
XLA Modules:
  0.0 223.2 jit_solution(9951740938253602047)
XLA Ops:
  0.7 4.1 %collective-permute-start.4 = (bf16[1,96,768]{2,1,0:T(8,128)(2,1)}, bf16[1,96,768]{2,1,0:T(8,128)(2,1)S(1)}, u32[]{:S(2)}, u32[]{:S(2)}) collective-permute-start(bf16[1,96,768]{2,1,0:T(8,128)(2,1)} %bitcast.52), channel_id=1, source_target_pairs={{0,4},{1,5},{2,6},{3,7},{4,0},{5,1},{6,2},{7,3},{8,12},{9,13},{10,... | collective-permute-start | bytes 442376 | tf_op jit(solution)/shard_map/ppermute | solution.py:712
  5.4 2.4 %pack_weights.1 = (bf16[24,1408]{1,0:T(8,128)(2,1)}, bf16[24,1408]{1,0:T(8,128)(2,1)}, bf16[24,1408]{1,0:T(8,128)(2,1)}, bf16[24,1408]{1,0:T(8,128)(2,1)}, bf16[...) custom-call(s32[2]{0:T(128)} %pad_add_fusion.2.place_ref, bf16[24,2304]{1,0:T(8,128)(2,1)} %qkv_ref.1, ...), custom_call_target="tpu_custom_call" | custom-call | flops 100000000 | bytes 688712 | tf_op jit(solution)/shard_map/pack_weights/pallas_call | solution.py:55
  9.8 2.5 %collective-permute-start.2 = (bf16[24,1408]{1,0:T(8,128)(2,1)}, bf16[24,1408]{1,0:T(8,128)(2,1)S(1)}, u32[]{:S(2)}, u32[]{:S(2)}) collective-permute-start(bf16[24,1408]{1,0:T(8,128)(2,1)} %get-tuple-element.110), channel_id=1, source_target_pairs={{0,6},{1,7},{2,4},{3,5},{4,2},{5,3},{6,0},{7,1},{8,14},{9,15},{10,... | collective-permute-start | bytes 202760 | tf_op jit(solution)/shard_map/ppermute | solution.py:731
  19.5 3.3 %collective-permute-start.6 = (bf16[128,768]{1,0:T(8,128)(2,1)S(1)}, bf16[128,768]{1,0:T(8,128)(2,1)S(1)}, u32[]{:S(2)}, u32[]{:S(2)}) collective-permute-start(bf16[128,768]{1,0:T(8,128)(2,1)S(1)} %bitcast.48), channel_id=1, source_target_pairs={{0,4},{1,5},{2,6},{3,7},{4,0},{5,1},{6,2},{7,3},{8,12},{9,13},{10,... | collective-permute-start | bytes 589832 | tf_op jit(solution)/shard_map/ppermute | solution.py:712
  27.0 3.2 %and_select_fusion.b_ref = f32[512,1024]{1,0:T(8,128)} fusion(s32[1024]{0:T(1024)S(1)} %bitcast.54, s32[1024]{0:T(1024)S(1)} %get-tuple-element.228, s32[512]{0:T(512)S(1)} %slice_bitcast_fusion, s32[512]{0:T(512)S(1)} %get-tuple-element.205, s32[512]{0:T(512)S(1)} %get-tuple-element.204, s32[512]{0:T(512)S(1)} %bitcast.56, s32[512]{0:T(512)S(1)} %bitcast.57, ...), kind=kLoop, calls=%fused_computation.13 | loop fusion | flops 8388608 | bytes 2121728 | tf_op jit(solution)/shard_map/jit(_where)/select_n | solution.py:900
  32.4 4.1 %collective-permute-done.7 = bf16[2,96,768]{2,1,0:T(8,128)(2,1)S(1)} collective-permute-done((bf16[2,96,768]{2,1,0:T(8,128)(2,1)S(1)}, bf16[2,96,768]{2,1,0:T(8,128)(2,1)S(1)}, u32[]{:S(2)}, u32[]{:S(2)}) %collective-permute-start.7) | collective-permute-done | bytes 294944 | tf_op jit(solution)/shard_map/ppermute | solution.py:712
  39.4 5.2 %collective-permute-done.9 = bf16[1,48,1536]{2,1,0:T(8,128)(2,1)S(1)} collective-permute-done((bf16[1,48,1536]{2,1,0:T(8,128)(2,1)S(1)}, bf16[1,48,1536]{2,1,0:T(8,128)(2,1)S(1)}, u32[]{:S(2)}, u32[]{:S(2)}) %collective-permute-start.9) | collective-permute-done | bytes 147488 | tf_op jit(solution)/shard_map/ppermute | solution.py:712
  44.7 5.0 %collective-permute-done.10 = bf16[256,768]{1,0:T(8,128)(2,1)S(1)} collective-permute-done((bf16[256,768]{1,0:T(8,128)(2,1)S(1)}, bf16[256,768]{1,0:T(8,128)(2,1)S(1)}, u32[]{:S(2)}, u32[]{:S(2)}) %collective-permute-start.10) | collective-permute-done | bytes 393248 | tf_op jit(solution)/shard_map/ppermute | solution.py:712
  52.0 2.4 %collective-permute-start.20 = (bf16[384,768]{1,0:T(8,128)(2,1)S(1)}, bf16[384,768]{1,0:T(8,128)(2,1)S(1)}, u32[]{:S(2)}, u32[]{:S(2)}) collective-permute-start(bf16[384,768]{1,0:T(8,128)(2,1)S(1)} %bitcast.42), channel_id=1, source_target_pairs={{0,16},{1,17},{2,18},{3,19},{4,20},{5,21},{6,22},{7,23},{8,9},{9,8... | collective-permute-start | bytes 1769480 | tf_op jit(solution)/shard_map/ppermute | solution.py:712
  54.3 6.7 %collective-permute-done.13 = bf16[2,48,1536]{2,1,0:T(8,128)(2,1)S(1)} collective-permute-done((bf16[2,48,1536]{2,1,0:T(8,128)(2,1)S(1)}, bf16[2,48,1536]{2,1,0:T(8,128)(2,1)S(1)}, u32[]{:S(2)}, u32[]{:S(2)}) %collective-permute-start.13) | collective-permute-done | bytes 294944 | tf_op jit(solution)/shard_map/ppermute | solution.py:712
  61.2 2.4 %collective-permute-start.14 = (bf16[192,1536]{1,0:T(8,128)(2,1)S(1)}, bf16[192,1536]{1,0:T(8,128)(2,1)S(1)}, u32[]{:S(2)}, u32[]{:S(2)}) collective-permute-start(bf16[192,1536]{1,0:T(8,128)(2,1)S(1)} %bitcast.44), channel_id=1, source_target_pairs={{0,16},{1,17},{2,18},{3,19},{4,20},{5,21},{6,22},{7,23},{8,9},{9,8... | collective-permute-start | bytes 1769480 | tf_op jit(solution)/shard_map/ppermute | solution.py:712
  64.6 3.6 %project.1 = (bf16[512,192]{1,0:T(8,128)(2,1)}, bf16[512,384]{1,0:T(8,128)(2,1)}) custom-call(bf16[512,768]{1,0:T(8,128)(2,1)} %fusion.5.x_ref, bf16[384,1408]{1,0:T(8,128)(2,1)} %copy-done.2, bf16[384,1408]{1,0:T(8,128)(2,1)} %copy-done.4, bf16[768,192]{1,0:T(8,128)(2,1)} %compare_convert_fusion.2.sel_ref), custom_call_target="tpu_custom_call" | custom-call | flops 100000000 | bytes 3244032 | tf_op jit(solution)/shard_map/project/pallas_call | solution.py:55
  72.6 6.6 %unfold_weights.1 = (bf16[768,576]{1,0:T(8,128)(2,1)}, bf16[768,768]{1,0:T(8,128)(2,1)}, f32[8,768]{1,0:T(8,128)}, f32[1,1536]{1,0:T(1,128)}) custom-call(bf16[384,1408]{1,0:T(8,128)(2,1)} %copy-done.2, bf16[384,1408]{1,0:T(8,128)(2,1)} %copy-done.4, bf16[768,768]{1,0:T(8,128)(2,1)} %get-tuple-element.131.near_ref, ...), custom_call_target="tpu_custom_call" | custom-call | flops 100000000 | bytes 6881280 | tf_op jit(solution)/shard_map/unfold_weights/pallas_call | solution.py:55
  80.0 6.1 %attention_forward.1 = (bf16[128,192]{1,0:T(8,128)(2,1)}, bf16[128,192]{1,0:T(8,128)(2,1)}, bf16[128,192]{1,0:T(8,128)(2,1)}, bf16[128,192]{1,0:T(8,128)(2,1)}, f32[512,128]{1,0:T(8,128)}) custom-call(bf16[512,192]{1,0:T(8,128)(2,1)} %get-tuple-element.127.q_ref, bf16[512,384]{1,0:T(8,128)(2,1)} %get-tuple-element.139.kv_ref, bf16[512,384]{1,0:T(8,128)(2,1)} %copy-done.21, ...), custom_call_target="tpu_custom_call" | custom-call | flops 1610612736 | bytes 2097152 | tf_op jit(solution)/shard_map/attention_forward/pallas_call | solution.py:287
  90.5 3.3 %collective-permute-done.15 = bf16[128,192]{1,0:T(8,128)(2,1)S(1)} collective-permute-done((bf16[128,192]{1,0:T(8,128)(2,1)}, bf16[128,192]{1,0:T(8,128)(2,1)S(1)}, u32[]{:S(2)}, u32[]{:S(2)}) %collective-permute-start.15) | collective-permute-done | bytes 49184 | tf_op jit(solution)/shard_map/ppermute | solution.py:731
  99.0 4.6 %collective-permute-done.19.in_far_hbm = bf16[384,1536]{1,0:T(8,128)(2,1)} collective-permute-done((bf16[384,1536]{1,0:T(8,128)(2,1)S(1)}, bf16[384,1536]{1,0:T(8,128)(2,1)}, u32[]{:S(2)}, u32[]{:S(2)}) %collective-permute-start.19) | collective-permute-done | bytes 1179680 | tf_op jit(solution)/shard_map/ppermute | solution.py:712
  103.6 7.9 %ffn_forward.1 = (f32[256,768]{1,0:T(8,128)}, f32[256,768]{1,0:T(8,128)}, f32[256,128]{1,0:T(8,128)}, bf16[256,768]{1,0:T(8,128)(2,1)}, f32[256,1536]{1,0:T(8,12...) custom-call(s32[2]{0:T(128)} %pad_add_fusion.1.flag_ref, ...), custom_call_target="tpu_custom_call" | custom-call | flops 100000000 | bytes 8165384 | tf_op jit(solution)/shard_map/ffn_forward/pallas_call | solution.py:55
  114.3 7.9 %ffn_backward.1 = (bf16[128,768]{1,0:T(8,128)(2,1)}, f32[128,768]{1,0:T(8,128)}, bf16[128,768]{1,0:T(8,128)(2,1)}, bf16[256,768]{1,0:T(8,128)(2,1)}, bf16[256,15...) custom-call(s32[2]{0:T(128)} %pad_add_fusion.1.flag_ref, f32[256,768]{1,0:T(8,128)} %get-tuple-element.152.part_ref, ...), custom_call_target="tpu_custom_call" | custom-call | flops 100000000 | bytes 10125320 | tf_op jit(solution)/shard_map/ffn_backward/pallas_call | solution.py:55
  129.8 3.0 %branch_backward.1 = (f32[128,768]{1,0:T(8,128)}, bf16[128,768]{1,0:T(8,128)(2,1)}, f32[8,768]{1,0:T(8,128)}, bf16[128,192]{1,0:T(8,128)(2,1)}, bf16[128,192]{1,...) custom-call(f32[128,768]{1,0:T(8,128)} %get-tuple-element.157.keep_ref, bf16[128,768]{1,0:T(8,128)(2,1)} %copy-done.14, ...), custom_call_target="tpu_custom_call" | custom-call | flops 100000000 | bytes 2252800 | tf_op jit(solution)/shard_map/branch_backward/pallas_call | solution.py:55
  134.9 2.3 %collective-permute-start.26 = (bf16[128,192]{1,0:T(8,128)(2,1)}, bf16[128,192]{1,0:T(8,128)(2,1)S(1)}, u32[]{:S(2)}, u32[]{:S(2)}) collective-permute-start(bf16[128,192]{1,0:T(8,128)(2,1)} %get-tuple-element.169), channel_id=1, source_target_pairs={{0,6},{1,7},{2,4},{3,5},{4,2},{5,3},{6,0},{7,1},{8,14},{9,15},{10,... | collective-permute-start | bytes 147464 | tf_op jit(solution)/shard_map/ppermute | solution.py:731
  137.2 3.3 %branch_gradients.1.out_ref = bf16[768,768]{1,0:T(8,128)(2,1)} custom-call(bf16[128,768]{1,0:T(8,128)(2,1)} %pad_maximum_fusion.6.att_ref, bf16[128,768]{1,0:T(8,128)(2,1)} %get-tuple-element.165.branch_ref, bf16[768,768]{1,0:T(8,128)(2,1)} %get-tuple-element.132.line_ref), custom_call_target="tpu_custom_call" | custom-call | flops 100000000 | bytes 1572864 | tf_op jit(solution)/shard_map/branch_gradients/pallas_call | solution.py:55
  141.9 8.4 %attention_backward.1 = (bf16[512,192]{1,0:T(8,128)(2,1)}, f32[512,384]{1,0:T(8,128)}, bf16[512,384]{1,0:T(8,128)(2,1)}) custom-call(bf16[512,192]{1,0:T(8,128)(2,1)} %get-tuple-element.127.q_ref, bf16[512,384]{1,0:T(8,128)(2,1)} %get-tuple-element.139.kv_ref, bf16[512,384]{1,0:T(8,128)(2,1)} %copy-done.21, f32[512,1024]{1,0:T(8,128)} %and_select_fusion.b_ref, ...), custom_call_target="tpu_custom_call" | custom-call | flops 3019898880 | bytes 2097152 | tf_op jit(solution)/shard_map/attention_backward/pallas_call | solution.py:314
  155.4 4.9 %query_gradients.1.last_ref = f32[768,256]{1,0:T(8,128)} custom-call(bf16[512,768]{1,0:T(8,128)(2,1)} %fusion.5.x_ref, bf16[512,192]{1,0:T(8,128)(2,1)} %get-tuple-element.176.dq_ref, bf16[768,192]{1,0:T(8,128)(2,1)} %compare_convert_fusion.2.sel_ref, f32[8,768]{1,0:T(8,128)} %get-tuple-element.179.sums_ref, f32[8,768]{1,0:T(8,128)} %get-tuple-element.180.sums_two_ref, ...), custom_call_target="tpu_custom_call" | custom-call | flops 100000000 | bytes 4872192 | tf_op jit(solution)/shard_map/query_gradients/pallas_call | solution.py:55
  161.1 4.6 %collective-permute-done.28.got_ref = bf16[512,384]{1,0:T(8,128)(2,1)} collective-permute-done((bf16[512,384]{1,0:T(8,128)(2,1)}, bf16[512,384]{1,0:T(8,128)(2,1)}, u32[]{:S(2)}, u32[]{:S(2)}) %collective-permute-start.28) | collective-permute-done | bytes 393248 | tf_op jit(solution)/shard_map/ppermute | solution.py:712
  165.7 5.6 %pair_gradients.1 = (bf16[384,1408]{1,0:T(8,128)(2,1)}, bf16[384,1408]{1,0:T(8,128)(2,1)}, f32[256,768]{1,0:T(8,128)}, bf16[256,768]{1,0:T(8,128)(2,1)}) custom-call(bf16[512,768]{1,0:T(8,128)(2,1)} %fusion.5.x_ref, f32[512,384]{1,0:T(8,128)} %get-tuple-element.174.own_ref, bf16[512,384]{1,0:T(8,128)(2,1)} %collective-permute-done.28.got_ref, ...), custom_call_target="tpu_custom_call" | custom-call | flops 100000000 | bytes 5308416 | tf_op jit(solution)/shard_map/pair_gradients/pallas_call | solution.py:55
  172.6 3.4 %collective-permute-start.32 = (bf16[384,1408]{1,0:T(8,128)(2,1)}, bf16[384,1408]{1,0:T(8,128)(2,1)S(1)}, u32[]{:S(2)}, u32[]{:S(2)}) collective-permute-start(bf16[384,1408]{1,0:T(8,128)(2,1)} %get-tuple-element.189), channel_id=1, source_target_pairs={{0,8},{1,9},{2,10},{3,11},{4,12},{5,13},{6,14},{7,15},{8,0},{9,1},... | collective-permute-start | bytes 3244040 | tf_op jit(solution)/shard_map/ppermute | solution.py:712
  176.4 3.5 %collective-permute-done.37 = bf16[256,768]{1,0:T(8,128)(2,1)} collective-permute-done((bf16[256,768]{1,0:T(8,128)(2,1)}, bf16[256,768]{1,0:T(8,128)(2,1)}, u32[]{:S(2)}, u32[]{:S(2)}) %collective-permute-start.37) | collective-permute-done | bytes 393248 | tf_op jit(solution)/shard_map/ppermute | solution.py:712
  183.0 5.6 %collective-permute-done.43 = bf16[192,768]{1,0:T(8,128)(2,1)S(1)} collective-permute-done((bf16[192,768]{1,0:T(8,128)(2,1)S(1)}, bf16[192,768]{1,0:T(8,128)(2,1)S(1)}, u32[]{:S(2)}, u32[]{:S(2)}) %collective-permute-start.43) | collective-permute-done | bytes 294944 | tf_op jit(solution)/shard_map/ppermute | solution.py:712
  191.4 7.9 %collective-permute-done.35 = bf16[96,1536]{1,0:T(8,128)(2,1)S(1)} collective-permute-done((bf16[96,1536]{1,0:T(8,128)(2,1)S(1)}, bf16[96,1536]{1,0:T(8,128)(2,1)S(1)}, u32[]{:S(2)}, u32[]{:S(2)}) %collective-permute-start.35) | collective-permute-done | bytes 294944 | tf_op jit(solution)/shard_map/ppermute | solution.py:712
  199.7 3.1 %collective-permute-start.34 = (bf16[96,1408]{1,0:T(8,128)(2,1)S(1)}, bf16[96,1408]{1,0:T(8,128)(2,1)S(1)}, u32[]{:S(2)}, u32[]{:S(2)}) collective-permute-start(bf16[96,1408]{1,0:T(8,128)(2,1)S(1)} %slice.184), channel_id=1, source_target_pairs={{0,16},{1,17},{2,18},{3,19},{4,20},{5,21},{6,22},{7,23},{8,9},{9,8... | collective-permute-start | bytes 811016 | tf_op jit(solution)/shard_map/ppermute | solution.py:712
  202.8 5.1 %collective-permute-done.36 = bf16[48,1536]{1,0:T(8,128)(2,1)S(1)} collective-permute-done((bf16[48,1536]{1,0:T(8,128)(2,1)S(1)}, bf16[48,1536]{1,0:T(8,128)(2,1)S(1)}, u32[]{:S(2)}, u32[]{:S(2)}) %collective-permute-start.36) | collective-permute-done | bytes 147488 | tf_op jit(solution)/shard_map/ppermute | solution.py:712
  208.8 2.3 %collective-permute-start.41 = (bf16[24,1408]{1,0:T(8,128)(2,1)S(1)}, bf16[24,1408]{1,0:T(8,128)(2,1)S(1)}, u32[]{:S(2)}, u32[]{:S(2)}) collective-permute-start(bf16[24,1408]{1,0:T(8,128)(2,1)S(1)} %get-tuple-element.210), channel_id=1, source_target_pairs={{0,6},{1,7},{2,4},{3,5},{4,2},{5,3},{6,0},{7,1},{8,14},{9,15},{10,... | collective-permute-start | bytes 202760 | tf_op jit(solution)/shard_map/ppermute | solution.py:731
  (221 shorter events, 77.6 us)
Async XLA Ops:
  0.7 17.5 %collective-permute-start.4 = (bf16[1,96,768]{2,1,0:T(8,128)(2,1)}, bf16[1,96,768]{2,1,0:T(8,128)(2,1)S(1)}, u32[]{:S(2)}, u32[]{:S(2)}) collective-permute-start(bf16[1,96,768]{2,1,0:T(8,128)(2,1)} %bitcast.52), channel_id=1, source_target_pairs={{0,4},{1,5},{2,6},{3,7},{4,0},{5,1},{6,2},{7,3},{8,12},{9,13},{10,... | collective-permute-start | bytes 442376 | tf_op jit(solution)/shard_map/ppermute | solution.py:712
  7.8 9.4 %collective-permute-start = (bf16[24,1408]{1,0:T(8,128)(2,1)}, bf16[24,1408]{1,0:T(8,128)(2,1)S(1)}, u32[]{:S(2)}, u32[]{:S(2)}) collective-permute-start(bf16[24,1408]{1,0:T(8,128)(2,1)} %get-tuple-element.108), channel_id=1, source_target_pairs={{0,4},{1,5},{2,6},{3,7},{4,0},{5,1},{6,2},{7,3},{8,12},{9,13},{10,... | collective-permute-start | bytes 202760 | tf_op jit(solution)/shard_map/ppermute | solution.py:731
  7.9 9.3 %collective-permute-start.1 = (bf16[24,1408]{1,0:T(8,128)(2,1)}, bf16[24,1408]{1,0:T(8,128)(2,1)S(1)}, u32[]{:S(2)}, u32[]{:S(2)}) collective-permute-start(bf16[24,1408]{1,0:T(8,128)(2,1)} %get-tuple-element.109), channel_id=1, source_target_pairs={{0,2},{1,3},{2,0},{3,1},{4,6},{5,7},{6,4},{7,5},{8,10},{9,11},{10,... | collective-permute-start | bytes 202760 | tf_op jit(solution)/shard_map/ppermute | solution.py:731
  19.5 12.7 %collective-permute-start.6 = (bf16[128,768]{1,0:T(8,128)(2,1)S(1)}, bf16[128,768]{1,0:T(8,128)(2,1)S(1)}, u32[]{:S(2)}, u32[]{:S(2)}) collective-permute-start(bf16[128,768]{1,0:T(8,128)(2,1)S(1)} %bitcast.48), channel_id=1, source_target_pairs={{0,4},{1,5},{2,6},{3,7},{4,0},{5,1},{6,2},{7,3},{8,12},{9,13},{10,... | collective-permute-start | bytes 589832 | tf_op jit(solution)/shard_map/ppermute | solution.py:712
  22.8 9.5 %collective-permute-start.5 = (bf16[96,1408]{1,0:T(8,128)(2,1)S(1)}, bf16[96,1408]{1,0:T(8,128)(2,1)S(1)}, u32[]{:S(2)}, u32[]{:S(2)}) collective-permute-start(bf16[96,1408]{1,0:T(8,128)(2,1)S(1)} %pad_maximum_fusion.5), channel_id=1, source_target_pairs={{0,16},{1,17},{2,18},{3,19},{4,20},{5,21},{6,22},{7,23},{8,9},{9,8... | collective-permute-start | bytes 811016 | tf_op jit(solution)/shard_map/ppermute | solution.py:712
  24.3 12.2 %collective-permute-start.7 = (bf16[2,96,768]{2,1,0:T(8,128)(2,1)S(1)}, bf16[2,96,768]{2,1,0:T(8,128)(2,1)S(1)}, u32[]{:S(2)}, u32[]{:S(2)}) collective-permute-start(bf16[2,96,768]{2,1,0:T(8,128)(2,1)S(1)} %maximum_select_fusion.2), channel_id=1, source_target_pairs={{0,2},{1,3},{2,0},{3,1},{4,6},{5,7},{6,4},{7,5},{8,10},{9,11},{10,... | collective-permute-start | bytes 884744 | tf_op jit(solution)/shard_map/ppermute | solution.py:712
  36.6 8.0 %collective-permute-start.9 = (bf16[1,48,1536]{2,1,0:T(8,128)(2,1)S(1)}, bf16[1,48,1536]{2,1,0:T(8,128)(2,1)S(1)}, u32[]{:S(2)}, u32[]{:S(2)}) collective-permute-start(bf16[1,48,1536]{2,1,0:T(8,128)(2,1)S(1)} %maximum_bitcast_fusion), channel_id=1, source_target_pairs={{0,4},{1,5},{2,6},{3,7},{4,0},{5,1},{6,2},{7,3},{8,12},{9,13},{10,... | collective-permute-start | bytes 442376 | tf_op jit(solution)/shard_map/ppermute | solution.py:712
  36.7 13.0 %collective-permute-start.10 = (bf16[256,768]{1,0:T(8,128)(2,1)S(1)}, bf16[256,768]{1,0:T(8,128)(2,1)S(1)}, u32[]{:S(2)}, u32[]{:S(2)}) collective-permute-start(bf16[256,768]{1,0:T(8,128)(2,1)S(1)} %pad_maximum_fusion.4), channel_id=1, source_target_pairs={{0,2},{1,3},{2,0},{3,1},{4,6},{5,7},{6,4},{7,5},{8,10},{9,11},{10,... | collective-permute-start | bytes 1179656 | tf_op jit(solution)/shard_map/ppermute | solution.py:712
  37.5 13.9 %collective-permute-start.8 = (bf16[192,1408]{1,0:T(8,128)(2,1)S(1)}, bf16[192,1408]{1,0:T(8,128)(2,1)S(1)}, u32[]{:S(2)}, u32[]{:S(2)}) collective-permute-start(bf16[192,1408]{1,0:T(8,128)(2,1)S(1)} %pad_maximum_fusion.3), channel_id=1, source_target_pairs={{0,1},{1,0},{2,3},{3,2},{4,5},{5,4},{6,7},{7,6},{8,24},{9,25},{10,... | collective-permute-start | bytes 1622024 | tf_op jit(solution)/shard_map/ppermute | solution.py:712
  51.6 12.0 %collective-permute-start.11 = (bf16[384,1408]{1,0:T(8,128)(2,1)S(1)}, bf16[384,1408]{1,0:T(8,128)(2,1)S(1)}, u32[]{:S(2)}, u32[]{:S(2)}) collective-permute-start(bf16[384,1408]{1,0:T(8,128)(2,1)S(1)} %pad_maximum_fusion.2.table_ref), channel_id=1, source_target_pairs={{0,8},{1,9},{2,10},{3,11},{4,12},{5,13},{6,14},{7,15},{8,0},{9,1},... | collective-permute-start | bytes 3244040 | tf_op jit(solution)/shard_map/ppermute | solution.py:712
  51.7 9.4 %collective-permute-start.13 = (bf16[2,48,1536]{2,1,0:T(8,128)(2,1)S(1)}, bf16[2,48,1536]{2,1,0:T(8,128)(2,1)S(1)}, u32[]{:S(2)}, u32[]{:S(2)}) collective-permute-start(bf16[2,48,1536]{2,1,0:T(8,128)(2,1)S(1)} %maximum_select_fusion.3), channel_id=1, source_target_pairs={{0,2},{1,3},{2,0},{3,1},{4,6},{5,7},{6,4},{7,5},{8,10},{9,11},{10,... | collective-permute-start | bytes 884744 | tf_op jit(solution)/shard_map/ppermute | solution.py:712
  52.0 16.3 %collective-permute-start.20 = (bf16[384,768]{1,0:T(8,128)(2,1)S(1)}, bf16[384,768]{1,0:T(8,128)(2,1)S(1)}, u32[]{:S(2)}, u32[]{:S(2)}) collective-permute-start(bf16[384,768]{1,0:T(8,128)(2,1)S(1)} %bitcast.42), channel_id=1, source_target_pairs={{0,16},{1,17},{2,18},{3,19},{4,20},{5,21},{6,22},{7,23},{8,9},{9,8... | collective-permute-start | bytes 1769480 | tf_op jit(solution)/shard_map/ppermute | solution.py:712
  61.2 11.4 %collective-permute-start.14 = (bf16[192,1536]{1,0:T(8,128)(2,1)S(1)}, bf16[192,1536]{1,0:T(8,128)(2,1)S(1)}, u32[]{:S(2)}, u32[]{:S(2)}) collective-permute-start(bf16[192,1536]{1,0:T(8,128)(2,1)S(1)} %bitcast.44), channel_id=1, source_target_pairs={{0,16},{1,17},{2,18},{3,19},{4,20},{5,21},{6,22},{7,23},{8,9},{9,8... | collective-permute-start | bytes 1769480 | tf_op jit(solution)/shard_map/ppermute | solution.py:712
  68.2 11.0 %collective-permute-start.12 = (bf16[512,384]{1,0:T(8,128)(2,1)}, bf16[512,384]{1,0:T(8,128)(2,1)S(1)}, u32[]{:S(2)}, u32[]{:S(2)}) collective-permute-start(bf16[512,384]{1,0:T(8,128)(2,1)} %get-tuple-element.139.kv_ref), channel_id=1, source_target_pairs={{0,1},{1,0},{2,3},{3,2},{4,5},{5,4},{6,7},{7,6},{8,9},{9,8},{10,11... | collective-permute-start | bytes 1179656 | tf_op jit(solution)/shard_map/ppermute | solution.py:712
  68.4 30.7 %collective-permute-start.21 = (bf16[768,768]{1,0:T(8,128)(2,1)S(1)}, bf16[768,768]{1,0:T(8,128)(2,1)S(1)}, u32[]{:S(2)}, u32[]{:S(2)}) collective-permute-start(bf16[768,768]{1,0:T(8,128)(2,1)S(1)} %pad_maximum_fusion.1.down_near_hbm), channel_id=1, source_target_pairs={{0,1},{1,0},{2,3},{3,2},{4,5},{5,4},{6,7},{7,6},{8,24},{9,25},{10,... | collective-permute-start | bytes 3538952 | tf_op jit(solution)/shard_map/ppermute | solution.py:712
  79.3 24.4 %collective-permute-start.19 = (bf16[384,1536]{1,0:T(8,128)(2,1)S(1)}, bf16[384,1536]{1,0:T(8,128)(2,1)}, u32[]{:S(2)}, u32[]{:S(2)}) collective-permute-start(bf16[384,1536]{1,0:T(8,128)(2,1)S(1)} %pad_maximum_fusion.in_near_hbm), channel_id=1, source_target_pairs={{0,1},{1,0},{2,3},{3,2},{4,5},{5,4},{6,7},{7,6},{8,24},{9,25},{10,... | collective-permute-start | bytes 3538952 | tf_op jit(solution)/shard_map/ppermute | solution.py:712
  86.1 7.7 %collective-permute-start.15 = (bf16[128,192]{1,0:T(8,128)(2,1)}, bf16[128,192]{1,0:T(8,128)(2,1)S(1)}, u32[]{:S(2)}, u32[]{:S(2)}) collective-permute-start(bf16[128,192]{1,0:T(8,128)(2,1)} %get-tuple-element.143.refs_5_), channel_id=1, source_target_pairs={{0,4},{1,5},{2,6},{3,7},{4,0},{5,1},{6,2},{7,3},{8,12},{9,13},{10,... | collective-permute-start | bytes 147464 | tf_op jit(solution)/shard_map/ppermute | solution.py:731
  125.7 26.2 %collective-permute-start.27 = (bf16[384,1536]{1,0:T(8,128)(2,1)S(1)}, bf16[384,1536]{1,0:T(8,128)(2,1)S(1)}, u32[]{:S(2)}, u32[]{:S(2)}) collective-permute-start(bf16[384,1536]{1,0:T(8,128)(2,1)S(1)} %convolution_convert_fusion), channel_id=1, source_target_pairs={{0,1},{1,0},{2,3},{3,2},{4,5},{5,4},{6,7},{7,6},{8,24},{9,25},{10,... | collective-permute-start | bytes 3538952 | tf_op jit(solution)/shard_map/ppermute | solution.py:712
  126.5 33.7 %collective-permute-start.29 = (bf16[768,768]{1,0:T(8,128)(2,1)S(1)}, bf16[768,768]{1,0:T(8,128)(2,1)S(1)}, u32[]{:S(2)}, u32[]{:S(2)}) collective-permute-start(bf16[768,768]{1,0:T(8,128)(2,1)S(1)} %convolution_convert_fusion.2), channel_id=1, source_target_pairs={{0,1},{1,0},{2,3},{3,2},{4,5},{5,4},{6,7},{7,6},{8,24},{9,25},{10,... | collective-permute-start | bytes 3538952 | tf_op jit(solution)/shard_map/ppermute | solution.py:712
  132.8 7.7 %collective-permute-start.24 = (bf16[128,192]{1,0:T(8,128)(2,1)}, bf16[128,192]{1,0:T(8,128)(2,1)S(1)}, u32[]{:S(2)}, u32[]{:S(2)}) collective-permute-start(bf16[128,192]{1,0:T(8,128)(2,1)} %get-tuple-element.167), channel_id=1, source_target_pairs={{0,4},{1,5},{2,6},{3,7},{4,0},{5,1},{6,2},{7,3},{8,12},{9,13},{10,... | collective-permute-start | bytes 147464 | tf_op jit(solution)/shard_map/ppermute | solution.py:731
  150.3 15.4 %collective-permute-start.28 = (bf16[512,384]{1,0:T(8,128)(2,1)}, bf16[512,384]{1,0:T(8,128)(2,1)}, u32[]{:S(2)}, u32[]{:S(2)}) collective-permute-start(bf16[512,384]{1,0:T(8,128)(2,1)} %get-tuple-element.175), channel_id=1, source_target_pairs={{0,1},{1,0},{2,3},{3,2},{4,5},{5,4},{6,7},{7,6},{8,9},{9,8},{10,11... | collective-permute-start | bytes 1179656 | tf_op jit(solution)/shard_map/ppermute | solution.py:712
  153.3 18.0 %collective-permute-start.31 = (bf16[192,1536]{1,0:T(8,128)(2,1)}, bf16[192,1536]{1,0:T(8,128)(2,1)}, u32[]{:S(2)}, u32[]{:S(2)}) collective-permute-start(bf16[192,1536]{1,0:T(8,128)(2,1)} %slice.181), channel_id=1, source_target_pairs={{0,16},{1,17},{2,18},{3,19},{4,20},{5,21},{6,22},{7,23},{8,9},{9,8... | collective-permute-start | bytes 1769480 | tf_op jit(solution)/shard_map/ppermute | solution.py:712
  160.6 11.9 %collective-permute-start.30 = (bf16[384,768]{1,0:T(8,128)(2,1)S(1)}, bf16[384,768]{1,0:T(8,128)(2,1)S(1)}, u32[]{:S(2)}, u32[]{:S(2)}) collective-permute-start(bf16[384,768]{1,0:T(8,128)(2,1)S(1)} %slice.182), channel_id=1, source_target_pairs={{0,16},{1,17},{2,18},{3,19},{4,20},{5,21},{6,22},{7,23},{8,9},{9,8... | collective-permute-start | bytes 1769480 | tf_op jit(solution)/shard_map/ppermute | solution.py:712
  171.3 8.6 %collective-permute-start.37 = (bf16[256,768]{1,0:T(8,128)(2,1)}, bf16[256,768]{1,0:T(8,128)(2,1)}, u32[]{:S(2)}, u32[]{:S(2)}) collective-permute-start(bf16[256,768]{1,0:T(8,128)(2,1)} %get-tuple-element.194), channel_id=1, source_target_pairs={{0,2},{1,3},{2,0},{3,1},{4,6},{5,7},{6,4},{7,5},{8,10},{9,11},{10,... | collective-permute-start | bytes 1179656 | tf_op jit(solution)/shard_map/ppermute | solution.py:712
  172.6 16.3 %collective-permute-start.32 = (bf16[384,1408]{1,0:T(8,128)(2,1)}, bf16[384,1408]{1,0:T(8,128)(2,1)S(1)}, u32[]{:S(2)}, u32[]{:S(2)}) collective-permute-start(bf16[384,1408]{1,0:T(8,128)(2,1)} %get-tuple-element.189), channel_id=1, source_target_pairs={{0,8},{1,9},{2,10},{3,11},{4,12},{5,13},{6,14},{7,15},{8,0},{9,1},... | collective-permute-start | bytes 3244040 | tf_op jit(solution)/shard_map/ppermute | solution.py:712
  176.1 12.6 %collective-permute-start.43 = (bf16[192,768]{1,0:T(8,128)(2,1)S(1)}, bf16[192,768]{1,0:T(8,128)(2,1)S(1)}, u32[]{:S(2)}, u32[]{:S(2)}) collective-permute-start(bf16[192,768]{1,0:T(8,128)(2,1)S(1)} %dynamic-slice_convert_fusion), channel_id=1, source_target_pairs={{0,2},{1,3},{2,0},{3,1},{4,6},{5,7},{6,4},{7,5},{8,10},{9,11},{10,... | collective-permute-start | bytes 884744 | tf_op jit(solution)/shard_map/ppermute | solution.py:712
  181.2 32.7 %collective-permute-start.38 = (bf16[128,768]{1,0:T(8,128)(2,1)S(1)}, bf16[128,768]{1,0:T(8,128)(2,1)S(1)}, u32[]{:S(2)}, u32[]{:S(2)}) collective-permute-start(bf16[128,768]{1,0:T(8,128)(2,1)S(1)} %slice.185), channel_id=1, source_target_pairs={{0,4},{1,5},{2,6},{3,7},{4,0},{5,1},{6,2},{7,3},{8,12},{9,13},{10,... | collective-permute-start | bytes 589832 | tf_op jit(solution)/shard_map/ppermute | solution.py:712
  181.4 18.0 %collective-permute-start.35 = (bf16[96,1536]{1,0:T(8,128)(2,1)S(1)}, bf16[96,1536]{1,0:T(8,128)(2,1)S(1)}, u32[]{:S(2)}, u32[]{:S(2)}) collective-permute-start(bf16[96,1536]{1,0:T(8,128)(2,1)S(1)} %dynamic-slice_convert_fusion.1), channel_id=1, source_target_pairs={{0,2},{1,3},{2,0},{3,1},{4,6},{5,7},{6,4},{7,5},{8,10},{9,11},{10,... | collective-permute-start | bytes 884744 | tf_op jit(solution)/shard_map/ppermute | solution.py:712
  188.7 19.2 %collective-permute-start.44 = (bf16[96,768]{1,0:T(8,128)(2,1)S(1)}, bf16[96,768]{1,0:T(8,128)(2,1)S(1)}, u32[]{:S(2)}, u32[]{:S(2)}) collective-permute-start(bf16[96,768]{1,0:T(8,128)(2,1)S(1)} %dynamic-slice_convert_fusion.2), channel_id=1, source_target_pairs={{0,4},{1,5},{2,6},{3,7},{4,0},{5,1},{6,2},{7,3},{8,12},{9,13},{10,... | collective-permute-start | bytes 442376 | tf_op jit(solution)/shard_map/ppermute | solution.py:712
  189.3 10.2 %collective-permute-start.33 = (bf16[192,1408]{1,0:T(8,128)(2,1)S(1)}, bf16[192,1408]{1,0:T(8,128)(2,1)S(1)}, u32[]{:S(2)}, u32[]{:S(2)}) collective-permute-start(bf16[192,1408]{1,0:T(8,128)(2,1)S(1)} %slice.183), channel_id=1, source_target_pairs={{0,1},{1,0},{2,3},{3,2},{4,5},{5,4},{6,7},{7,6},{8,24},{9,25},{10,... | collective-permute-start | bytes 1622024 | tf_op jit(solution)/shard_map/ppermute | solution.py:712
  199.4 8.5 %collective-permute-start.36 = (bf16[48,1536]{1,0:T(8,128)(2,1)S(1)}, bf16[48,1536]{1,0:T(8,128)(2,1)S(1)}, u32[]{:S(2)}, u32[]{:S(2)}) collective-permute-start(bf16[48,1536]{1,0:T(8,128)(2,1)S(1)} %dynamic-slice_convert_fusion.3), channel_id=1, source_target_pairs={{0,4},{1,5},{2,6},{3,7},{4,0},{5,1},{6,2},{7,3},{8,12},{9,13},{10,... | collective-permute-start | bytes 442376 | tf_op jit(solution)/shard_map/ppermute | solution.py:712
  199.7 9.0 %collective-permute-start.34 = (bf16[96,1408]{1,0:T(8,128)(2,1)S(1)}, bf16[96,1408]{1,0:T(8,128)(2,1)S(1)}, u32[]{:S(2)}, u32[]{:S(2)}) collective-permute-start(bf16[96,1408]{1,0:T(8,128)(2,1)S(1)} %slice.184), channel_id=1, source_target_pairs={{0,16},{1,17},{2,18},{3,19},{4,20},{5,21},{6,22},{7,23},{8,9},{9,8... | collective-permute-start | bytes 811016 | tf_op jit(solution)/shard_map/ppermute | solution.py:712
  (41 other events, 225.5 us)

commit v5 on v4

--- a/solution.py
+++ b/solution.py
@@ -639,16 +639,18 @@
 
 
 def units_kernel(unit_ids, place_ref, keep_ref, got_ref, out_ref):
-    core = place_ref[0]
-    keep, got = keep_ref[...], got_ref[...].astype(f32)
-    sources = [jnp.where(core == 0, keep, got), jnp.where(core == 0, got, keep)]
     count = 2 * len(unit_ids[0])
     each = out_ref.shape[1] // count
-    blocks = {}
-    for c, ids in enumerate(unit_ids):
-        for slot, device in enumerate(ids):
-            blocks[int(device)] = sources[c][:, slot * each : (slot + 1) * each]
-    out_ref[...] = jnp.concatenate([blocks[i] for i in range(count)], axis=1)
+    for core in range(2):
+
+        @pl.when(place_ref[0] == core)
+        def _(core=core):
+            keep, got = keep_ref[...], got_ref[...].astype(f32)
+            blocks = {}
+            for ids, source in ((unit_ids[core], keep), (unit_ids[1 - core], got)):
+                for slot, device in enumerate(ids):
+                    blocks[int(device)] = source[:, slot * each : (slot + 1) * each]
+            out_ref[...] = jnp.concatenate([blocks[i] for i in range(count)], axis=1)
 
 
 class Grid:
@@ -1023,9 +1025,7 @@
         + [pltpu.SemaphoreType.DMA((5,))],
     )
     first_got = chip_swap(first_send)
-    first_got, d_hidden, d_second = tie(first_got, d_hidden, d_second)
-    down_send = dot(active[:, width:], d_second, 0, 0).astype(bf16)
-    down_keep = dot(active[:, :width], d_second, 0, 0).astype(bf16)
+    first_got, d_hidden = tie(first_got, d_hidden)
     d_hidden, ffn_sums = outer_swap(d_hidden), outer_swap(ffn_sums)
     in_send = dot(mixed[:, half:], d_hidden, 0, 0).astype(bf16)
     in_keep = dot(mixed[:, :half], d_hidden, 0, 0).astype(bf16)
@@ -1042,6 +1042,9 @@
         name="branch_backward",
     )
     got_d_att = line_swap(grid, d_pieces[1:])
+    d_branch, d_second = tie(d_branch, d_second)
+    down_send = dot(active[:, width:], d_second, 0, 0).astype(bf16)
+    down_keep = dot(active[:, :width], d_second, 0, 0).astype(bf16)
 
     def far_sum(keep, send):
         return keep.astype(f32) + swap(grid, send, grid.plane_bits[-1]).astype(f32)
@@ -1136,6 +1139,7 @@
         grid, [total[k * rows_each : (k + 1) * rows_each].astype(bf16) for k in range(1, groups)]
     )
     input_grad = d_one + back
+    own_total, sum_in = tie(total[:rows_each], sum_in)
     sum_qkv, sum_out, sum_vec, sum_ffn, sum_gain, sum_shift = call(
         functools.partial(finish_kernel, small_each),
         [
@@ -1147,7 +1151,7 @@
             ((2, rows_each), f32),
         ],
         place,
-        total[:rows_each],
+        own_total,
         *got_total,
         name="finish",
     )

time: 224 us -> 222 us (level)
  waiting for transfers between devices: 67.5 us -> 62.8 us
    ppermute x12, waiting for transfers between devices: 8.28 us -> 5.59 us  [line_swap(): lax.ppermute(piece, BOTH, grid.cross(crossed(k + 1)))]
    unnamed x57 -> x65, local copies, waits for them, and re-layouts: 5.33 us -> 5.8 us
  transfers between devices with their start and end apart: 45 -> 45, of which waited for: 21 -> 18; matrix products, arithmetic and copies ran while one was open for 13% -> 14% of each run, Pallas kernels for 21% -> 21%
where the time goes in v5:
time: 222 us; the launch traced here: 221 us
  Pallas kernels  63.7 us (29%)
  waiting for transfers between devices  62.8 us (28%)
  starting transfers between devices  54.5 us (25%)
  other arithmetic  20.9 us (9%)
  local copies, waits for them, and re-layouts  11.6 us (5%)
  matrix products  5.89 us (3%)
    ppermute x33, waiting for transfers between devices, swap(): return lax.ppermute(held, BOTH, grid.flip(bits))  57.2 us
    pallas_call x11, Pallas kernels, call(): pl.pallas_call(body, in_specs=specs, out_specs=[pl.BlockSpec(memory_space...  49.1 us
    ppermute x33, starting transfers between devices, swap(): return lax.ppermute(held, BOTH, grid.flip(bits))  36.8 us
    ppermute x12, starting transfers between devices, line_swap(): lax.ppermute(piece, BOTH, grid.cross(crossed(k + 1)))  17.7 us
    pallas_call x1, Pallas kernels, attention_backward(): pl.pallas_call(backward_kernel, grid=(rows // tile,), in_specs=[pl.BlockS...  8.5 us
    pallas_call x1, Pallas kernels, attention_forward(): pl.pallas_call(forward_kernel, grid=(rows // tile,), in_specs=[pl.BlockSp...  6.12 us
    dot_general x5, matrix products, dot(): lax.dot_general(left, right, (((left_dim,), (right_dim,)), ((), ())), pre...  5.89 us
    unnamed x65, local copies, waits for them, and re-layouts  5.8 us
  transfers between devices with their start and end apart: 45, of which 18 were waited for; matrix products, arithmetic and copies ran while one was open for 14% of the time, Pallas kernels for 21%

profile of v5, /device:TPU:0, one launch (start us, length us, event | category | flops | bytes accessed | tf_op | source)
XLA Modules:
  0.0 220.6 jit_solution(11061064645917750584)
XLA Ops:
  0.7 4.1 %collective-permute-start.4 = (bf16[1,96,768]{2,1,0:T(8,128)(2,1)}, bf16[1,96,768]{2,1,0:T(8,128)(2,1)S(1)}, u32[]{:S(2)}, u32[]{:S(2)}) collective-permute-start(bf16[1,96,768]{2,1,0:T(8,128)(2,1)} %bitcast.52), channel_id=1, source_target_pairs={{0,4},{1,5},{2,6},{3,7},{4,0},{5,1},{6,2},{7,3},{8,12},{9,13},{10,... | collective-permute-start | bytes 442376 | tf_op jit(solution)/shard_map/ppermute | solution.py:714
  5.3 2.4 %pack_weights.1 = (bf16[24,1408]{1,0:T(8,128)(2,1)}, bf16[24,1408]{1,0:T(8,128)(2,1)}, bf16[24,1408]{1,0:T(8,128)(2,1)}, bf16[24,1408]{1,0:T(8,128)(2,1)}, bf16[...) custom-call(s32[2]{0:T(128)} %pad_add_fusion.2.place_ref, bf16[24,2304]{1,0:T(8,128)(2,1)} %qkv_ref.1, ...), custom_call_target="tpu_custom_call" | custom-call | flops 100000000 | bytes 688712 | tf_op jit(solution)/shard_map/pack_weights/pallas_call | solution.py:55
  9.7 2.5 %collective-permute-start.2 = (bf16[24,1408]{1,0:T(8,128)(2,1)}, bf16[24,1408]{1,0:T(8,128)(2,1)S(1)}, u32[]{:S(2)}, u32[]{:S(2)}) collective-permute-start(bf16[24,1408]{1,0:T(8,128)(2,1)} %get-tuple-element.113), channel_id=1, source_target_pairs={{0,6},{1,7},{2,4},{3,5},{4,2},{5,3},{6,0},{7,1},{8,14},{9,15},{10,... | collective-permute-start | bytes 202760 | tf_op jit(solution)/shard_map/ppermute | solution.py:733
  19.5 3.3 %collective-permute-start.6 = (bf16[128,768]{1,0:T(8,128)(2,1)S(1)}, bf16[128,768]{1,0:T(8,128)(2,1)S(1)}, u32[]{:S(2)}, u32[]{:S(2)}) collective-permute-start(bf16[128,768]{1,0:T(8,128)(2,1)S(1)} %bitcast.48), channel_id=1, source_target_pairs={{0,4},{1,5},{2,6},{3,7},{4,0},{5,1},{6,2},{7,3},{8,12},{9,13},{10,... | collective-permute-start | bytes 589832 | tf_op jit(solution)/shard_map/ppermute | solution.py:714
  27.0 3.2 %and_select_fusion.b_ref = f32[512,1024]{1,0:T(8,128)} fusion(s32[1024]{0:T(1024)S(1)} %bitcast.54, s32[1024]{0:T(1024)S(1)} %get-tuple-element.234, s32[512]{0:T(512)S(1)} %slice_bitcast_fusion, s32[512]{0:T(512)S(1)} %get-tuple-element.211, s32[512]{0:T(512)S(1)} %get-tuple-element.210, s32[512]{0:T(512)S(1)} %bitcast.56, s32[512]{0:T(512)S(1)} %bitcast.57, ...), kind=kLoop, calls=%fused_computation.13 | loop fusion | flops 8388608 | bytes 2121728 | tf_op jit(solution)/shard_map/jit(_where)/select_n | solution.py:902
  32.4 4.1 %collective-permute-done.7 = bf16[2,96,768]{2,1,0:T(8,128)(2,1)S(1)} collective-permute-done((bf16[2,96,768]{2,1,0:T(8,128)(2,1)S(1)}, bf16[2,96,768]{2,1,0:T(8,128)(2,1)S(1)}, u32[]{:S(2)}, u32[]{:S(2)}) %collective-permute-start.7) | collective-permute-done | bytes 294944 | tf_op jit(solution)/shard_map/ppermute | solution.py:714
  39.4 5.2 %collective-permute-done.9 = bf16[1,48,1536]{2,1,0:T(8,128)(2,1)S(1)} collective-permute-done((bf16[1,48,1536]{2,1,0:T(8,128)(2,1)S(1)}, bf16[1,48,1536]{2,1,0:T(8,128)(2,1)S(1)}, u32[]{:S(2)}, u32[]{:S(2)}) %collective-permute-start.9) | collective-permute-done | bytes 147488 | tf_op jit(solution)/shard_map/ppermute | solution.py:714
  44.7 5.0 %collective-permute-done.10 = bf16[256,768]{1,0:T(8,128)(2,1)S(1)} collective-permute-done((bf16[256,768]{1,0:T(8,128)(2,1)S(1)}, bf16[256,768]{1,0:T(8,128)(2,1)S(1)}, u32[]{:S(2)}, u32[]{:S(2)}) %collective-permute-start.10) | collective-permute-done | bytes 393248 | tf_op jit(solution)/shard_map/ppermute | solution.py:714
  52.0 2.4 %collective-permute-start.20 = (bf16[384,768]{1,0:T(8,128)(2,1)S(1)}, bf16[384,768]{1,0:T(8,128)(2,1)S(1)}, u32[]{:S(2)}, u32[]{:S(2)}) collective-permute-start(bf16[384,768]{1,0:T(8,128)(2,1)S(1)} %bitcast.42), channel_id=1, source_target_pairs={{0,16},{1,17},{2,18},{3,19},{4,20},{5,21},{6,22},{7,23},{8,9},{9,8... | collective-permute-start | bytes 1769480 | tf_op jit(solution)/shard_map/ppermute | solution.py:714
  54.3 6.7 %collective-permute-done.13 = bf16[2,48,1536]{2,1,0:T(8,128)(2,1)S(1)} collective-permute-done((bf16[2,48,1536]{2,1,0:T(8,128)(2,1)S(1)}, bf16[2,48,1536]{2,1,0:T(8,128)(2,1)S(1)}, u32[]{:S(2)}, u32[]{:S(2)}) %collective-permute-start.13) | collective-permute-done | bytes 294944 | tf_op jit(solution)/shard_map/ppermute | solution.py:714
  61.2 2.4 %collective-permute-start.14 = (bf16[192,1536]{1,0:T(8,128)(2,1)S(1)}, bf16[192,1536]{1,0:T(8,128)(2,1)S(1)}, u32[]{:S(2)}, u32[]{:S(2)}) collective-permute-start(bf16[192,1536]{1,0:T(8,128)(2,1)S(1)} %bitcast.44), channel_id=1, source_target_pairs={{0,16},{1,17},{2,18},{3,19},{4,20},{5,21},{6,22},{7,23},{8,9},{9,8... | collective-permute-start | bytes 1769480 | tf_op jit(solution)/shard_map/ppermute | solution.py:714
  64.6 3.6 %project.1 = (bf16[512,192]{1,0:T(8,128)(2,1)}, bf16[512,384]{1,0:T(8,128)(2,1)}) custom-call(bf16[512,768]{1,0:T(8,128)(2,1)} %fusion.5.x_ref, bf16[384,1408]{1,0:T(8,128)(2,1)} %copy-done.2, bf16[384,1408]{1,0:T(8,128)(2,1)} %copy-done.4, bf16[768,192]{1,0:T(8,128)(2,1)} %compare_convert_fusion.2.sel_ref), custom_call_target="tpu_custom_call" | custom-call | flops 100000000 | bytes 3244032 | tf_op jit(solution)/shard_map/project/pallas_call | solution.py:55
  72.6 6.6 %unfold_weights.1 = (bf16[768,576]{1,0:T(8,128)(2,1)}, bf16[768,768]{1,0:T(8,128)(2,1)}, f32[8,768]{1,0:T(8,128)}, f32[1,1536]{1,0:T(1,128)}) custom-call(bf16[384,1408]{1,0:T(8,128)(2,1)} %copy-done.2, bf16[384,1408]{1,0:T(8,128)(2,1)} %copy-done.4, bf16[768,768]{1,0:T(8,128)(2,1)} %get-tuple-element.134.near_ref, ...), custom_call_target="tpu_custom_call" | custom-call | flops 100000000 | bytes 6881280 | tf_op jit(solution)/shard_map/unfold_weights/pallas_call | solution.py:55
  80.0 6.1 %attention_forward.1 = (bf16[128,192]{1,0:T(8,128)(2,1)}, bf16[128,192]{1,0:T(8,128)(2,1)}, bf16[128,192]{1,0:T(8,128)(2,1)}, bf16[128,192]{1,0:T(8,128)(2,1)}, f32[512,128]{1,0:T(8,128)}) custom-call(bf16[512,192]{1,0:T(8,128)(2,1)} %get-tuple-element.130.q_ref, bf16[512,384]{1,0:T(8,128)(2,1)} %get-tuple-element.142.kv_ref, bf16[512,384]{1,0:T(8,128)(2,1)} %copy-done.22, ...), custom_call_target="tpu_custom_call" | custom-call | flops 1610612736 | bytes 2097152 | tf_op jit(solution)/shard_map/attention_forward/pallas_call | solution.py:287
  90.5 3.2 %collective-permute-done.15 = bf16[128,192]{1,0:T(8,128)(2,1)S(1)} collective-permute-done((bf16[128,192]{1,0:T(8,128)(2,1)}, bf16[128,192]{1,0:T(8,128)(2,1)S(1)}, u32[]{:S(2)}, u32[]{:S(2)}) %collective-permute-start.15) | collective-permute-done | bytes 49184 | tf_op jit(solution)/shard_map/ppermute | solution.py:733
  99.0 4.6 %collective-permute-done.19.in_far_hbm = bf16[384,1536]{1,0:T(8,128)(2,1)} collective-permute-done((bf16[384,1536]{1,0:T(8,128)(2,1)S(1)}, bf16[384,1536]{1,0:T(8,128)(2,1)}, u32[]{:S(2)}, u32[]{:S(2)}) %collective-permute-start.19) | collective-permute-done | bytes 1179680 | tf_op jit(solution)/shard_map/ppermute | solution.py:714
  103.6 7.9 %ffn_forward.1 = (f32[256,768]{1,0:T(8,128)}, f32[256,768]{1,0:T(8,128)}, f32[256,128]{1,0:T(8,128)}, bf16[256,768]{1,0:T(8,128)(2,1)}, f32[256,1536]{1,0:T(8,12...) custom-call(s32[2]{0:T(128)} %pad_add_fusion.1.flag_ref, ...), custom_call_target="tpu_custom_call" | custom-call | flops 100000000 | bytes 8165384 | tf_op jit(solution)/shard_map/ffn_forward/pallas_call | solution.py:55
  114.3 7.9 %ffn_backward.1 = (bf16[128,768]{1,0:T(8,128)(2,1)}, f32[128,768]{1,0:T(8,128)}, bf16[128,768]{1,0:T(8,128)(2,1)}, bf16[256,768]{1,0:T(8,128)(2,1)}, bf16[256,15...) custom-call(s32[2]{0:T(128)} %pad_add_fusion.1.flag_ref, f32[256,768]{1,0:T(8,128)} %get-tuple-element.155.part_ref, ...), custom_call_target="tpu_custom_call" | custom-call | flops 100000000 | bytes 10125320 | tf_op jit(solution)/shard_map/ffn_backward/pallas_call | solution.py:55
  127.4 3.1 %branch_backward.1 = (f32[128,768]{1,0:T(8,128)}, bf16[128,768]{1,0:T(8,128)(2,1)}, f32[8,768]{1,0:T(8,128)}, bf16[128,192]{1,0:T(8,128)(2,1)}, bf16[128,192]{1,...) custom-call(f32[128,768]{1,0:T(8,128)} %get-tuple-element.160.keep_ref, bf16[128,768]{1,0:T(8,128)(2,1)} %copy-done.15, ...), custom_call_target="tpu_custom_call" | custom-call | flops 100000000 | bytes 2252800 | tf_op jit(solution)/shard_map/branch_backward/pallas_call | solution.py:55
  135.0 2.3 %collective-permute-start.26 = (bf16[128,192]{1,0:T(8,128)(2,1)S(1)}, bf16[128,192]{1,0:T(8,128)(2,1)S(1)}, u32[]{:S(2)}, u32[]{:S(2)}) collective-permute-start(bf16[128,192]{1,0:T(8,128)(2,1)S(1)} %copy-done.26), channel_id=1, source_target_pairs={{0,6},{1,7},{2,4},{3,5},{4,2},{5,3},{6,0},{7,1},{8,14},{9,15},{10,... | collective-permute-start | bytes 147464 | tf_op jit(solution)/shard_map/ppermute | solution.py:733
  137.3 3.3 %branch_gradients.1.out_ref = bf16[768,768]{1,0:T(8,128)(2,1)} custom-call(bf16[128,768]{1,0:T(8,128)(2,1)} %pad_maximum_fusion.6.att_ref, bf16[128,768]{1,0:T(8,128)(2,1)} %get-tuple-element.169.branch_ref, bf16[768,768]{1,0:T(8,128)(2,1)} %get-tuple-element.135.line_ref), custom_call_target="tpu_custom_call" | custom-call | flops 100000000 | bytes 1572864 | tf_op jit(solution)/shard_map/branch_gradients/pallas_call | solution.py:55
  141.7 8.5 %attention_backward.1 = (bf16[512,192]{1,0:T(8,128)(2,1)}, f32[512,384]{1,0:T(8,128)}, bf16[512,384]{1,0:T(8,128)(2,1)}) custom-call(bf16[512,192]{1,0:T(8,128)(2,1)} %get-tuple-element.130.q_ref, bf16[512,384]{1,0:T(8,128)(2,1)} %get-tuple-element.142.kv_ref, bf16[512,384]{1,0:T(8,128)(2,1)} %copy-done.22, f32[512,1024]{1,0:T(8,128)} %and_select_fusion.b_ref, ...), custom_call_target="tpu_custom_call" | custom-call | flops 3019898880 | bytes 2097152 | tf_op jit(solution)/shard_map/attention_backward/pallas_call | solution.py:314
  156.3 4.9 %query_gradients.1.last_ref = f32[768,256]{1,0:T(8,128)} custom-call(bf16[512,768]{1,0:T(8,128)(2,1)} %fusion.5.x_ref, bf16[512,192]{1,0:T(8,128)(2,1)} %get-tuple-element.180.dq_ref, bf16[768,192]{1,0:T(8,128)(2,1)} %compare_convert_fusion.2.sel_ref, f32[8,768]{1,0:T(8,128)} %get-tuple-element.183.sums_ref, f32[8,768]{1,0:T(8,128)} %get-tuple-element.184.sums_two_ref, ...), custom_call_target="tpu_custom_call" | custom-call | flops 100000000 | bytes 4872192 | tf_op jit(solution)/shard_map/query_gradients/pallas_call | solution.py:55
  162.1 3.3 %collective-permute-done.28.got_ref = bf16[512,384]{1,0:T(8,128)(2,1)} collective-permute-done((bf16[512,384]{1,0:T(8,128)(2,1)}, bf16[512,384]{1,0:T(8,128)(2,1)}, u32[]{:S(2)}, u32[]{:S(2)}) %collective-permute-start.28) | collective-permute-done | bytes 393248 | tf_op jit(solution)/shard_map/ppermute | solution.py:714
  165.4 5.6 %pair_gradients.1 = (bf16[384,1408]{1,0:T(8,128)(2,1)}, bf16[384,1408]{1,0:T(8,128)(2,1)}, f32[256,768]{1,0:T(8,128)}, bf16[256,768]{1,0:T(8,128)(2,1)}) custom-call(bf16[512,768]{1,0:T(8,128)(2,1)} %fusion.5.x_ref, f32[512,384]{1,0:T(8,128)} %get-tuple-element.178.own_ref, bf16[512,384]{1,0:T(8,128)(2,1)} %collective-permute-done.28.got_ref, ...), custom_call_target="tpu_custom_call" | custom-call | flops 100000000 | bytes 5308416 | tf_op jit(solution)/shard_map/pair_gradients/pallas_call | solution.py:55
  172.3 3.7 %collective-permute-start.32 = (bf16[384,1408]{1,0:T(8,128)(2,1)}, bf16[384,1408]{1,0:T(8,128)(2,1)S(1)}, u32[]{:S(2)}, u32[]{:S(2)}) collective-permute-start(bf16[384,1408]{1,0:T(8,128)(2,1)} %get-tuple-element.193), channel_id=1, source_target_pairs={{0,8},{1,9},{2,10},{3,11},{4,12},{5,13},{6,14},{7,15},{8,0},{9,1},... | collective-permute-start | bytes 3244040 | tf_op jit(solution)/shard_map/ppermute | solution.py:714
  176.4 2.8 %collective-permute-done.37 = bf16[256,768]{1,0:T(8,128)(2,1)} collective-permute-done((bf16[256,768]{1,0:T(8,128)(2,1)}, bf16[256,768]{1,0:T(8,128)(2,1)}, u32[]{:S(2)}, u32[]{:S(2)}) %collective-permute-start.37) | collective-permute-done | bytes 393248 | tf_op jit(solution)/shard_map/ppermute | solution.py:714
  182.7 6.2 %collective-permute-done.43 = bf16[192,768]{1,0:T(8,128)(2,1)S(1)} collective-permute-done((bf16[192,768]{1,0:T(8,128)(2,1)S(1)}, bf16[192,768]{1,0:T(8,128)(2,1)S(1)}, u32[]{:S(2)}, u32[]{:S(2)}) %collective-permute-start.43) | collective-permute-done | bytes 294944 | tf_op jit(solution)/shard_map/ppermute | solution.py:714
  191.0 8.0 %collective-permute-done.35 = bf16[96,1536]{1,0:T(8,128)(2,1)S(1)} collective-permute-done((bf16[96,1536]{1,0:T(8,128)(2,1)S(1)}, bf16[96,1536]{1,0:T(8,128)(2,1)S(1)}, u32[]{:S(2)}, u32[]{:S(2)}) %collective-permute-start.35) | collective-permute-done | bytes 294944 | tf_op jit(solution)/shard_map/ppermute | solution.py:714
  199.3 3.6 %collective-permute-start.34 = (bf16[96,1408]{1,0:T(8,128)(2,1)S(1)}, bf16[96,1408]{1,0:T(8,128)(2,1)S(1)}, u32[]{:S(2)}, u32[]{:S(2)}) collective-permute-start(bf16[96,1408]{1,0:T(8,128)(2,1)S(1)} %slice.184), channel_id=1, source_target_pairs={{0,16},{1,17},{2,18},{3,19},{4,20},{5,21},{6,22},{7,23},{8,9},{9,8... | collective-permute-start | bytes 811016 | tf_op jit(solution)/shard_map/ppermute | solution.py:714
  202.9 4.4 %collective-permute-done.36 = bf16[48,1536]{1,0:T(8,128)(2,1)S(1)} collective-permute-done((bf16[48,1536]{1,0:T(8,128)(2,1)S(1)}, bf16[48,1536]{1,0:T(8,128)(2,1)S(1)}, u32[]{:S(2)}, u32[]{:S(2)}) %collective-permute-start.36) | collective-permute-done | bytes 147488 | tf_op jit(solution)/shard_map/ppermute | solution.py:714
  208.3 2.3 %collective-permute-start.42 = (bf16[24,1408]{1,0:T(8,128)(2,1)S(1)}, bf16[24,1408]{1,0:T(8,128)(2,1)S(1)}, u32[]{:S(2)}, u32[]{:S(2)}) collective-permute-start(bf16[24,1408]{1,0:T(8,128)(2,1)S(1)} %get-tuple-element.216), channel_id=1, source_target_pairs={{0,6},{1,7},{2,4},{3,5},{4,2},{5,3},{6,0},{7,1},{8,14},{9,15},{10,... | collective-permute-start | bytes 202760 | tf_op jit(solution)/shard_map/ppermute | solution.py:733
  (229 shorter events, 76.1 us)
Async XLA Ops:
  0.7 17.5 %collective-permute-start.4 = (bf16[1,96,768]{2,1,0:T(8,128)(2,1)}, bf16[1,96,768]{2,1,0:T(8,128)(2,1)S(1)}, u32[]{:S(2)}, u32[]{:S(2)}) collective-permute-start(bf16[1,96,768]{2,1,0:T(8,128)(2,1)} %bitcast.52), channel_id=1, source_target_pairs={{0,4},{1,5},{2,6},{3,7},{4,0},{5,1},{6,2},{7,3},{8,12},{9,13},{10,... | collective-permute-start | bytes 442376 | tf_op jit(solution)/shard_map/ppermute | solution.py:714
  7.8 9.4 %collective-permute-start = (bf16[24,1408]{1,0:T(8,128)(2,1)}, bf16[24,1408]{1,0:T(8,128)(2,1)S(1)}, u32[]{:S(2)}, u32[]{:S(2)}) collective-permute-start(bf16[24,1408]{1,0:T(8,128)(2,1)} %get-tuple-element.111), channel_id=1, source_target_pairs={{0,4},{1,5},{2,6},{3,7},{4,0},{5,1},{6,2},{7,3},{8,12},{9,13},{10,... | collective-permute-start | bytes 202760 | tf_op jit(solution)/shard_map/ppermute | solution.py:733
  7.9 9.3 %collective-permute-start.1 = (bf16[24,1408]{1,0:T(8,128)(2,1)}, bf16[24,1408]{1,0:T(8,128)(2,1)S(1)}, u32[]{:S(2)}, u32[]{:S(2)}) collective-permute-start(bf16[24,1408]{1,0:T(8,128)(2,1)} %get-tuple-element.112), channel_id=1, source_target_pairs={{0,2},{1,3},{2,0},{3,1},{4,6},{5,7},{6,4},{7,5},{8,10},{9,11},{10,... | collective-permute-start | bytes 202760 | tf_op jit(solution)/shard_map/ppermute | solution.py:733
  19.5 12.7 %collective-permute-start.6 = (bf16[128,768]{1,0:T(8,128)(2,1)S(1)}, bf16[128,768]{1,0:T(8,128)(2,1)S(1)}, u32[]{:S(2)}, u32[]{:S(2)}) collective-permute-start(bf16[128,768]{1,0:T(8,128)(2,1)S(1)} %bitcast.48), channel_id=1, source_target_pairs={{0,4},{1,5},{2,6},{3,7},{4,0},{5,1},{6,2},{7,3},{8,12},{9,13},{10,... | collective-permute-start | bytes 589832 | tf_op jit(solution)/shard_map/ppermute | solution.py:714
  22.8 9.5 %collective-permute-start.5 = (bf16[96,1408]{1,0:T(8,128)(2,1)S(1)}, bf16[96,1408]{1,0:T(8,128)(2,1)S(1)}, u32[]{:S(2)}, u32[]{:S(2)}) collective-permute-start(bf16[96,1408]{1,0:T(8,128)(2,1)S(1)} %pad_maximum_fusion.5), channel_id=1, source_target_pairs={{0,16},{1,17},{2,18},{3,19},{4,20},{5,21},{6,22},{7,23},{8,9},{9,8... | collective-permute-start | bytes 811016 | tf_op jit(solution)/shard_map/ppermute | solution.py:714
  24.3 12.2 %collective-permute-start.7 = (bf16[2,96,768]{2,1,0:T(8,128)(2,1)S(1)}, bf16[2,96,768]{2,1,0:T(8,128)(2,1)S(1)}, u32[]{:S(2)}, u32[]{:S(2)}) collective-permute-start(bf16[2,96,768]{2,1,0:T(8,128)(2,1)S(1)} %maximum_select_fusion.2), channel_id=1, source_target_pairs={{0,2},{1,3},{2,0},{3,1},{4,6},{5,7},{6,4},{7,5},{8,10},{9,11},{10,... | collective-permute-start | bytes 884744 | tf_op jit(solution)/shard_map/ppermute | solution.py:714
  36.6 8.0 %collective-permute-start.9 = (bf16[1,48,1536]{2,1,0:T(8,128)(2,1)S(1)}, bf16[1,48,1536]{2,1,0:T(8,128)(2,1)S(1)}, u32[]{:S(2)}, u32[]{:S(2)}) collective-permute-start(bf16[1,48,1536]{2,1,0:T(8,128)(2,1)S(1)} %maximum_bitcast_fusion), channel_id=1, source_target_pairs={{0,4},{1,5},{2,6},{3,7},{4,0},{5,1},{6,2},{7,3},{8,12},{9,13},{10,... | collective-permute-start | bytes 442376 | tf_op jit(solution)/shard_map/ppermute | solution.py:714
  36.7 13.0 %collective-permute-start.10 = (bf16[256,768]{1,0:T(8,128)(2,1)S(1)}, bf16[256,768]{1,0:T(8,128)(2,1)S(1)}, u32[]{:S(2)}, u32[]{:S(2)}) collective-permute-start(bf16[256,768]{1,0:T(8,128)(2,1)S(1)} %pad_maximum_fusion.4), channel_id=1, source_target_pairs={{0,2},{1,3},{2,0},{3,1},{4,6},{5,7},{6,4},{7,5},{8,10},{9,11},{10,... | collective-permute-start | bytes 1179656 | tf_op jit(solution)/shard_map/ppermute | solution.py:714
  37.5 13.9 %collective-permute-start.8 = (bf16[192,1408]{1,0:T(8,128)(2,1)S(1)}, bf16[192,1408]{1,0:T(8,128)(2,1)S(1)}, u32[]{:S(2)}, u32[]{:S(2)}) collective-permute-start(bf16[192,1408]{1,0:T(8,128)(2,1)S(1)} %pad_maximum_fusion.3), channel_id=1, source_target_pairs={{0,1},{1,0},{2,3},{3,2},{4,5},{5,4},{6,7},{7,6},{8,24},{9,25},{10,... | collective-permute-start | bytes 1622024 | tf_op jit(solution)/shard_map/ppermute | solution.py:714
  51.6 12.0 %collective-permute-start.11 = (bf16[384,1408]{1,0:T(8,128)(2,1)S(1)}, bf16[384,1408]{1,0:T(8,128)(2,1)S(1)}, u32[]{:S(2)}, u32[]{:S(2)}) collective-permute-start(bf16[384,1408]{1,0:T(8,128)(2,1)S(1)} %pad_maximum_fusion.2.table_ref), channel_id=1, source_target_pairs={{0,8},{1,9},{2,10},{3,11},{4,12},{5,13},{6,14},{7,15},{8,0},{9,1},... | collective-permute-start | bytes 3244040 | tf_op jit(solution)/shard_map/ppermute | solution.py:714
  51.7 9.4 %collective-permute-start.13 = (bf16[2,48,1536]{2,1,0:T(8,128)(2,1)S(1)}, bf16[2,48,1536]{2,1,0:T(8,128)(2,1)S(1)}, u32[]{:S(2)}, u32[]{:S(2)}) collective-permute-start(bf16[2,48,1536]{2,1,0:T(8,128)(2,1)S(1)} %maximum_select_fusion.3), channel_id=1, source_target_pairs={{0,2},{1,3},{2,0},{3,1},{4,6},{5,7},{6,4},{7,5},{8,10},{9,11},{10,... | collective-permute-start | bytes 884744 | tf_op jit(solution)/shard_map/ppermute | solution.py:714
  52.0 16.3 %collective-permute-start.20 = (bf16[384,768]{1,0:T(8,128)(2,1)S(1)}, bf16[384,768]{1,0:T(8,128)(2,1)S(1)}, u32[]{:S(2)}, u32[]{:S(2)}) collective-permute-start(bf16[384,768]{1,0:T(8,128)(2,1)S(1)} %bitcast.42), channel_id=1, source_target_pairs={{0,16},{1,17},{2,18},{3,19},{4,20},{5,21},{6,22},{7,23},{8,9},{9,8... | collective-permute-start | bytes 1769480 | tf_op jit(solution)/shard_map/ppermute | solution.py:714
  61.2 11.4 %collective-permute-start.14 = (bf16[192,1536]{1,0:T(8,128)(2,1)S(1)}, bf16[192,1536]{1,0:T(8,128)(2,1)S(1)}, u32[]{:S(2)}, u32[]{:S(2)}) collective-permute-start(bf16[192,1536]{1,0:T(8,128)(2,1)S(1)} %bitcast.44), channel_id=1, source_target_pairs={{0,16},{1,17},{2,18},{3,19},{4,20},{5,21},{6,22},{7,23},{8,9},{9,8... | collective-permute-start | bytes 1769480 | tf_op jit(solution)/shard_map/ppermute | solution.py:714
  68.2 11.0 %collective-permute-start.12 = (bf16[512,384]{1,0:T(8,128)(2,1)}, bf16[512,384]{1,0:T(8,128)(2,1)S(1)}, u32[]{:S(2)}, u32[]{:S(2)}) collective-permute-start(bf16[512,384]{1,0:T(8,128)(2,1)} %get-tuple-element.142.kv_ref), channel_id=1, source_target_pairs={{0,1},{1,0},{2,3},{3,2},{4,5},{5,4},{6,7},{7,6},{8,9},{9,8},{10,11... | collective-permute-start | bytes 1179656 | tf_op jit(solution)/shard_map/ppermute | solution.py:714
  68.4 30.7 %collective-permute-start.21 = (bf16[768,768]{1,0:T(8,128)(2,1)S(1)}, bf16[768,768]{1,0:T(8,128)(2,1)S(1)}, u32[]{:S(2)}, u32[]{:S(2)}) collective-permute-start(bf16[768,768]{1,0:T(8,128)(2,1)S(1)} %pad_maximum_fusion.1.down_near_hbm), channel_id=1, source_target_pairs={{0,1},{1,0},{2,3},{3,2},{4,5},{5,4},{6,7},{7,6},{8,24},{9,25},{10,... | collective-permute-start | bytes 3538952 | tf_op jit(solution)/shard_map/ppermute | solution.py:714
  79.3 24.4 %collective-permute-start.19 = (bf16[384,1536]{1,0:T(8,128)(2,1)S(1)}, bf16[384,1536]{1,0:T(8,128)(2,1)}, u32[]{:S(2)}, u32[]{:S(2)}) collective-permute-start(bf16[384,1536]{1,0:T(8,128)(2,1)S(1)} %pad_maximum_fusion.in_near_hbm), channel_id=1, source_target_pairs={{0,1},{1,0},{2,3},{3,2},{4,5},{5,4},{6,7},{7,6},{8,24},{9,25},{10,... | collective-permute-start | bytes 3538952 | tf_op jit(solution)/shard_map/ppermute | solution.py:714
  125.6 26.3 %collective-permute-start.27 = (bf16[384,1536]{1,0:T(8,128)(2,1)S(1)}, bf16[384,1536]{1,0:T(8,128)(2,1)S(1)}, u32[]{:S(2)}, u32[]{:S(2)}) collective-permute-start(bf16[384,1536]{1,0:T(8,128)(2,1)S(1)} %convolution_convert_fusion), channel_id=1, source_target_pairs={{0,1},{1,0},{2,3},{3,2},{4,5},{5,4},{6,7},{7,6},{8,24},{9,25},{10,... | collective-permute-start | bytes 3538952 | tf_op jit(solution)/shard_map/ppermute | solution.py:714
  131.0 30.2 %collective-permute-start.29 = (bf16[768,768]{1,0:T(8,128)(2,1)S(1)}, bf16[768,768]{1,0:T(8,128)(2,1)S(1)}, u32[]{:S(2)}, u32[]{:S(2)}) collective-permute-start(bf16[768,768]{1,0:T(8,128)(2,1)S(1)} %convolution_convert_fusion.2), channel_id=1, source_target_pairs={{0,1},{1,0},{2,3},{3,2},{4,5},{5,4},{6,7},{7,6},{8,24},{9,25},{10,... | collective-permute-start | bytes 3538952 | tf_op jit(solution)/shard_map/ppermute | solution.py:714
  132.9 7.7 %collective-permute-start.24 = (bf16[128,192]{1,0:T(8,128)(2,1)S(1)}, bf16[128,192]{1,0:T(8,128)(2,1)S(1)}, u32[]{:S(2)}, u32[]{:S(2)}) collective-permute-start(bf16[128,192]{1,0:T(8,128)(2,1)S(1)} %copy-done.30), channel_id=1, source_target_pairs={{0,4},{1,5},{2,6},{3,7},{4,0},{5,1},{6,2},{7,3},{8,12},{9,13},{10,... | collective-permute-start | bytes 147464 | tf_op jit(solution)/shard_map/ppermute | solution.py:733
  150.2 15.2 %collective-permute-start.28 = (bf16[512,384]{1,0:T(8,128)(2,1)}, bf16[512,384]{1,0:T(8,128)(2,1)}, u32[]{:S(2)}, u32[]{:S(2)}) collective-permute-start(bf16[512,384]{1,0:T(8,128)(2,1)} %get-tuple-element.179), channel_id=1, source_target_pairs={{0,1},{1,0},{2,3},{3,2},{4,5},{5,4},{6,7},{7,6},{8,9},{9,8},{10,11... | collective-permute-start | bytes 1179656 | tf_op jit(solution)/shard_map/ppermute | solution.py:714
  154.2 16.8 %collective-permute-start.31 = (bf16[192,1536]{1,0:T(8,128)(2,1)}, bf16[192,1536]{1,0:T(8,128)(2,1)}, u32[]{:S(2)}, u32[]{:S(2)}) collective-permute-start(bf16[192,1536]{1,0:T(8,128)(2,1)} %slice.181), channel_id=1, source_target_pairs={{0,16},{1,17},{2,18},{3,19},{4,20},{5,21},{6,22},{7,23},{8,9},{9,8... | collective-permute-start | bytes 1769480 | tf_op jit(solution)/shard_map/ppermute | solution.py:714
  161.5 10.6 %collective-permute-start.30 = (bf16[384,768]{1,0:T(8,128)(2,1)S(1)}, bf16[384,768]{1,0:T(8,128)(2,1)S(1)}, u32[]{:S(2)}, u32[]{:S(2)}) collective-permute-start(bf16[384,768]{1,0:T(8,128)(2,1)S(1)} %slice.182), channel_id=1, source_target_pairs={{0,16},{1,17},{2,18},{3,19},{4,20},{5,21},{6,22},{7,23},{8,9},{9,8... | collective-permute-start | bytes 1769480 | tf_op jit(solution)/shard_map/ppermute | solution.py:714
  171.0 8.2 %collective-permute-start.37 = (bf16[256,768]{1,0:T(8,128)(2,1)}, bf16[256,768]{1,0:T(8,128)(2,1)}, u32[]{:S(2)}, u32[]{:S(2)}) collective-permute-start(bf16[256,768]{1,0:T(8,128)(2,1)} %get-tuple-element.198), channel_id=1, source_target_pairs={{0,2},{1,3},{2,0},{3,1},{4,6},{5,7},{6,4},{7,5},{8,10},{9,11},{10,... | collective-permute-start | bytes 1179656 | tf_op jit(solution)/shard_map/ppermute | solution.py:714
  172.3 16.8 %collective-permute-start.32 = (bf16[384,1408]{1,0:T(8,128)(2,1)}, bf16[384,1408]{1,0:T(8,128)(2,1)S(1)}, u32[]{:S(2)}, u32[]{:S(2)}) collective-permute-start(bf16[384,1408]{1,0:T(8,128)(2,1)} %get-tuple-element.193), channel_id=1, source_target_pairs={{0,8},{1,9},{2,10},{3,11},{4,12},{5,13},{6,14},{7,15},{8,0},{9,1},... | collective-permute-start | bytes 3244040 | tf_op jit(solution)/shard_map/ppermute | solution.py:714
  176.0 12.8 %collective-permute-start.43 = (bf16[192,768]{1,0:T(8,128)(2,1)S(1)}, bf16[192,768]{1,0:T(8,128)(2,1)S(1)}, u32[]{:S(2)}, u32[]{:S(2)}) collective-permute-start(bf16[192,768]{1,0:T(8,128)(2,1)S(1)} %dynamic-slice_convert_fusion), channel_id=1, source_target_pairs={{0,2},{1,3},{2,0},{3,1},{4,6},{5,7},{6,4},{7,5},{8,10},{9,11},{10,... | collective-permute-start | bytes 884744 | tf_op jit(solution)/shard_map/ppermute | solution.py:714
  180.6 32.9 %collective-permute-start.38 = (bf16[128,768]{1,0:T(8,128)(2,1)S(1)}, bf16[128,768]{1,0:T(8,128)(2,1)S(1)}, u32[]{:S(2)}, u32[]{:S(2)}) collective-permute-start(bf16[128,768]{1,0:T(8,128)(2,1)S(1)} %slice.185), channel_id=1, source_target_pairs={{0,4},{1,5},{2,6},{3,7},{4,0},{5,1},{6,2},{7,3},{8,12},{9,13},{10,... | collective-permute-start | bytes 589832 | tf_op jit(solution)/shard_map/ppermute | solution.py:714
  180.9 18.1 %collective-permute-start.35 = (bf16[96,1536]{1,0:T(8,128)(2,1)S(1)}, bf16[96,1536]{1,0:T(8,128)(2,1)S(1)}, u32[]{:S(2)}, u32[]{:S(2)}) collective-permute-start(bf16[96,1536]{1,0:T(8,128)(2,1)S(1)} %dynamic-slice_convert_fusion.1), channel_id=1, source_target_pairs={{0,2},{1,3},{2,0},{3,1},{4,6},{5,7},{6,4},{7,5},{8,10},{9,11},{10,... | collective-permute-start | bytes 884744 | tf_op jit(solution)/shard_map/ppermute | solution.py:714
  188.9 18.5 %collective-permute-start.44 = (bf16[96,768]{1,0:T(8,128)(2,1)S(1)}, bf16[96,768]{1,0:T(8,128)(2,1)S(1)}, u32[]{:S(2)}, u32[]{:S(2)}) collective-permute-start(bf16[96,768]{1,0:T(8,128)(2,1)S(1)} %dynamic-slice_convert_fusion.2), channel_id=1, source_target_pairs={{0,4},{1,5},{2,6},{3,7},{4,0},{5,1},{6,2},{7,3},{8,12},{9,13},{10,... | collective-permute-start | bytes 442376 | tf_op jit(solution)/shard_map/ppermute | solution.py:714
  189.4 9.8 %collective-permute-start.33 = (bf16[192,1408]{1,0:T(8,128)(2,1)S(1)}, bf16[192,1408]{1,0:T(8,128)(2,1)S(1)}, u32[]{:S(2)}, u32[]{:S(2)}) collective-permute-start(bf16[192,1408]{1,0:T(8,128)(2,1)S(1)} %slice.183), channel_id=1, source_target_pairs={{0,1},{1,0},{2,3},{3,2},{4,5},{5,4},{6,7},{7,6},{8,24},{9,25},{10,... | collective-permute-start | bytes 1622024 | tf_op jit(solution)/shard_map/ppermute | solution.py:714
  199.1 8.3 %collective-permute-start.36 = (bf16[48,1536]{1,0:T(8,128)(2,1)S(1)}, bf16[48,1536]{1,0:T(8,128)(2,1)S(1)}, u32[]{:S(2)}, u32[]{:S(2)}) collective-permute-start(bf16[48,1536]{1,0:T(8,128)(2,1)S(1)} %dynamic-slice_convert_fusion.3), channel_id=1, source_target_pairs={{0,4},{1,5},{2,6},{3,7},{4,0},{5,1},{6,2},{7,3},{8,12},{9,13},{10,... | collective-permute-start | bytes 442376 | tf_op jit(solution)/shard_map/ppermute | solution.py:714
  199.3 8.8 %collective-permute-start.34 = (bf16[96,1408]{1,0:T(8,128)(2,1)S(1)}, bf16[96,1408]{1,0:T(8,128)(2,1)S(1)}, u32[]{:S(2)}, u32[]{:S(2)}) collective-permute-start(bf16[96,1408]{1,0:T(8,128)(2,1)S(1)} %slice.184), channel_id=1, source_target_pairs={{0,16},{1,17},{2,18},{3,19},{4,20},{5,21},{6,22},{7,23},{8,9},{9,8... | collective-permute-start | bytes 811016 | tf_op jit(solution)/shard_map/ppermute | solution.py:714
  208.3 9.1 %collective-permute-start.42 = (bf16[24,1408]{1,0:T(8,128)(2,1)S(1)}, bf16[24,1408]{1,0:T(8,128)(2,1)S(1)}, u32[]{:S(2)}, u32[]{:S(2)}) collective-permute-start(bf16[24,1408]{1,0:T(8,128)(2,1)S(1)} %get-tuple-element.216), channel_id=1, source_target_pairs={{0,6},{1,7},{2,4},{3,5},{4,2},{5,3},{6,0},{7,1},{8,14},{9,15},{10,... | collective-permute-start | bytes 202760 | tf_op jit(solution)/shard_map/ppermute | solution.py:733
  (45 other events, 234.2 us)
